TPU v7x, 128 devices: a whole 4x4x4 slice. The times are simulated.
128 devices in a mesh: rep: 4 (over z), fsdp: 8 (over x_lo, y), ctx: 4 (over x_hi, core).
Axes of the slice: x: 4 (x_hi: 2, x_lo: 2; x = x_hi * 2 + x_lo), y: 4, z: 4, core: 2. Of those that a mesh axis runs over, the one named last changes fastest.
Arguments:
- tokens: bfloat16 [32, 1024, 960], P(('rep', 'fsdp'), 'ctx'), may hold values from -6 to 6
- cotangent: bfloat16 [32, 1024, 960], P(('rep', 'fsdp'), 'ctx'), may hold values from -6 to 6
- query_weight: bfloat16 [960, 960], P('fsdp'), may hold values from -0.375 to 0.375
- keyval_weight: bfloat16 [2, 960, 320], P(None, 'fsdp'), may hold values from -0.1875 to 0.1875
- output_weight: bfloat16 [960, 960], P('fsdp'), may hold values from -0.5 to 0.5
- gateup_weight: bfloat16 [2, 960, 2560], P(None, 'fsdp'), may hold values from -0.1875 to 0.1875
- down_weight: bfloat16 [2560, 960], P('fsdp'), may hold values from -0.125 to 0.125
- norm_gains: bfloat16 [2, 960], P(None, 'fsdp'), may hold values from 0.5 to 1.5
- query_first: bfloat16 [960, 960], P('fsdp'), may hold values from -128 to 128
- keyval_first: bfloat16 [2, 960, 320], P(None, 'fsdp'), may hold values from -128 to 128
- output_first: bfloat16 [960, 960], P('fsdp'), may hold values from -48 to 48
- gateup_first: bfloat16 [2, 960, 2560], P(None, 'fsdp'), may hold values from -40 to 40
- down_first: bfloat16 [2560, 960], P('fsdp'), may hold values from -64 to 64
- gains_first: bfloat16 [2, 960], P(None, 'fsdp'), may hold values from -192 to 192
- query_second: bfloat16 [960, 960], P('fsdp'), may hold values from 1736 to 6880
- keyval_second: bfloat16 [2, 960, 320], P(None, 'fsdp'), may hold values from 1736 to 6880
- output_second: bfloat16 [960, 960], P('fsdp'), may hold values from 278 to 1112
- gateup_second: bfloat16 [2, 960, 2560], P(None, 'fsdp'), may hold values from 212 to 848
- down_second: bfloat16 [2560, 960], P('fsdp'), may hold values from 620 to 2480
- gains_second: bfloat16 [2, 960], P(None, 'fsdp'), may hold values from 3920 to 15680
Outputs:
- outputs: bfloat16 [32, 1024, 960], P(('rep', 'fsdp'), 'ctx')
- input_grad: float32 [32, 1024, 960], P(('rep', 'fsdp'), 'ctx')
- query_new: float32 [960, 960], P('fsdp')
- keyval_new: float32 [2, 960, 320], P(None, 'fsdp')
- output_new: float32 [960, 960], P('fsdp')
- gateup_new: float32 [2, 960, 2560], P(None, 'fsdp')
- down_new: float32 [2560, 960], P('fsdp')
- gains_new: float32 [2, 960], P(None, 'fsdp')
- query_first_new: float32 [960, 960], P('fsdp')
- keyval_first_new: float32 [2, 960, 320], P(None, 'fsdp')
- output_first_new: float32 [960, 960], P('fsdp')
- gateup_first_new: float32 [2, 960, 2560], P(None, 'fsdp')
- down_first_new: float32 [2560, 960], P('fsdp')
- gains_first_new: float32 [2, 960], P(None, 'fsdp')
- query_second_new: float32 [960, 960], P('fsdp')
- keyval_second_new: float32 [2, 960, 320], P(None, 'fsdp')
- output_second_new: float32 [960, 960], P('fsdp')
- gateup_second_new: float32 [2, 960, 2560], P(None, 'fsdp')
- down_second_new: float32 [2560, 960], P('fsdp')
- gains_second_new: float32 [2, 960], P(None, 'fsdp')
All inputs are finite; a program needn't handle non-finite values.
Results may differ from a plain program's by a relative error of at most 0.035.
Values may be sent and summed in bfloat16 or wider, within the bound.
A program may use at most 192 MiB of HBM per device.

v0:
```python
import jax
import jax.numpy as jnp
from jax import lax
from jax.sharding import PartitionSpec as P

QUERY_HEADS = 15
KEY_VALUE_HEADS = 5
HEAD_WIDTH = 64
STEP = 10


norm_epsilon = 1e-05
rotary_base = 100000.0
beta_first = 0.9
beta_second = 0.95
adam_epsilon = 1e-08
matrix_rate = 0.06
matrix_decay = 0.1
gain_rate = 0.6


def matmul(left, right):
    return jnp.dot(left, right, preferred_element_type=jnp.float32)


def rms_norm(stream, gain_row):
    scale = lax.rsqrt(jnp.mean(stream * stream, axis=-1, keepdims=True) + norm_epsilon)
    return stream * scale * gain_row


def norm_backward(stream, gain_row, incoming):
    scale = lax.rsqrt(jnp.mean(stream * stream, axis=-1, keepdims=True) + norm_epsilon)
    normal = stream * scale
    gain_grad = jnp.sum(incoming * normal, axis=0)
    scaled = incoming * gain_row
    stream_grad = scale * (scaled - normal * jnp.mean(scaled * normal, axis=-1, keepdims=True))
    return (stream_grad, gain_grad)


def rotary_tables(positions, width):
    counter = jnp.arange(width // 2, dtype=jnp.float32)
    frequency = 1.0 / rotary_base ** (counter * (2.0 / width))
    angles = positions[:, None] * frequency[None, :]
    return (jnp.cos(angles), jnp.sin(angles))


def apply_rotary(field, cosine_table, sine_table):
    half_width = field.shape[-1] // 2
    former = field[..., :half_width]
    latter = field[..., half_width:]
    cos_rows = cosine_table[:, None, :]
    sin_rows = sine_table[:, None, :]
    return jnp.concatenate(
        [former * cos_rows - latter * sin_rows, latter * cos_rows + former * sin_rows], axis=-1
    )


def adamw_update(weight, gradient, first, second, rate, decay):
    weight = weight.astype(jnp.float32)
    first_new = beta_first * first.astype(jnp.float32) + (1.0 - beta_first) * gradient
    second_new = (
        beta_second * second.astype(jnp.float32) + (1.0 - beta_second) * gradient * gradient
    )
    first_hat = first_new / (1.0 - beta_first**STEP)
    second_hat = second_new / (1.0 - beta_second**STEP)
    weight_new = weight - rate * (
        first_hat / (jnp.sqrt(second_hat) + adam_epsilon) + decay * weight
    )
    return (weight_new, first_new, second_new)


def body(
    tokens,
    cotangent,
    query_weight,
    keyval_weight,
    output_weight,
    gateup_weight,
    down_weight,
    norm_gains,
    query_first,
    keyval_first,
    output_first,
    gateup_first,
    down_first,
    gains_first,
    query_second,
    keyval_second,
    output_second,
    gateup_second,
    down_second,
    gains_second,
):
    shards = (query_weight, keyval_weight, output_weight, gateup_weight, down_weight, norm_gains)
    gathered = (
        lax.all_gather(query_weight, "fsdp", axis=0, tiled=True),
        lax.all_gather(keyval_weight, "fsdp", axis=1, tiled=True),
        lax.all_gather(output_weight, "fsdp", axis=0, tiled=True),
        lax.all_gather(gateup_weight, "fsdp", axis=1, tiled=True),
        lax.all_gather(down_weight, "fsdp", axis=0, tiled=True),
        lax.all_gather(norm_gains, "fsdp", axis=1, tiled=True),
    )
    query_full, keyval_full, output_full, gateup_full, down_full, gain_full = gathered
    stream = tokens[0].astype(jnp.float32)
    row_total = stream.shape[0]
    heads_per_group = QUERY_HEADS // KEY_VALUE_HEADS
    score_scale = HEAD_WIDTH ** (-0.5)
    offset = lax.axis_index("ctx") * row_total
    query_pos = offset + jnp.arange(row_total, dtype=jnp.int32)
    cosine_table, sine_table = rotary_tables(query_pos.astype(jnp.float32), HEAD_WIDTH)
    gain_rows = gain_full.astype(jnp.float32)
    normed_one = rms_norm(stream, gain_rows[0]).astype(jnp.bfloat16)
    query_linear = matmul(normed_one, query_full)
    key_linear = matmul(normed_one, keyval_full[0])
    value_low = matmul(normed_one, keyval_full[1]).astype(jnp.bfloat16)
    query_lower = apply_rotary(
        query_linear.reshape(row_total, QUERY_HEADS, HEAD_WIDTH), cosine_table, sine_table
    ).astype(jnp.bfloat16)
    key_low = (
        apply_rotary(
            key_linear.reshape(row_total, KEY_VALUE_HEADS, HEAD_WIDTH), cosine_table, sine_table
        )
        .astype(jnp.bfloat16)
        .reshape(row_total, KEY_VALUE_HEADS * HEAD_WIDTH)
    )
    keys_complete, values_complete = (
        lax.all_gather(key_low, "ctx", axis=0, tiled=True),
        lax.all_gather(value_low, "ctx", axis=0, tiled=True),
    )
    key_total = keys_complete.shape[0]
    key_head_rows = keys_complete.reshape(key_total, KEY_VALUE_HEADS, HEAD_WIDTH)
    value_head_rows = values_complete.reshape(key_total, KEY_VALUE_HEADS, HEAD_WIDTH)
    query_grouped = query_lower.reshape(row_total, KEY_VALUE_HEADS, heads_per_group, HEAD_WIDTH)
    key_pos = jnp.arange(key_total, dtype=jnp.int32)
    allowed = key_pos[None, :] <= query_pos[:, None]
    scores = (
        jnp.einsum(
            "qhgd,khd->hgqk", query_grouped, key_head_rows, preferred_element_type=jnp.float32
        )
        * score_scale
    )
    scores = jnp.where(allowed, scores, -1e30)
    largest = jnp.max(scores, axis=-1, keepdims=True)
    lifted = jnp.exp(scores - largest)
    probs = lifted / jnp.sum(lifted, axis=-1, keepdims=True)
    probs_low = probs.astype(jnp.bfloat16)
    attended = jnp.einsum(
        "hgqk,khd->qhgd", probs_low, value_head_rows, preferred_element_type=jnp.float32
    )
    attended = attended.reshape(row_total, QUERY_HEADS * HEAD_WIDTH).astype(jnp.bfloat16)
    middle = stream + matmul(attended, output_full)
    normed_two = rms_norm(middle, gain_rows[1]).astype(jnp.bfloat16)
    gate = matmul(normed_two, gateup_full[0])
    upward = matmul(normed_two, gateup_full[1])
    sigmoid_gate = jax.nn.sigmoid(gate)
    hidden_low = (gate * sigmoid_gate * upward).astype(jnp.bfloat16)
    result = middle + matmul(hidden_low, down_full)
    regathered = (
        lax.all_gather(query_weight, "fsdp", axis=0, tiled=True),
        lax.all_gather(keyval_weight, "fsdp", axis=1, tiled=True),
        lax.all_gather(output_weight, "fsdp", axis=0, tiled=True),
        lax.all_gather(gateup_weight, "fsdp", axis=1, tiled=True),
        lax.all_gather(down_weight, "fsdp", axis=0, tiled=True),
        lax.all_gather(norm_gains, "fsdp", axis=1, tiled=True),
    )
    query_back, keyval_back, output_back, gateup_back, down_back, gain_back = regathered
    gain_values = gain_back.astype(jnp.float32)
    incoming_low = cotangent[0]
    incoming = incoming_low.astype(jnp.float32)
    grad_down = matmul(hidden_low.T, incoming_low)
    hidden_grad = matmul(incoming_low, down_back.T)
    gate_grad = (hidden_grad * upward * sigmoid_gate * (1.0 + gate * (1.0 - sigmoid_gate))).astype(
        jnp.bfloat16
    )
    up_grad = (hidden_grad * gate * sigmoid_gate).astype(jnp.bfloat16)
    grad_gateup = jnp.stack([matmul(normed_two.T, gate_grad), matmul(normed_two.T, up_grad)])
    normed_two_grad = matmul(gate_grad, gateup_back[0].T) + matmul(up_grad, gateup_back[1].T)
    middle_norm_grad, gain_two_grad = norm_backward(middle, gain_values[1], normed_two_grad)
    middle_grad = incoming + middle_norm_grad
    middle_low = middle_grad.astype(jnp.bfloat16)
    grad_output = matmul(attended.T, middle_low)
    attended_grad = (
        matmul(middle_low, output_back.T)
        .astype(jnp.bfloat16)
        .reshape(row_total, KEY_VALUE_HEADS, heads_per_group, HEAD_WIDTH)
    )
    probs_grad = jnp.einsum(
        "qhgd,khd->hgqk", attended_grad, value_head_rows, preferred_element_type=jnp.float32
    )
    row_dots = jnp.sum(probs * probs_grad, axis=-1, keepdims=True)
    scores_grad = (probs * (probs_grad - row_dots)).astype(jnp.bfloat16)
    query_grad = (
        jnp.einsum("hgqk,khd->qhgd", scores_grad, key_head_rows, preferred_element_type=jnp.float32)
        * score_scale
    )
    key_gradient = (
        jnp.einsum("hgqk,qhgd->khd", scores_grad, query_grouped, preferred_element_type=jnp.float32)
        * score_scale
    )
    value_gradient = jnp.einsum(
        "hgqk,qhgd->khd", probs_low, attended_grad, preferred_element_type=jnp.float32
    )
    key_local, value_own = (
        lax.psum_scatter(
            key_gradient.reshape(key_total, KEY_VALUE_HEADS * HEAD_WIDTH).astype(jnp.bfloat16),
            "ctx",
            scatter_dimension=0,
            tiled=True,
        ).astype(jnp.float32),
        lax.psum_scatter(
            value_gradient.reshape(key_total, KEY_VALUE_HEADS * HEAD_WIDTH).astype(jnp.bfloat16),
            "ctx",
            scatter_dimension=0,
            tiled=True,
        ).astype(jnp.float32),
    )
    query_back_low = (
        apply_rotary(
            query_grad.reshape(row_total, QUERY_HEADS, HEAD_WIDTH), cosine_table, -sine_table
        )
        .reshape(row_total, QUERY_HEADS * HEAD_WIDTH)
        .astype(jnp.bfloat16)
    )
    key_back_low = (
        apply_rotary(
            key_local.reshape(row_total, KEY_VALUE_HEADS, HEAD_WIDTH), cosine_table, -sine_table
        )
        .reshape(row_total, KEY_VALUE_HEADS * HEAD_WIDTH)
        .astype(jnp.bfloat16)
    )
    value_back_low = value_own.astype(jnp.bfloat16)
    grad_query = matmul(normed_one.T, query_back_low)
    grad_keyval = jnp.stack(
        [matmul(normed_one.T, key_back_low), matmul(normed_one.T, value_back_low)]
    )
    normed_one_grad = (
        matmul(query_back_low, query_back.T)
        + matmul(key_back_low, keyval_back[0].T)
        + matmul(value_back_low, keyval_back[1].T)
    )
    stream_norm_grad, gain_one_grad = norm_backward(stream, gain_values[0], normed_one_grad)
    input_grad = middle_grad + stream_norm_grad
    grad_gains = jnp.stack([gain_one_grad, gain_two_grad])
    owned = (
        lax.psum_scatter(
            grad_query.astype(jnp.bfloat16), "fsdp", scatter_dimension=0, tiled=True
        ).astype(jnp.float32),
        lax.psum_scatter(
            grad_keyval.astype(jnp.bfloat16), "fsdp", scatter_dimension=1, tiled=True
        ).astype(jnp.float32),
        lax.psum_scatter(
            grad_output.astype(jnp.bfloat16), "fsdp", scatter_dimension=0, tiled=True
        ).astype(jnp.float32),
        lax.psum_scatter(
            grad_gateup.astype(jnp.bfloat16), "fsdp", scatter_dimension=1, tiled=True
        ).astype(jnp.float32),
        lax.psum_scatter(
            grad_down.astype(jnp.bfloat16), "fsdp", scatter_dimension=0, tiled=True
        ).astype(jnp.float32),
        lax.psum_scatter(
            grad_gains.astype(jnp.bfloat16), "fsdp", scatter_dimension=1, tiled=True
        ).astype(jnp.float32),
    )
    summed = (
        lax.psum(owned[0].astype(jnp.bfloat16), ("rep", "ctx")).astype(jnp.float32),
        lax.psum(owned[1].astype(jnp.bfloat16), ("rep", "ctx")).astype(jnp.float32),
        lax.psum(owned[2].astype(jnp.bfloat16), ("rep", "ctx")).astype(jnp.float32),
        lax.psum(owned[3].astype(jnp.bfloat16), ("rep", "ctx")).astype(jnp.float32),
        lax.psum(owned[4].astype(jnp.bfloat16), ("rep", "ctx")).astype(jnp.float32),
        lax.psum(owned[5].astype(jnp.bfloat16), ("rep", "ctx")).astype(jnp.float32),
    )
    firsts = (query_first, keyval_first, output_first, gateup_first, down_first, gains_first)
    seconds = (query_second, keyval_second, output_second, gateup_second, down_second, gains_second)
    rates = (matrix_rate, matrix_rate, matrix_rate, matrix_rate, matrix_rate, gain_rate)
    decays = (matrix_decay, matrix_decay, matrix_decay, matrix_decay, matrix_decay, 0.0)
    updated = [
        adamw_update(
            shards[slot], summed[slot], firsts[slot], seconds[slot], rates[slot], decays[slot]
        )
        for slot in range(6)
    ]
    return (
        result.astype(jnp.bfloat16)[None],
        input_grad[None],
        updated[0][0],
        updated[1][0],
        updated[2][0],
        updated[3][0],
        updated[4][0],
        updated[5][0],
        updated[0][1],
        updated[1][1],
        updated[2][1],
        updated[3][1],
        updated[4][1],
        updated[5][1],
        updated[0][2],
        updated[1][2],
        updated[2][2],
        updated[3][2],
        updated[4][2],
        updated[5][2],
    )


def solution(mesh):
    in_specs = (
        P(("rep", "fsdp"), "ctx", None),
        P(("rep", "fsdp"), "ctx", None),
        P("fsdp", None),
        P(None, "fsdp", None),
        P("fsdp", None),
        P(None, "fsdp", None),
        P("fsdp", None),
        P(None, "fsdp"),
        P("fsdp", None),
        P(None, "fsdp", None),
        P("fsdp", None),
        P(None, "fsdp", None),
        P("fsdp", None),
        P(None, "fsdp"),
        P("fsdp", None),
        P(None, "fsdp", None),
        P("fsdp", None),
        P(None, "fsdp", None),
        P("fsdp", None),
        P(None, "fsdp"),
    )
    out_specs = (
        P(("rep", "fsdp"), "ctx", None),
        P(("rep", "fsdp"), "ctx", None),
        P("fsdp", None),
        P(None, "fsdp", None),
        P("fsdp", None),
        P(None, "fsdp", None),
        P("fsdp", None),
        P(None, "fsdp"),
        P("fsdp", None),
        P(None, "fsdp", None),
        P("fsdp", None),
        P(None, "fsdp", None),
        P("fsdp", None),
        P(None, "fsdp"),
        P("fsdp", None),
        P(None, "fsdp", None),
        P("fsdp", None),
        P(None, "fsdp", None),
        P("fsdp", None),
        P(None, "fsdp"),
    )
    return jax.shard_map(body, mesh=mesh, in_specs=in_specs, out_specs=out_specs, check_vma=False)
```

profile of v0, /device:TPU:1, one launch (start us, length us, event | category | flops | bytes accessed | tf_op | source)
XLA Modules:
  0.0 919.9 jit_solution(805535147432989845)
XLA Ops:
  11.8 16.8 %all-gather = bf16[8,120,2]{1,2,0:T(2,128)(2,1)S(1)} all-gather(bf16[1,120,2]{1,2,0:T(2,128)(2,1)S(1)} %bitcast.249), channel_id=1, replica_groups=mesh['rep'=4,'fsdp'=8,'ctx'=4] {'fsdp'}, dimensions={0}, use_global_device_ids=true | all-gather | bytes 4320 | tf_op jit(solution)/shard_map/all_gather | solution.py:101
  30.0 17.7 %all-gather.7.cloned.1.call-done = bf16[2,960,320]{2,0,1:T(2,128)(2,1)} async-done(((bf16[2,120,320]{2,0,1:T(2,128)(2,1)}), bf16[2,960,320]{2,0,1:T(2,128)(2,1)}) %all-gather.7.cloned.1.call-update) | async-done | bytes 1228816 | tf_op jit(solution)/shard_map/all_gather | solution.py:97
  59.8 18.8 %all_gather.33 = bf16[1024,320]{0,1:T(8,128)(2,1)S(1)} all-gather(bf16[256,320]{0,1:T(8,128)(2,1)S(1)} %bitcast.231), channel_id=1, replica_groups=mesh['rep'=4,'fsdp'=8,'ctx'=4] {'ctx'}, dimensions={0}, use_global_device_ids=true | all-gather | bytes 819200 | tf_op jit(solution)/shard_map/all_gather | solution.py:127
  79.0 13.4 %all_gather.32 = bf16[1024,320]{0,1:T(8,128)(2,1)} all-gather(bf16[256,320]{0,1:T(8,128)(2,1)S(1)} %convolution_convert_fusion.8), channel_id=1, replica_groups=mesh['rep'=4,'fsdp'=8,'ctx'=4] {'ctx'}, dimensions={0}, use_global_device_ids=true | all-gather | bytes 819200 | tf_op jit(solution)/shard_map/all_gather | solution.py:128
  99.0 8.7 fusion.123
  107.7 7.0 fusion.38
  114.8 20.8 %all-gather.11.cloned.1.call-done = bf16[960,960]{1,0:T(8,128)(2,1)} async-done(((bf16[120,960]{1,0:T(8,128)(2,1)}), bf16[960,960]{1,0:T(8,128)(2,1)}) %all-gather.11.cloned.1.call-update) | async-done | bytes 1843216 | tf_op jit(solution)/shard_map/all_gather | solution.py:98
  138.3 108.7 %all-gather.13.cloned.1.call-done = bf16[2,960,2560]{2,1,0:T(8,128)(2,1)} async-done(((bf16[2,120,2560]{2,1,0:T(8,128)(2,1)}), bf16[2,960,2560]{2,1,0:T(8,128)(2,1)}) %all-gather.13.cloned.1.call-update) | async-done | bytes 9830416 | tf_op jit(solution)/shard_map/all_gather | solution.py:99
  257.9 51.9 %all-gather.15.cloned.1.call-done = bf16[2560,960]{1,0:T(8,128)(2,1)} async-done(((bf16[320,960]{1,0:T(8,128)(2,1)}), bf16[2560,960]{1,0:T(8,128)(2,1)}) %all-gather.15.cloned.1.call-update) | async-done | bytes 4915216 | tf_op jit(solution)/shard_map/all_gather | solution.py:100
  309.8 8.5 multiply_convert_fusion
  336.9 7.2 fusion.3
  347.7 8.8 fusion.29
  356.6 19.4 %reduce-scatter.11.cloned.1.call-done = bf16[256,320]{0,1:T(8,128)(2,1)} async-done(((bf16[1024,320]{0,1:T(8,128)(2,1)}), bf16[256,320]{0,1:T(8,128)(2,1)}) %reduce-scatter.11.cloned.1.call-update) | async-done | bytes 163856 | tf_op jit(solution)/shard_map/reduce_scatter | solution.py:204
  377.4 30.5 %reduce-scatter.13.cloned.1.call-done = bf16[256,320]{0,1:T(8,128)(2,1)} async-done(((bf16[1024,320]{0,1:T(8,128)(2,1)}), bf16[256,320]{0,1:T(8,128)(2,1)}) %reduce-scatter.13.cloned.1.call-update) | async-done | bytes 163856 | tf_op jit(solution)/shard_map/reduce_scatter | solution.py:210
  419.4 8.6 pad_maximum_fusion
  428.0 44.7 %copy.87 = bf16[2,960,2560]{2,0,1:T(2,128)(2,1)} copy(bf16[2,960,2560]{2,1,0:T(8,128)(2,1)} %pad_maximum_fusion) | data formatting | bytes 19660800
  472.6 10.1 %copy.93 = bf16[120,8,2,2560]{3,1,2,0:T(8,128)(2,1)} copy(bf16[120,8,2,2560]{3,2,1,0:T(2,128)(2,1)} %bitcast.209) | data formatting | bytes 19660800
  501.4 95.9 %reduce-scatter.21.cloned.1.call-done = bf16[120,5120]{1,0:T(8,128)(2,1)} async-done(((bf16[960,5120]{1,0:T(8,128)(2,1)}), bf16[120,5120]{1,0:T(8,128)(2,1)}) %reduce-scatter.21.cloned.1.call-update) | async-done | bytes 1228816
  601.9 33.9 %reduce-scatter.17.cloned.1.call-done = bf16[120,960]{1,0:T(8,128)(2,1)} async-done(((bf16[960,960]{1,0:T(8,128)(2,1)}), bf16[120,960]{1,0:T(8,128)(2,1)}) %reduce-scatter.17.cloned.1.call-update) | async-done | bytes 230416 | tf_op jit(solution)/shard_map/reduce_scatter | solution.py:251
  635.9 44.1 %reduce-scatter.15.cloned.1.call-done = bf16[120,960]{1,0:T(8,128)(2,1)} async-done(((bf16[960,960]{1,0:T(8,128)(2,1)}), bf16[120,960]{1,0:T(8,128)(2,1)}) %reduce-scatter.15.cloned.1.call-update) | async-done | bytes 230416 | tf_op jit(solution)/shard_map/reduce_scatter | solution.py:245
  679.9 69.5 %reduce-scatter.19.cloned.1.call-done = bf16[320,960]{1,0:T(8,128)(2,1)} async-done(((bf16[2560,960]{1,0:T(8,128)(2,1)}), bf16[320,960]{1,0:T(8,128)(2,1)}) %reduce-scatter.19.cloned.1.call-update) | async-done | bytes 614416 | tf_op jit(solution)/shard_map/reduce_scatter | solution.py:257
  758.8 14.0 %all-reduce.1 = bf16[2,960]{1,0:T(2,128)(2,1)S(1)} all-reduce(bf16[2,960]{1,0:T(2,128)(2,1)S(1)} %pad_maximum_fusion.12), channel_id=9, replica_groups=mesh['rep'=4,'fsdp'=8,'ctx'=4] {'fsdp'}, use_global_device_ids=true, to_apply=%region_21.22.clone | all-reduce | flops 1920 | bytes 7680
  773.0 36.1 %psum.47 = bf16[2,120]{1,0:T(2,128)(2,1)S(1)} all-reduce(bf16[2,120]{1,0:T(2,128)(2,1)S(1)} %constant_dynamic-slice_fusion), channel_id=1, replica_groups=mesh['rep'=4,'fsdp'=8,'ctx'=4] {'rep','ctx'}, use_global_device_ids=true, to_apply=%region_22.23 | all-reduce | flops 240 | bytes 960 | tf_op jit(solution)/shard_map/psum | solution.py:270
  810.9 89.0 %all-reduce.8.cloned.1.call-done = (bf16[120,960]{1,0:T(8,128)(2,1)}, bf16[2,120,320]{1,2,0:T(8,128)(2,1)}, bf16[120,960]{1,0:T(8,128)(2,1)}, bf16[2,120,2560]{2,1,0:T(8,128)(2,1)}, bf16[320,960]{1,0:T(8,128)(2,1)}) async-done(((bf16[120,960]{1,0:T(8,128)(2,1)}, bf16[2,120,320]{1,2,0:T(8,128)(2,1)}, bf16[120,960]{1,0:T(8,128)(2,1)}, bf16[2,120,2560]{2,1,0:T(8,128)(2,1)}, bf16[320,960]{1,0:T(8,128)(2,1)}), ...) | async-done | bytes 2457616 | tf_op jit(solution)/shard_map/psum | solution.py:265
  (207 shorter events, 120.2 us)
Async XLA Ops:
  7.2 40.5 %all-gather.7.cloned.1.call-start = ((), (), s32[]{:S(2)}) async-start(), calls=%async_computation.6 | async-start | bytes 1658880 | tf_op jit(solution)/shard_map/all_gather | solution.py:97
  9.1 85.9 %all-gather.9.cloned.1.call-start = ((), (), s32[]{:S(2)}) async-start(), calls=%async_computation.7 | async-start | bytes 2211840 | tf_op jit(solution)/shard_map/all_gather | solution.py:96
  9.8 125.8 %all-gather.11.cloned.1.call-start = ((), (), s32[]{:S(2)}) async-start(), calls=%async_computation.8 | async-start | bytes 2211840 | tf_op jit(solution)/shard_map/all_gather | solution.py:98
  10.6 236.4 %all-gather.13.cloned.1.call-start = ((), (), s32[]{:S(2)}) async-start(), calls=%async_computation.9 | async-start | bytes 11059200 | tf_op jit(solution)/shard_map/all_gather | solution.py:99
  11.1 298.6 %all-gather.15.cloned.1.call-start = ((), (), s32[]{:S(2)}) async-start(), calls=%async_computation.10 | async-start | bytes 5898240 | tf_op jit(solution)/shard_map/all_gather | solution.py:100
  11.7 364.2 %reduce-scatter.11.cloned.1.call-start = ((), (), s32[]{:S(2)}) async-start(), calls=%async_computation.11 | async-start | bytes 819200 | tf_op jit(solution)/shard_map/reduce_scatter | solution.py:204
  114.7 23.6 %copy-start.35 = (bf16[5,64,3,256]{3,1,2,0:T(8,128)(2,1)}, bf16[5,64,3,256]{3,1,2,0:T(8,128)(2,1)S(1)}, u32[]{:S(2)}) copy-start(bf16[5,64,3,256]{3,1,2,0:T(8,128)(2,1)S(1)} %fusion.38) | copy-start | bytes 1474564
  138.1 189.3 %copy-start.3 = (f32[256,960]{0,1:T(8,128)}, f32[256,960]{0,1:T(8,128)S(1)}, u32[]{:S(2)}) copy-start(f32[256,960]{0,1:T(8,128)S(1)} %get-tuple-element.68) | copy-start | bytes 2949124
  252.5 57.3 %copy-start.15 = (bf16[1,256,960]{1,2,0:T(8,128)(2,1)S(1)}, bf16[1,256,960]{1,2,0:T(8,128)(2,1)}, u32[]{:S(2)}) copy-start(bf16[1,256,960]{1,2,0:T(8,128)(2,1)} %param.21) | copy-start | bytes 1474564
  347.7 60.3 %reduce-scatter.13.cloned.1.call-start = ((), (), s32[]{:S(2)}) async-start(), calls=%async_computation.12 | async-start | bytes 819200 | tf_op jit(solution)/shard_map/reduce_scatter | solution.py:210
  356.5 142.9 %all-reduce.6.cloned.1.call-start = ((), (), s32[]{:S(2)}) async-start(), calls=%async_computation.17 | async-start | bytes 2621440
  377.0 33.6 %copy-start.17 = (bf16[256,5,64]{0,2,1:T(8,128)(2,1)}, bf16[256,5,64]{0,2,1:T(8,128)(2,1)S(1)}, u32[]{:S(2)}) copy-start(bf16[256,5,64]{0,2,1:T(8,128)(2,1)S(1)} %pad_maximum_fusion.4) | copy-start | bytes 491524
  410.6 186.7 %reduce-scatter.21.cloned.1.call-start = ((), (), s32[]{:S(2)}) async-start(), calls=%async_computation.16 | async-start | bytes 11059200
  482.8 153.0 %reduce-scatter.17.cloned.1.call-start = ((), (), s32[]{:S(2)}) async-start(), calls=%async_computation.14 | async-start | bytes 2211840 | tf_op jit(solution)/shard_map/reduce_scatter | solution.py:251
  485.8 194.1 %reduce-scatter.15.cloned.1.call-start = ((), (), s32[]{:S(2)}) async-start(), calls=%async_computation.13 | async-start | bytes 2211840 | tf_op jit(solution)/shard_map/reduce_scatter | solution.py:245
  493.6 255.9 %reduce-scatter.19.cloned.1.call-start = ((), (), s32[]{:S(2)}) async-start(), calls=%async_computation.15 | async-start | bytes 5898240 | tf_op jit(solution)/shard_map/reduce_scatter | solution.py:257
  497.6 402.3 %all-reduce.8.cloned.1.call-start = ((), (), s32[]{:S(2)}) async-start(), calls=%async_computation.18 | async-start | bytes 5079040 | tf_op jit(solution)/shard_map/psum | solution.py:265
  601.9 147.5 %copy-start.13 = (bf16[960,960]{1,0:T(8,128)(2,1)S(1)}, bf16[960,960]{1,0:T(8,128)(2,1)}, u32[]{:S(2)}) copy-start(bf16[960,960]{1,0:T(8,128)(2,1)} %all-gather.9.cloned.1.call-done) | copy-start | bytes 5529604
  757.0 52.1 %copy-start.48 = (bf16[2,120]{1,0:T(2,128)(2,1)S(1)}, bf16[2,120]{1,0:T(2,128)(2,1)}, u32[]{:S(2)}) copy-start(bf16[2,120]{1,0:T(2,128)(2,1)} %param.27) | copy-start | bytes 1444
  757.0 52.1 %copy-start.49 = (bf16[2,120]{1,0:T(2,128)(2,1)S(1)}, bf16[2,120]{1,0:T(2,128)(2,1)}, u32[]{:S(2)}) copy-start(bf16[2,120]{1,0:T(2,128)(2,1)} %param.33) | copy-start | bytes 1444
  757.0 52.1 %copy-start.50 = (bf16[2,120]{1,0:T(2,128)(2,1)S(1)}, bf16[2,120]{1,0:T(2,128)(2,1)}, u32[]{:S(2)}) copy-start(bf16[2,120]{1,0:T(2,128)(2,1)} %param.39) | copy-start | bytes 1444
  758.8 141.1 %copy-start.32 = (bf16[2,120,320]{1,2,0:T(8,128)(2,1)S(1)}, bf16[2,120,320]{1,2,0:T(8,128)(2,1)}, u32[]{:S(2)}) copy-start(bf16[2,120,320]{1,2,0:T(8,128)(2,1)} %param.23) | copy-start | bytes 460804
  758.8 141.1 %copy-start.46 = (bf16[2,120,320]{1,2,0:T(8,128)(2,1)S(1)}, bf16[2,120,320]{1,2,0:T(8,128)(2,1)}, u32[]{:S(2)}) copy-start(bf16[2,120,320]{1,2,0:T(8,128)(2,1)} %param.29) | copy-start | bytes 460804
  809.7 92.3 %copy-start.9 = (bf16[320,960]{1,0:T(8,128)(2,1)S(1)}, bf16[320,960]{1,0:T(8,128)(2,1)}, u32[]{:S(2)}) copy-start(bf16[320,960]{1,0:T(8,128)(2,1)} %param.26) | copy-start | bytes 1843204
  (45 other events, 255.3 us)
Sparse Core Ops, SparseCore 0:
  10.3 37.3 all-gather.6
  49.3 45.6 all-gather.8
  96.6 38.9 all-gather.10
  137.1 109.8 all-gather.12
  248.5 61.2 all-gather.14
  347.8 28.1 reduce-scatter.10
  379.1 28.7 reduce-scatter.12
  411.0 72.6 all-reduce.5
  486.2 110.9 reduce-scatter.20
  600.2 35.6 reduce-scatter.16
  638.9 41.0 reduce-scatter.14
  682.3 67.0 reduce-scatter.18
  753.2 146.6 all-reduce.7
where the time goes:
time: 925 us; the launch traced here: 920 us
  waiting for transfers between devices  587 us (63%)
  matrix products  101 us (11%)
  blocking collectives  99.1 us (11%)
  local copies, waits for them, and re-layouts  82 us (9%)
  other arithmetic  35.1 us (4%)
  between operations  15.7 us (2%)
    all_gather x1, waiting for transfers between devices, body(): lax.all_gather(gateup_weight, 'fsdp', axis=1, tiled=True)  109 us
    unnamed x15, waiting for transfers between devices  98.5 us
    psum x1, waiting for transfers between devices, body(): lax.psum(owned[0].astype(jnp.bfloat16), ('rep', 'ctx')).astype(jnp.float32)  89 us
    unnamed x122, local copies, waits for them, and re-layouts  74.4 us
    reduce_scatter x1, waiting for transfers between devices, body(): lax.psum_scatter(grad_down.astype(jnp.bfloat16), 'fsdp', scatter_dimensio...  69.5 us
    dot_general x21, matrix products, matmul(): return jnp.dot(left, right, preferred_element_type=jnp.float32)  61.5 us
    all_gather x1, waiting for transfers between devices, body(): lax.all_gather(down_weight, 'fsdp', axis=0, tiled=True)  51.9 us
    reduce_scatter x1, waiting for transfers between devices, body(): lax.psum_scatter(grad_query.astype(jnp.bfloat16), 'fsdp', scatter_dimensi...  44.1 us
  transfers between devices with their start and end apart: 13, of which 12 were waited for; matrix products, arithmetic and copies ran while one was open for 17% of the time, Pallas kernels for 0%

commit v1 on v0

v1 whole, which is shorter than its diff:
```python
import functools

import jax
import jax.numpy as jnp
from jax import lax
from jax.experimental import pallas as pl
from jax.experimental.pallas import tpu as pltpu
from jax.sharding import PartitionSpec as P

QUERY_HEADS = 15
KEY_VALUE_HEADS = 5
GROUP = QUERY_HEADS // KEY_VALUE_HEADS
HEAD_WIDTH = 64
HALF = HEAD_WIDTH // 2
STEP = 10
TOK = 256
D = 960
KW = 320
FF = 2560
FH = FF // 2
ROWS = 120
PAD = 128
BF = jnp.bfloat16
F32 = jnp.float32
MESH = pl.DeviceIdType.MESH

norm_epsilon = 1e-05
rotary_base = 100000.0
beta_first = 0.9
beta_second = 0.95
adam_epsilon = 1e-08
matrix_rate = 0.06
matrix_decay = 0.1
gain_rate = 0.6
score_scale = HEAD_WIDTH ** (-0.5)

ANY = pl.BlockSpec(memory_space=pl.ANY)
VM = pl.BlockSpec(memory_space=pltpu.VMEM)


def place():
    f = lax.axis_index("fsdp")
    q = lax.axis_index("ctx")
    z = lax.axis_index("rep")
    return (q // 2) * 2 + f // 4, f % 4, z, q % 2


def at(x, y, z, core):
    x, y, z = lax.rem(x, 4), lax.rem(y, 4), lax.rem(z, 4)
    return {"rep": z, "fsdp": lax.rem(x, 2) * 4 + y, "ctx": (x // 2) * 2 + core}


def greet(devices):
    barrier = pltpu.get_barrier_semaphore()
    for device in devices:
        pl.semaphore_signal(barrier, inc=1, device_id=device, device_id_type=MESH)
    pl.semaphore_wait(barrier, len(devices))


def remote(src, dst, send, recv, device):
    return pltpu.make_async_remote_copy(
        src_ref=src, dst_ref=dst, send_sem=send, recv_sem=recv, device_id=device, device_id_type=MESH
    )


def params(number, vmem=56):
    return pltpu.CompilerParams(
        collective_id=number, has_side_effects=True, vmem_limit_bytes=vmem * 2**20
    )


def gather_kernel(
    qo, kv, gu, dn, dy, qo_all, kv_all, gu_all, dn_all, dy_all, send_y, send_x, send_s, recv, recv_s, local
):
    x, y, z, c = place()
    xl = lax.rem(x, 2)
    f = 4 * xl + y
    sibling = at(x, y, z, 1 - c)
    lanes = pl.ds(pl.multiple_of(c * FH, 128), FH)
    greet([at(x, y + j, z, c) for j in (1, 2, 3)] + [at(x + j, y, z, c) for j in (1, 3)] + [sibling])
    holds = c == xl

    own = (qo.at[c], kv.at[c], gu.at[:, :, lanes], dn)

    def slot(item, g):
        if item == 0:
            return qo_all.at[c, g]
        if item == 1:
            return kv_all.at[c, g]
        if item == 2:
            return gu_all.at[:, g]
        return dn_all.at[lax.rem(g, 4)]

    def wait_slot(item, g):
        remote(slot(item, g), slot(item, g), send_s.at[0, 0], recv.at[item, g], sibling).wait_recv()

    def send_row(item, j):
        return remote(own[item], slot(item, f), send_y.at[item, j - 1], recv.at[item, f], at(x, y + j, z, c))

    def send_side(item, j):
        g = 4 * xl + lax.rem(y + j, 4)
        step = 3 if item == 2 else 1
        return remote(
            own[item] if j == 0 else slot(item, g),
            slot(item, g),
            send_x.at[item, j],
            recv.at[item, g],
            at(x + step, y, z, c),
        )

    def send_sib(item, k):
        g = 4 * xl + lax.rem(y + k + 1, 4) if k < 3 else 4 * (1 - xl) + lax.rem(y + k - 3, 4)
        return remote(slot(item, g), slot(item, g), send_s.at[item, k], recv_s.at[item, g], sibling)

    def other(k):
        return 4 * (1 - xl) + lax.rem(y + k, 4)

    order = (1, 3, 2)
    for item in (0, 1):
        for j in order:
            send_row(item, j).start()
        send_side(item, 0).start()
    exchange = remote(dy, dy_all.at[1], send_s.at[2, 0], recv_s.at[2, 0], sibling)
    exchange.start()
    for item in (2, 3):

        def begin(item=item):
            for j in order:
                send_row(item, j).start()
            send_side(item, 0).start()

        if item == 3:
            pl.when(holds)(begin)
        else:
            begin()
    copies = [
        pltpu.make_async_copy(qo, qo_all.at[:, f], local.at[0]),
        pltpu.make_async_copy(kv, kv_all.at[:, f], local.at[1]),
        pltpu.make_async_copy(own[2], gu_all.at[:, f], local.at[2]),
        pltpu.make_async_copy(dy, dy_all.at[0], local.at[4]),
    ]
    for copy in copies:
        copy.start()
    own_down = pltpu.make_async_copy(dn, dn_all.at[y], local.at[3])
    pl.when(holds)(own_down.start)

    for j in order:
        g = 4 * xl + lax.rem(y + j, 4)
        for item in (0, 1):
            wait_slot(item, g)
            send_side(item, j).start()
            send_sib(item, j - 1).start()
    for k in (0, 1, 3, 2):
        for item in (0, 1):
            wait_slot(item, other(k))
            send_sib(item, k + 3).start()
    for j in order:
        g = 4 * xl + lax.rem(y + j, 4)
        wait_slot(2, g)
        send_side(2, j).start()

        @pl.when(holds)
        def _():
            wait_slot(3, g)
            send_side(3, j).start()

    for k in (0, 1, 3, 2):
        wait_slot(2, other(k))
        pl.when(jnp.logical_not(holds))(functools.partial(wait_slot, 3, other(k)))

    for copy in copies:
        copy.wait()
    exchange.wait()
    for item in (0, 1):
        for k in range(7):
            g = 4 * xl + lax.rem(y + k + 1, 4) if k < 3 else other(k - 3)
            arriving = (qo_all, kv_all)[item].at[1 - c, g]
            remote(arriving, arriving, send_s.at[0, 0], recv_s.at[item, g], sibling).wait_recv()
            send_sib(item, k).wait_send()
    for item in (0, 1, 2):
        for j in order:
            send_row(item, j).wait_send()
        for j in range(4):
            send_side(item, j).wait_send()

    @pl.when(holds)
    def _():
        own_down.wait()
        for j in order:
            send_row(3, j).wait_send()
        for j in range(4):
            send_side(3, j).wait_send()


def gather_weights(qo, kv, gu, dn, dy):
    sem = pltpu.SemaphoreType.DMA
    return pl.pallas_call(
        gather_kernel,
        name="gather_weights",
        out_shape=(
            jax.ShapeDtypeStruct((2, 8, ROWS, D), BF),
            jax.ShapeDtypeStruct((2, 8, ROWS, KW), BF),
            jax.ShapeDtypeStruct((2, 8, ROWS, FH), BF),
            jax.ShapeDtypeStruct((4, KW, D), BF),
            jax.ShapeDtypeStruct((2, TOK, D), BF),
        ),
        in_specs=[ANY] * 5,
        out_specs=(ANY,) * 5,
        scratch_shapes=[sem((4, 3)), sem((4, 4)), sem((3, 7)), sem((4, 8)), sem((3, 8)), sem((5,))],
        compiler_params=params(0),
    )(qo, kv, gu, dn, dy)


def swap_kernel(count, *refs):
    ins, outs = refs[:count], refs[count : 2 * count]
    send, recv = refs[2 * count :]
    x, y, z, c = place()
    sibling = at(x, y, z, 1 - c)
    greet([sibling])
    copies = [
        remote(ins[i], outs[i], send.at[i], recv.at[i], sibling) for i in range(count)
    ]
    for copy in copies:
        copy.start()
    for copy in copies:
        copy.wait()


def swap(number, *arrays):
    count = len(arrays)
    return pl.pallas_call(
        functools.partial(swap_kernel, count),
        name="swap_%d" % number,
        out_shape=tuple(jax.ShapeDtypeStruct(a.shape, a.dtype) for a in arrays),
        in_specs=[ANY] * count,
        out_specs=(ANY,) * count,
        scratch_shapes=[pltpu.SemaphoreType.DMA((count,)), pltpu.SemaphoreType.DMA((count,))],
        compiler_params=params(number),
    )(*arrays)


def dot(a, b, ca, cb):
    return lax.dot_general(a, b, (((ca,), (cb,)), ((), ())), preferred_element_type=F32)


def attend_kernel(q, kv, cos, sin, q_low, att, lse, kv_out, keys, send, recv):
    x, y, z, c = place()
    me = 2 * (x // 2) + c
    sib_slot, far_slot, diag_slot = me + 1 - 2 * c, lax.rem(me + 2, 4), lax.rem(me + 2, 4) + 1 - 2 * c
    sibling, far = at(x, y, z, 1 - c), at(x + 2, y, z, c)
    greet([sibling, far])
    co, si = cos[...], sin[...]
    for h in range(KEY_VALUE_HEADS):
        a, b = kv[64 * h : 64 * h + 32, :], kv[64 * h + 32 : 64 * h + 64, :]
        keys[me, 64 * h : 64 * h + 32, :] = (a * co - b * si).astype(BF)
        keys[me, 64 * h + 32 : 64 * h + 64, :] = (b * co + a * si).astype(BF)
    keys[me, KW:, :] = kv[KW:, :].astype(BF)
    to_far = remote(keys.at[me], keys.at[me], send.at[0], recv.at[0], far)
    to_sib = remote(keys.at[me], keys.at[me], send.at[1], recv.at[1], sibling)
    to_far.start()
    to_sib.start()
    for h in range(QUERY_HEADS):
        a, b = q[64 * h : 64 * h + 32, :], q[64 * h + 32 : 64 * h + 64, :]
        q_low[64 * h : 64 * h + 32, :] = ((a * co - b * si).astype(BF) * score_scale).astype(BF)
        q_low[64 * h + 32 : 64 * h + 64, :] = ((b * co + a * si).astype(BF) * score_scale).astype(BF)
    remote(keys.at[far_slot], keys.at[far_slot], send.at[0], recv.at[0], far).wait_recv()
    on = remote(keys.at[far_slot], keys.at[far_slot], send.at[2], recv.at[2], sibling)
    on.start()
    remote(keys.at[sib_slot], keys.at[sib_slot], send.at[1], recv.at[1], sibling).wait_recv()
    remote(keys.at[diag_slot], keys.at[diag_slot], send.at[2], recv.at[2], sibling).wait_recv()
    gap = lax.broadcasted_iota(jnp.int32, (TOK, TOK), 0) - lax.broadcasted_iota(jnp.int32, (TOK, TOK), 1)

    def head(h, carry):
        rows = pl.ds(pl.multiple_of(h * 64, 64), 64)
        g = h // GROUP
        krows = pl.ds(pl.multiple_of(g * 64, 64), 64)
        vrows = pl.ds(pl.multiple_of(KW + g * 64, 64), 64)
        qh = q_low[rows, :]
        s = []
        for j in range(4):
            part = dot(keys[j, krows, :], qh, 0, 0)
            s.append(jnp.where(gap <= 256 * (me - j), part, -1e30))
        top = jnp.max(jnp.maximum(jnp.maximum(s[0], s[1]), jnp.maximum(s[2], s[3])), axis=0, keepdims=True)
        e = [jnp.exp(part - top) for part in s]
        total = jnp.sum(e[0] + e[1] + (e[2] + e[3]), axis=0, keepdims=True)
        acc = dot(keys[0, vrows, :], e[0].astype(BF), 1, 0)
        for j in range(1, 4):
            acc += dot(keys[j, vrows, :], e[j].astype(BF), 1, 0)
        att[rows, :] = (acc / total).astype(BF)
        lse[pl.ds(h, 1), 0, :] = top + jnp.log(total)
        return carry

    lax.fori_loop(0, QUERY_HEADS, head, 0)
    kv_out[...] = keys[...]
    to_far.wait_send()
    to_sib.wait_send()
    on.wait_send()


def attend(q, kv, cos, sin):
    sem = pltpu.SemaphoreType.DMA
    return pl.pallas_call(
        attend_kernel,
        name="attend",
        out_shape=(
            jax.ShapeDtypeStruct((D, TOK), BF),
            jax.ShapeDtypeStruct((D, TOK), BF),
            jax.ShapeDtypeStruct((16, 1, TOK), F32),
            jax.ShapeDtypeStruct((4, 2 * KW, TOK), BF),
        ),
        in_specs=[VM] * 4,
        out_specs=(VM,) * 4,
        scratch_shapes=[pltpu.VMEM((4, 2 * KW, TOK), BF), sem((3,)), sem((3,))],
        compiler_params=params(1),
    )(q, kv, cos, sin)


def attend_back_kernel(
    q_low, keys, lse, att, grad, cos, sin, q_back, kv_back, mine, got, far_got, acc, send, recv
):
    x, y, z, c = place()
    me = 2 * (x // 2) + c
    far_slot = lax.rem(me + 2, 4)
    sib_slot = me + 1 - 2 * c
    diag_slot = far_slot + 1 - 2 * c
    sibling, far = at(x, y, z, 1 - c), at(x + 2, y, z, c)
    greet([sibling, far])
    co, si = cos[...], sin[...]
    gap = lax.broadcasted_iota(jnp.int32, (TOK, TOK), 0) - lax.broadcasted_iota(jnp.int32, (TOK, TOK), 1)

    def group(g, carry):
        krows = pl.ds(pl.multiple_of(g * 64, 64), 64)
        vrows = pl.ds(pl.multiple_of(KW + g * 64, 64), 64)

        def head(t, inner):
            h = g * GROUP + t
            rows = pl.ds(pl.multiple_of(h * 64, 64), 64)
            qh, gh = q_low[rows, :], grad[rows, :]
            row_dot = jnp.sum(gh.astype(F32) * att[rows, :].astype(F32), axis=0, keepdims=True)
            level = lse[pl.ds(h, 1), 0, :]
            dq = jnp.zeros((64, TOK), F32)
            for j in range(4):
                s = dot(keys[j, krows, :], qh, 0, 0)
                s = jnp.where(gap <= 256 * (me - j), s, -1e30)
                p = jnp.exp(s - level)
                dp = dot(keys[j, vrows, :], gh, 0, 0)
                ds = (p * (dp - row_dot)).astype(BF)
                pb = p.astype(BF)
                dq += dot(keys[j, krows, :], ds, 1, 0)
                dk = dot(qh, ds, 1, 1)
                dv = dot(gh, pb, 1, 1)
                first = t == 0
                acc[j, 0] = jnp.where(first, dk, acc[j, 0] + dk)
                acc[j, 1] = jnp.where(first, dv, acc[j, 1] + dv)
            dq = dq * score_scale
            a, b = dq[:32], dq[32:]
            q_back[pl.ds(pl.multiple_of(h * 64, 32), 32), :] = (a * co + b * si).astype(BF)
            q_back[pl.ds(pl.multiple_of(h * 64 + 32, 32), 32), :] = (b * co - a * si).astype(BF)
            return inner

        lax.fori_loop(0, GROUP, head, 0)
        for j in range(4):
            mine[j, krows, :] = acc[j, 0].astype(BF)
            mine[j, vrows, :] = acc[j, 1].astype(BF)
        return carry

    acc[...] = jnp.zeros_like(acc)
    lax.fori_loop(0, KEY_VALUE_HEADS, group, 0)
    to_sib_far = remote(mine.at[diag_slot], got.at[1], send.at[0], recv.at[0], sibling)
    to_sib = remote(mine.at[sib_slot], got.at[0], send.at[1], recv.at[1], sibling)
    to_sib_far.start()
    to_sib.start()
    to_sib_far.wait_recv()
    got[1] = (mine[far_slot].astype(F32) + got[1].astype(F32)).astype(BF)
    to_far = remote(got.at[1], far_got, send.at[2], recv.at[2], far)
    to_far.start()
    to_sib.wait_recv()
    near = mine[me].astype(F32) + got[0].astype(F32)
    to_far.wait_recv()
    total = near + far_got[...].astype(F32)
    for h in range(KEY_VALUE_HEADS):
        a, b = total[64 * h : 64 * h + 32, :], total[64 * h + 32 : 64 * h + 64, :]
        kv_back[64 * h : 64 * h + 32, :] = (a * co + b * si).astype(BF)
        kv_back[64 * h + 32 : 64 * h + 64, :] = (b * co - a * si).astype(BF)
    kv_back[KW:, :] = total[KW:, :].astype(BF)
    to_sib_far.wait_send()
    to_sib.wait_send()
    to_far.wait_send()


def attend_back(q_low, keys, lse, att, grad, cos, sin):
    sem = pltpu.SemaphoreType.DMA
    return pl.pallas_call(
        attend_back_kernel,
        name="attend_back",
        out_shape=(
            jax.ShapeDtypeStruct((D, TOK), BF),
            jax.ShapeDtypeStruct((2 * KW, TOK), BF),
        ),
        in_specs=[VM] * 7,
        out_specs=(VM,) * 2,
        scratch_shapes=[
            pltpu.VMEM((4, 2 * KW, TOK), BF),
            pltpu.VMEM((2, 2 * KW, TOK), BF),
            pltpu.VMEM((2 * KW, TOK), BF),
            pltpu.VMEM((4, 2, 64, TOK), F32),
            sem((3,)),
            sem((3,)),
        ],
        compiler_params=params(2),
    )(q_low, keys, lse, att, grad, cos, sin)


def add_up(out, own, got):
    out[...] = (
        own[...].astype(F32) + got[0].astype(F32) + (got[1].astype(F32) + got[2].astype(F32))
    ).astype(BF)


def reduce_kernel(
    a, b, cc, d,
    a_sum, b_sum, c_sum, d_sum,
    a1, a1r, a2, a2r, a3, a3r,
    b1, b1r, b2, b2r, b3, b3r,
    d1, d1r, d2, d2r, d3, d3r,
    c1, c1r, c2, c2r, c3, c3r,
    send1, recv1, send2, recv2, send3, recv3, send4, recv4, send5, recv5, local,
):
    x, y, z, c = place()
    xl = lax.rem(x, 2)
    holds = c == xl
    sibling = at(x, y, z, 1 - c)
    along_x = [at(x + j, y, z, c) for j in (1, 2, 3)]
    along_y = [at(x, y + j, z, c) for j in (1, 2, 3)]
    along_z = [at(x, y, z + j, c) for j in (1, 2, 3)]
    greet(along_x + along_y + along_z + [sibling])
    offsets = (1, 3, 2)
    A, B, C, DN = 0, 1, 2, 3

    def quarter(index):
        index = lax.rem(index, 4)
        return index // 2, pl.ds(pl.multiple_of(640 * lax.rem(index, 2), 128), 640)

    def rows(index, size):
        return pl.ds(pl.multiple_of(lax.rem(index, 4) * size, 16), size)

    def first(item, j):
        to = lax.rem(y + j, 4)
        if item == C:
            m, lanes = quarter(z + j)
            return remote(cc.at[m, :, :, :, lanes], c1r.at[j - 1], send1.at[C, j - 1], recv1.at[C, j - 1], along_z[j - 1])
        src, dst = {
            A: (a.at[:, to], a1r), B: (b.at[:, to], b1r), DN: (d.at[to], d1r)
        }[item]
        return remote(src, dst.at[j - 1], send1.at[item, j - 1], recv1.at[item, j - 1], along_y[j - 1])

    for j in offsets:
        for item in (C, DN, A, B):
            first(item, j).start()
    m, lanes = quarter(z)
    copies = [
        pltpu.make_async_copy(a.at[:, y], a1, local.at[0]),
        pltpu.make_async_copy(b.at[:, y], b1, local.at[1]),
        pltpu.make_async_copy(cc.at[m, :, :, :, lanes], c1, local.at[2]),
        pltpu.make_async_copy(d.at[y], d1, local.at[3]),
    ]
    for copy in copies:
        copy.start()
    for copy in copies:
        copy.wait()

    def second(item, j):
        if item == C:
            return remote(c1.at[:, lax.rem(y + j, 4)], c2r.at[j - 1], send2.at[C, j - 1], recv2.at[C, j - 1], along_y[j - 1])
        if item == DN:
            return remote(d1, d2r.at[j - 1], send2.at[DN, j - 1], recv2.at[DN, j - 1], along_x[j - 1])
        src, dst = ((a1, a2r), (b1, b2r))[item]
        side = xl if j == 2 else 1 - xl
        return remote(src.at[side], dst.at[j - 1], send2.at[item, j - 1], recv2.at[item, j - 1], along_x[j - 1])

    for j in (1, 2, 3):
        first(DN, j).wait_recv()
    add_up(d1, d1, d1r)
    pl.when(holds)(lambda: second(DN, 2).start())

    @pl.when(jnp.logical_not(holds))
    def _():
        second(DN, 1).start()
        second(DN, 3).start()

    for item, own, got in ((A, a1, a1r), (B, b1, b1r)):
        for j in (1, 2, 3):
            first(item, j).wait_recv()
        add_up(own, own, got)
        for j in offsets:
            second(item, j).start()
    for j in (1, 2, 3):
        first(C, j).wait_recv()

    @pl.loop(0, 2)
    def _(i):
        for k in range(4):
            c1[i, k] = (
                c1[i, k].astype(F32)
                + c1r[0, i, k].astype(F32)
                + (c1r[1, i, k].astype(F32) + c1r[2, i, k].astype(F32))
            ).astype(BF)

    for j in offsets:
        second(C, j).start()

    def third(item, j):
        if item == C:
            side = xl if j == 2 else 1 - xl
            return remote(c2.at[side], c3r.at[j - 1], send3.at[C, j - 1], recv3.at[C, j - 1], along_x[j - 1])
        src, dst, size = {A: (a2, a3r, 32), B: (b2, b3r, 32), DN: (d2, d3r, 80)}[item]
        return remote(
            src.at[rows(z + j, size)], dst.at[j - 1], send3.at[item, j - 1], recv3.at[item, j - 1], along_z[j - 1]
        )

    @pl.when(holds)
    def _():
        for j in (1, 2, 3):
            second(DN, j).wait_recv()
        add_up(d2, d1, d2r)
        for j in offsets:
            third(DN, j).start()

    for item, out, own, got in ((A, a2, a1, a2r), (B, b2, b1, b2r)):
        for j in (1, 2, 3):
            second(item, j).wait_recv()
        add_up(out, own.at[xl], got)
        for j in offsets:
            third(item, j).start()
    for j in (1, 2, 3):
        second(C, j).wait_recv()
    for i in range(2):
        c2[i] = (
            c1[i, y].astype(F32)
            + c2r[0, i].astype(F32)
            + (c2r[1, i].astype(F32) + c2r[2, i].astype(F32))
        ).astype(BF)
    for j in offsets:
        third(C, j).start()

    def summed(item, index):
        if item == C:
            m, _ = quarter(index)
            start = FH * c + 640 * lax.rem(index, 2)
            return c_sum.at[m, :, pl.ds(pl.multiple_of(start, 128), 640)]
        if item == DN:
            return d_sum.at[rows(index, 80)]
        return (a_sum, b_sum)[item].at[c, rows(index, 32)]

    part = {A: a3, B: b3, C: c3, DN: d3}

    def spread(item, j):
        return remote(
            part[item], summed(item, z), send4.at[item, j - 1], recv4.at[item, j - 1], along_z[j - 1]
        )

    def keep(item):
        return pltpu.make_async_copy(part[item], summed(item, z), local.at[item])

    def landed(item, j):
        ref = summed(item, lax.rem(z + 4 - j, 4))
        remote(ref, ref, send4.at[item, j - 1], recv4.at[item, j - 1], sibling).wait_recv()

    @pl.when(holds)
    def _():
        for j in (1, 2, 3):
            third(DN, j).wait_recv()
        add_up(d3, d2.at[rows(z, 80)], d3r)
        for j in offsets:
            spread(DN, j).start()
        keep(DN).start()

    for item, out, own, got in ((A, a3, a2, a3r), (B, b3, b2, b3r)):
        for j in (1, 2, 3):
            third(item, j).wait_recv()
        add_up(out, own.at[rows(z, 32)], got)
        for j in offsets:
            spread(item, j).start()
        keep(item).start()
    for j in (1, 2, 3):
        third(C, j).wait_recv()
    add_up(c3, c2.at[xl], c3r)
    for j in offsets:
        spread(C, j).start()
    keep(C).start()

    def whole(item, core):
        if item == C:
            return c_sum.at[:, :, pl.ds(pl.multiple_of(FH * core, 128), FH)]
        if item == DN:
            return d_sum
        return (a_sum, b_sum)[item].at[core]

    def across(item):
        return remote(whole(item, c), whole(item, c), send5.at[item], recv5.at[item], sibling)

    def arrive(item):
        ref = whole(item, 1 - c)
        remote(ref, ref, send5.at[item], recv5.at[item], sibling).wait_recv()

    @pl.when(holds)
    def _():
        keep(DN).wait()
        for j in (1, 2, 3):
            landed(DN, j)
        across(DN).start()

    for item in (A, B, C):
        keep(item).wait()
        for j in (1, 2, 3):
            landed(item, j)
        across(item).start()
    for item in (A, B, C):
        arrive(item)
    pl.when(jnp.logical_not(holds))(lambda: arrive(DN))

    for item in (A, B, C):
        for j in (1, 2, 3):
            first(item, j).wait_send()
            second(item, j).wait_send()
            third(item, j).wait_send()
            spread(item, j).wait_send()
        across(item).wait_send()
    for j in (1, 2, 3):
        first(DN, j).wait_send()

    @pl.when(holds)
    def _():
        second(DN, 2).wait_send()
        for j in (1, 2, 3):
            third(DN, j).wait_send()
            spread(DN, j).wait_send()
        across(DN).wait_send()

    @pl.when(jnp.logical_not(holds))
    def _():
        second(DN, 1).wait_send()
        second(DN, 3).wait_send()


def reduce_gradients(a, b, c, d):
    sem = pltpu.SemaphoreType.DMA
    vm = lambda *shape: pltpu.VMEM(shape, BF)

    def planes(width):
        return [
            vm(2, PAD, width), vm(3, 2, PAD, width), vm(PAD, width), vm(3, PAD, width),
            vm(32, width), vm(3, 32, width),
        ]

    return pl.pallas_call(
        reduce_kernel,
        name="reduce_gradients",
        out_shape=(
            jax.ShapeDtypeStruct((2, PAD, D), BF),
            jax.ShapeDtypeStruct((2, PAD, KW), BF),
            jax.ShapeDtypeStruct((2, ROWS, FF), BF),
            jax.ShapeDtypeStruct((KW, D), BF),
        ),
        in_specs=[ANY] * 4,
        out_specs=(ANY,) * 4,
        scratch_shapes=planes(D)
        + planes(KW)
        + [vm(KW, D), vm(3, KW, D), vm(KW, D), vm(3, KW, D), vm(80, D), vm(3, 80, D)]
        + [
            vm(2, 4, ROWS, 640), vm(3, 2, 4, ROWS, 640), vm(2, ROWS, 640), vm(3, 2, ROWS, 640),
            vm(ROWS, 640), vm(3, ROWS, 640),
        ]
        + [sem((4, 3))] * 8
        + [sem((4,))] * 3,
        compiler_params=params(3),
    )(
        a.reshape(2, 4, PAD, D),
        b.reshape(2, 4, PAD, KW),
        c.reshape(2, 2, 4, ROWS, FH),
        d.reshape(4, KW, D),
    )


def matmul(left, right):
    return jnp.dot(left, right, preferred_element_type=F32)


def rms_scale(stream):
    return lax.rsqrt(jnp.mean(stream * stream, axis=-1, keepdims=True) + norm_epsilon)


def norm_backward(stream, gain_row, incoming):
    scale = rms_scale(stream)
    normal = stream * scale
    gain_grad = jnp.sum(incoming * normal, axis=0)
    scaled = incoming * gain_row
    stream_grad = scale * (scaled - normal * jnp.mean(scaled * normal, axis=-1, keepdims=True))
    return (stream_grad, gain_grad)


def adamw_update(weight, gradient, first, second, rate, decay):
    weight = weight.astype(F32)
    first_new = beta_first * first.astype(F32) + (1.0 - beta_first) * gradient
    second_new = beta_second * second.astype(F32) + (1.0 - beta_second) * gradient * gradient
    first_hat = first_new / (1.0 - beta_first**STEP)
    second_hat = second_new / (1.0 - beta_second**STEP)
    weight_new = weight - rate * (
        first_hat / (jnp.sqrt(second_hat) + adam_epsilon) + decay * weight
    )
    return (weight_new, first_new, second_new)


def body(
    tokens,
    cotangent,
    query_weight,
    keyval_weight,
    output_weight,
    gateup_weight,
    down_weight,
    norm_gains,
    query_first,
    keyval_first,
    output_first,
    gateup_first,
    down_first,
    gains_first,
    query_second,
    keyval_second,
    output_second,
    gateup_second,
    down_second,
    gains_second,
):
    ctx = lax.axis_index("ctx")
    core = lax.rem(ctx, 2)
    gains = lax.all_gather(norm_gains, "fsdp", axis=1, tiled=True).astype(F32)
    qo_all, kv_all, gu_all, dn_all, dy_all = gather_weights(
        jnp.stack([query_weight, output_weight]), keyval_weight, gateup_weight, down_weight, cotangent[0]
    )
    query_full, output_full = qo_all[0].reshape(D, D), qo_all[1].reshape(D, D)
    key_full, value_full = kv_all[0].reshape(D, KW), kv_all[1].reshape(D, KW)
    gate_full, up_full = gu_all[0].reshape(D, FH), gu_all[1].reshape(D, FH)
    down_full = dn_all.reshape(FH, D)
    both_dy = dy_all.reshape(2 * TOK, D)

    stream = tokens[0].astype(F32)
    positions = (ctx * TOK + jnp.arange(TOK, dtype=jnp.int32)).astype(F32)
    counter = jnp.arange(HALF, dtype=F32)
    frequency = 1.0 / rotary_base ** (counter * (2.0 / HEAD_WIDTH))
    angles = frequency[:, None] * positions[None, :]
    cosine, sine = jnp.cos(angles), jnp.sin(angles)

    normed_one = (stream * rms_scale(stream) * gains[0]).astype(BF)
    turn = lambda w, n: lax.dot_general(w, n, (((0,), (1,)), ((), ())), preferred_element_type=F32)
    query_t = turn(query_full, normed_one)
    keyval_t = jnp.concatenate([turn(key_full, normed_one), turn(value_full, normed_one)])
    query_low, attended_t, level, keys = attend(query_t, keyval_t, cosine, sine)
    attended = attended_t.T
    middle = stream + matmul(attended, output_full)
    normed_two = (middle * rms_scale(middle) * gains[1]).astype(BF)
    (normed_other,) = swap(4, normed_two)
    both_two = jnp.concatenate([normed_two, normed_other])
    gate = matmul(both_two, gate_full)
    upward = matmul(both_two, up_full)
    sigmoid_gate = jax.nn.sigmoid(gate)
    hidden = (gate * sigmoid_gate * upward).astype(BF)
    down_part = matmul(hidden, down_full)
    hidden_grad = matmul(both_dy, down_full.T)
    gate_grad = (hidden_grad * upward * sigmoid_gate * (1.0 + gate * (1.0 - sigmoid_gate))).astype(BF)
    up_grad = (hidden_grad * gate * sigmoid_gate).astype(BF)
    two_part = matmul(gate_grad, gate_full.T) + matmul(up_grad, up_full.T)
    down_other, two_other = swap(5, down_part[TOK:], two_part[TOK:])
    result = middle + down_part[:TOK] + down_other
    normed_two_grad = two_part[:TOK] + two_other
    grad_down = matmul(hidden.T, both_dy).astype(BF)
    grad_gateup = jnp.stack(
        [matmul(both_two.T, gate_grad).astype(BF), matmul(both_two.T, up_grad).astype(BF)]
    )

    incoming = cotangent[0].astype(F32)
    middle_norm_grad, gain_two_grad = norm_backward(middle, gains[1], normed_two_grad)
    middle_grad = incoming + middle_norm_grad
    middle_low = middle_grad.astype(BF)
    attended_grad_t = lax.dot_general(
        output_full, middle_low, (((1,), (1,)), ((), ())), preferred_element_type=F32
    ).astype(BF)
    query_back_t, keyval_back_t = attend_back(
        query_low, keys, level, attended_t, attended_grad_t, cosine, sine
    )
    query_back = query_back_t.T
    key_back, value_back = keyval_back_t[:KW].T, keyval_back_t[KW:].T

    zero = core == 0
    left_out, left_in = jnp.where(zero, attended, normed_one), jnp.where(zero, normed_one, attended)
    right_out, right_in = jnp.where(zero, middle_low, query_back), jnp.where(zero, query_back, middle_low)
    narrow_out, narrow_in = jnp.where(zero, value_back, key_back), jnp.where(zero, key_back, value_back)
    left_got, right_got, narrow_got, one_got = swap(6, left_out, right_out, narrow_out, normed_one)

    def padded(rows):
        return jnp.pad(rows.reshape(2 * TOK, 8, ROWS), ((0, 0), (0, 0), (0, PAD - ROWS))).reshape(2 * TOK, 8 * PAD)

    grad_wide = matmul(
        padded(jnp.concatenate([left_in, left_got])).T, jnp.concatenate([right_in, right_got])
    ).astype(BF)
    grad_narrow = matmul(
        padded(jnp.concatenate([normed_one, one_got])).T, jnp.concatenate([narrow_in, narrow_got])
    ).astype(BF)

    normed_one_grad = (
        matmul(query_back, query_full.T) + matmul(key_back, key_full.T) + matmul(value_back, value_full.T)
    )
    stream_norm_grad, gain_one_grad = norm_backward(stream, gains[0], normed_one_grad)
    input_grad = middle_grad + stream_norm_grad
    grad_gains = jnp.stack([gain_one_grad, gain_two_grad]).reshape(2, 8, ROWS).transpose(1, 0, 2).astype(BF)
    grad_wide = grad_wide.reshape(8, PAD, D).at[:, ROWS : ROWS + 2, :ROWS].set(grad_gains)

    wide, narrow, gateup, down = reduce_gradients(grad_wide, grad_narrow, grad_gateup, grad_down)
    gains_sum = wide[0, ROWS : ROWS + 2, :ROWS].astype(F32) + wide[1, ROWS : ROWS + 2, :ROWS].astype(F32)
    summed = (
        wide[0, :ROWS].astype(F32),
        narrow[:, :ROWS].astype(F32),
        wide[1, :ROWS].astype(F32),
        gateup.astype(F32),
        down.astype(F32),
        gains_sum,
    )
    shards = (query_weight, keyval_weight, output_weight, gateup_weight, down_weight, norm_gains)
    firsts = (query_first, keyval_first, output_first, gateup_first, down_first, gains_first)
    seconds = (query_second, keyval_second, output_second, gateup_second, down_second, gains_second)
    rates = (matrix_rate,) * 5 + (gain_rate,)
    decays = (matrix_decay,) * 5 + (0.0,)
    updated = [
        adamw_update(shards[i], summed[i], firsts[i], seconds[i], rates[i], decays[i])
        for i in range(6)
    ]
    return (
        result.astype(BF)[None],
        input_grad[None],
        *[updated[i][0] for i in range(6)],
        *[updated[i][1] for i in range(6)],
        *[updated[i][2] for i in range(6)],
    )


def solution(mesh):
    row, mid = P("fsdp", None), P(None, "fsdp", None)
    weights = (row, mid, row, mid, row, P(None, "fsdp"))
    stream = P(("rep", "fsdp"), "ctx", None)
    return jax.shard_map(
        body,
        mesh=mesh,
        in_specs=(stream, stream) + weights * 3,
        out_specs=(stream, stream) + weights * 3,
        check_vma=False,
    )
```

time: 925 us -> 396 us (0.43)
  waiting for transfers between devices: 587 us -> 0 us
  Pallas kernels: 0 us -> 265 us
  blocking collectives: 99.1 us -> 14.8 us
  matrix products: 101 us -> 34.9 us
  local copies, waits for them, and re-layouts: 82 us -> 42.9 us
  between operations: 15.7 us -> 1.75 us
    pallas_call x0 -> x7, Pallas kernels: none -> 265 us  [the longest x1 104 us: reduce_gradients(): pl.pallas_call(reduce_kernel, name='reduce_gradients', out_shape=(jax.Sha...]
    all_gather x5 -> x0, waiting for transfers between devices: 202 us -> none  [the longest x1 109 us: body(): lax.all_gather(gateup_weight, 'fsdp', axis=1, tiled=True)]
    reduce_scatter x5 -> x0, waiting for transfers between devices: 197 us -> none  [the longest x1 69.5 us: body(): lax.psum_scatter(grad_down.astype(jnp.bfloat16), 'fsdp', scatter_dimensio...]
    unnamed x15 -> x0, waiting for transfers between devices: 98.5 us -> none
    psum x1 -> x0, waiting for transfers between devices: 89 us -> none  [body(): lax.psum(owned[0].astype(jnp.bfloat16), ('rep', 'ctx')).astype(jnp.float32)]
    dot_general x26 -> x19, matrix products: 92.4 us -> 34.9 us  [the longest x15 27.9 us: matmul(): return jnp.dot(left, right, preferred_element_type=F32)]
    unnamed x122, local copies, waits for them, and re-layouts: 74.4 us -> 18.4 us
    psum x1 -> x0, blocking collectives: 36.1 us -> none  [body(): lax.psum(owned[5].astype(jnp.bfloat16), ('rep', 'ctx')).astype(jnp.float32)]
  transfers between devices with their start and end apart: 13 -> 0, of which waited for: 12 -> 0; matrix products, arithmetic and copies ran while one was open for 17% -> 0% of each run, Pallas kernels for 0% -> 0%
where the time goes in v1:
time: 396 us; the launch traced here: 392 us
  Pallas kernels  265 us (67%)
  local copies, waits for them, and re-layouts  42.9 us (11%)
  matrix products  34.9 us (9%)
  other arithmetic  32 us (8%)
  blocking collectives  14.8 us (4%)
    pallas_call x1, Pallas kernels, reduce_gradients(): pl.pallas_call(reduce_kernel, name='reduce_gradients', out_shape=(jax.Sha...  104 us
    pallas_call x1, Pallas kernels, gather_weights(): pl.pallas_call(gather_kernel, name='gather_weights', out_shape=(jax.Shape...  82 us
    pallas_call x1, Pallas kernels, attend_back(): pl.pallas_call(attend_back_kernel, name='attend_back', out_shape=(jax.Sha...  34.9 us
    pallas_call x1, Pallas kernels, attend(): pl.pallas_call(attend_kernel, name='attend', out_shape=(jax.ShapeDtypeStr...  33.2 us
    dot_general x15, matrix products, matmul(): return jnp.dot(left, right, preferred_element_type=F32)  27.9 us
    unnamed x122, local copies, waits for them, and re-layouts  18.4 us
    all_gather x1, blocking collectives, body(): gains = lax.all_gather(norm_gains, 'fsdp', axis=1, tiled=True).astype(F32)  14.8 us
    sub x4, other arithmetic, adamw_update(): weight - rate * (first_hat / (jnp.sqrt(second_hat) + adam_epsilon) + deca...  13.9 us

profile of v1, /device:TPU:1, one launch (start us, length us, event | category | flops | bytes accessed | tf_op | source)
XLA Modules:
  0.0 391.5 jit_solution(11222143331050264725)
XLA Ops:
  6.3 82.0 %gather_weights.1 = (bf16[2,8,120,960]{3,2,1,0:T(8,128)(2,1)}, bf16[2,8,120,320]{3,2,1,0:T(8,128)(2,1)}, bf16[2,8,120,1280]{3,2,1,0:T(8,128)(2,1)}, bf16[4,320,960]{2,1,0:T(8,128)(2,1)}, bf16[2,256,960]{2,1,0:T(8,128)(2,1)}) custom-call(bf16[2,120,960]{2,1,0:T(8,128)(2,1)} %pad_maximum_fusion.5.qo, bf16[2,120,320]{2,1,0:T(8,128)(2,1)} %copy.128.kv, ...), custom_call_target="tpu_custom_call" | custom-call | tf_op jit(solution)/shard_map/gather_weights/pallas_call | solution.py:197
  88.3 3.9 %fusion.75 = (bf16[1,8,120,960]{3,2,1,0:T(8,128)(2,1)S(1)}, bf16[1,8,120,960]{3,2,1,0:T(8,128)(2,1)}) fusion(bf16[2,8,120,960]{3,2,1,0:T(8,128)(2,1)} %get-tuple-element.53), kind=kLoop, calls=%fused_computation.132 | loop fusion | bytes 7372800 | tf_op jit(solution)/shard_map/slice | solution.py:742
  92.5 14.8 %all-gather = bf16[8,120,2]{1,2,0:T(2,128)(2,1)S(1)} all-gather(bf16[1,120,2]{1,2,0:T(2,128)(2,1)S(1)} %bitcast.164), channel_id=1, replica_groups=mesh['rep'=4,'fsdp'=8,'ctx'=4] {'fsdp'}, dimensions={0}, use_global_device_ids=true | all-gather | bytes 4320 | tf_op jit(solution)/shard_map/all_gather | solution.py:738
  107.6 3.4 fusion.61.q
  113.8 33.2 %attend.1 = (bf16[960,256]{1,0:T(8,128)(2,1)}, bf16[960,256]{1,0:T(8,128)(2,1)}, f32[16,1,256]{2,1,0:T(1,128)}, bf16[4,640,256]{2,1,0:T(8,128)(2,1)}) custom-call(f32[960,256]{1,0:T(8,128)} %fusion.61.q, f32[640,256]{1,0:T(8,128)} %pad_maximum_fusion.4.kv, f32[32,256]{1,0:T(8,128)} %get-tuple-element.201.cos, f32[32,256]{1,0:T(8,128)} %get-tuple-element.200.sin), custom_call_target="tpu_custom_call" | custom-call | tf_op jit(solution)/shard_map/attend/pallas_call | solution.py:302
  148.9 4.2 %fusion.74 = (bf16[1,8,120,1280]{3,2,1,0:T(8,128)(2,1)}, bf16[1,8,120,1280]{3,2,1,0:T(8,128)(2,1)S(1)}) fusion(bf16[2,8,120,1280]{3,2,1,0:T(8,128)(2,1)} %get-tuple-element.56), kind=kLoop, calls=%fused_computation.131 | loop fusion | bytes 9830400 | tf_op jit(solution)/shard_map/slice | solution.py:744
  156.4 3.6 fusion.56
  162.1 3.8 multiply_convert_fusion
  170.3 2.5 copy.163
  172.8 3.7 fusion.79
  179.0 2.5 copy.162.refs_1_
  181.5 4.5 %swap_5.1 = (f32[256,960]{1,0:T(8,128)}, f32[256,960]{1,0:T(8,128)}) custom-call(f32[256,960]{1,0:T(8,128)} %slice.109.refs_0_, f32[256,960]{1,0:T(8,128)} %copy.162.refs_1_), custom_call_target="tpu_custom_call" | custom-call | tf_op jit(solution)/shard_map/swap_5/pallas_call | solution.py:231
  188.4 2.8 multiply_add_fusion
  193.2 2.7 convolution_convert_fusion.5.grad
  195.9 34.9 %attend_back.1 = (bf16[960,256]{1,0:T(8,128)(2,1)}, bf16[640,256]{1,0:T(8,128)(2,1)}) custom-call(bf16[960,256]{1,0:T(8,128)(2,1)} %get-tuple-element.61.q_low, bf16[4,640,256]{2,1,0:T(8,128)(2,1)} %get-tuple-element.62.keys, f32[16,1,256]{2,1,0:T(1,128)} %get-tuple-element.63.lse, bf16[960,256]{1,0:T(8,128)(2,1)} %get-tuple-element.55.att, ...), custom_call_target="tpu_custom_call" | custom-call | tf_op jit(solution)/shard_map/attend_back/pallas_call | solution.py:393
  241.3 4.4 %swap_6.1 = (bf16[256,960]{1,0:T(8,128)(2,1)}, bf16[256,960]{1,0:T(8,128)(2,1)}, bf16[256,320]{1,0:T(8,128)(2,1)}, bf16[256,960]{1,0:T(8,128)(2,1)}) custom-call(bf16[256,960]{1,0:T(8,128)(2,1)} %get-tuple-element.205.refs_0_, bf16[256,960]{1,0:T(8,128)(2,1)} %get-tuple-element.185.refs_1_, bf16[256,320]{1,0:T(8,128)(2,1)} %get-tuple-element.197.refs_2_, ...), custom_call_target="tpu_custom_call" | custom-call | tf_op jit(solution)/shard_map/swap_6/pallas_call | solution.py:231
  248.0 2.5 convolution_convert_fusion.3
  250.6 2.9 copy.161
  262.0 2.6 pad_maximum_fusion.cc
  266.2 3.6 copy.147
  269.8 103.9 %reduce_gradients.1 = (bf16[2,128,960]{2,1,0:T(8,128)(2,1)}, bf16[2,128,320]{2,1,0:T(8,128)(2,1)}, bf16[2,120,2560]{2,1,0:T(8,128)(2,1)}, bf16[320,960]{1,0:T(8,128)(2,1)}) custom-call(bf16[2,4,128,960]{3,2,1,0:T(8,128)(2,1)} %bitcast.133, bf16[2,4,128,320]{3,2,1,0:T(8,128)(2,1)} %bitcast.139, bf16[2,2,4,120,1280]{4,3,2,1,0:T(8,128)(2,1)} %pad_maximum_fusion.cc, ...), custom_call_target="tpu_custom_call" | custom-call | tf_op jit(solution)/shard_map/reduce_gradients/pallas_call | solution.py:656
  373.8 3.3 convert_subtract_fusion.2
  378.8 6.7 %convert_subtract_fusion = (f32[2,120,2560]{2,1,0:T(8,128)}, f32[2,120,2560]{2,1,0:T(8,128)}, f32[2,120,2560]{2,1,0:T(8,128)}) fusion(bf16[2,120,2560]{2,1,0:T(8,128)(2,1)S(1)} %copy-done.6, bf16[2,120,2560]{2,1,0:T(8,128)(2,1)} %get-tuple-element.72, bf16[2,120,2560]{2,1,0:T(8,128)(2,1)} %param.33, bf16[2,120,2560]{2,1,0:T(8,128)(2,1)} %param.39), kind=kLoop, calls=%fused_computation.6 | loop fusion | flops 11673600 | bytes 12288000 | tf_op jit(solution)/shard_map/sub | solution.py:708
  385.5 2.8 convert_subtract_fusion.1
  (173 shorter events, 54.6 us)
Async XLA Ops:
  88.3 4.0 %copy-start.31 = (bf16[1,256,960]{1,2,0:T(8,128)(2,1)S(1)}, bf16[1,256,960]{1,2,0:T(8,128)(2,1)}, u32[]{:S(2)}) copy-start(bf16[1,256,960]{1,2,0:T(8,128)(2,1)} %param.22) | copy-start | bytes 1474564
  88.3 4.2 %copy-start.41 = (bf16[2,120]{1,0:T(2,128)(2,1)S(1)}, bf16[2,120]{1,0:T(2,128)(2,1)}, u32[]{:S(2)}) copy-start(bf16[2,120]{1,0:T(2,128)(2,1)} %param.29) | copy-start | bytes 1444
  107.6 3.4 copy-start.21
  156.4 3.6 copy-start.16
  156.4 3.6 copy-start.28
  162.1 3.8 copy-start.15
  181.5 4.6 %copy-start.1 = (f32[256,960]{1,0:T(8,128)S(1)}, f32[256,960]{1,0:T(8,128)}, u32[]{:S(2)}) copy-start(f32[256,960]{1,0:T(8,128)} %copy.163) | copy-start | bytes 2949124
  181.5 6.9 %copy-start.19 = (f32[512,960]{1,0:T(8,128)S(1)}, f32[512,960]{1,0:T(8,128)}, u32[]{:S(2)}) copy-start(f32[512,960]{1,0:T(8,128)} %copy-done.18) | copy-start | bytes 5898244
  195.9 34.9 %copy-start.5 = (bf16[1,8,120,960]{3,2,1,0:T(8,128)(2,1)S(1)}, bf16[1,8,120,960]{3,2,1,0:T(8,128)(2,1)}, u32[]{:S(2)}) copy-start(bf16[1,8,120,960]{3,2,1,0:T(8,128)(2,1)} %get-tuple-element.181) | copy-start | bytes 5529604
  250.6 3.6 copy-start.4
  250.6 3.6 copy-start.30
  269.8 103.9 %copy-start.22 = (bf16[120,960]{1,0:T(8,128)(2,1)S(1)}, bf16[120,960]{1,0:T(8,128)(2,1)}, u32[]{:S(2)}) copy-start(bf16[120,960]{1,0:T(8,128)(2,1)} %param.26) | copy-start | bytes 691204
  269.8 103.9 %copy-start.23 = (bf16[120,960]{1,0:T(8,128)(2,1)S(1)}, bf16[120,960]{1,0:T(8,128)(2,1)}, u32[]{:S(2)}) copy-start(bf16[120,960]{1,0:T(8,128)(2,1)} %param.24) | copy-start | bytes 691204
  269.8 104.0 %copy-start.32 = (bf16[120,960]{1,0:T(8,128)(2,1)S(1)}, bf16[120,960]{1,0:T(8,128)(2,1)}, u32[]{:S(2)}) copy-start(bf16[120,960]{1,0:T(8,128)(2,1)} %param.32) | copy-start | bytes 691204
  269.8 104.0 %copy-start.33 = (bf16[120,960]{1,0:T(8,128)(2,1)S(1)}, bf16[120,960]{1,0:T(8,128)(2,1)}, u32[]{:S(2)}) copy-start(bf16[120,960]{1,0:T(8,128)(2,1)} %param.38) | copy-start | bytes 691204
  269.8 104.0 %copy-start.34 = (bf16[120,960]{1,0:T(8,128)(2,1)S(1)}, bf16[120,960]{1,0:T(8,128)(2,1)}, u32[]{:S(2)}) copy-start(bf16[120,960]{1,0:T(8,128)(2,1)} %param.36) | copy-start | bytes 691204
  269.8 104.0 %copy-start.35 = (bf16[120,960]{1,0:T(8,128)(2,1)S(1)}, bf16[120,960]{1,0:T(8,128)(2,1)}, u32[]{:S(2)}) copy-start(bf16[120,960]{1,0:T(8,128)(2,1)} %param.30) | copy-start | bytes 691204
  373.8 3.5 copy-start.39
  373.8 3.7 copy-start.20
  373.8 3.7 copy-start.37
  378.8 6.7 %copy-start.14 = (bf16[320,960]{1,0:T(8,128)(2,1)S(1)}, bf16[320,960]{1,0:T(8,128)(2,1)}, u32[]{:S(2)}) copy-start(bf16[320,960]{1,0:T(8,128)(2,1)} %dn.1) | copy-start | bytes 1843204
  378.8 6.7 %copy-start.24 = (bf16[320,960]{1,0:T(8,128)(2,1)S(1)}, bf16[320,960]{1,0:T(8,128)(2,1)}, u32[]{:S(2)}) copy-start(bf16[320,960]{1,0:T(8,128)(2,1)} %param.34) | copy-start | bytes 1843204
  378.8 6.7 %copy-start.25 = (bf16[320,960]{1,0:T(8,128)(2,1)S(1)}, bf16[320,960]{1,0:T(8,128)(2,1)}, u32[]{:S(2)}) copy-start(bf16[320,960]{1,0:T(8,128)(2,1)} %param.40) | copy-start | bytes 1843204
  378.8 6.7 %copy-start.26 = (bf16[320,960]{1,0:T(8,128)(2,1)S(1)}, bf16[320,960]{1,0:T(8,128)(2,1)}, u32[]{:S(2)}) copy-start(bf16[320,960]{1,0:T(8,128)(2,1)} %get-tuple-element.73) | copy-start | bytes 1843204
  (31 other events, 63.9 us)

commit v2 on v1

v2 whole, which is shorter than its diff:
```python
import functools

import jax
import jax.numpy as jnp
from jax import lax
from jax.experimental import pallas as pl
from jax.experimental.pallas import tpu as pltpu
from jax.sharding import PartitionSpec as P

QUERY_HEADS = 15
KEY_VALUE_HEADS = 5
GROUP = QUERY_HEADS // KEY_VALUE_HEADS
HEAD_WIDTH = 64
HALF = HEAD_WIDTH // 2
STEP = 10
TOK = 256
D = 960
KW = 320
FF = 2560
FH = FF // 2
ROWS = 120
PAD = 128
BF = jnp.bfloat16
F32 = jnp.float32
MESH = pl.DeviceIdType.MESH

norm_epsilon = 1e-05
rotary_base = 100000.0
beta_first = 0.9
beta_second = 0.95
adam_epsilon = 1e-08
matrix_rate = 0.06
matrix_decay = 0.1
gain_rate = 0.6
score_scale = HEAD_WIDTH ** (-0.5)

ANY = pl.BlockSpec(memory_space=pl.ANY)
VM = pl.BlockSpec(memory_space=pltpu.VMEM)


def place():
    f = lax.axis_index("fsdp")
    q = lax.axis_index("ctx")
    z = lax.axis_index("rep")
    return (q // 2) * 2 + f // 4, f % 4, z, q % 2


def at(x, y, z, core):
    x, y, z = lax.rem(x, 4), lax.rem(y, 4), lax.rem(z, 4)
    return {"rep": z, "fsdp": lax.rem(x, 2) * 4 + y, "ctx": (x // 2) * 2 + core}


def greet(devices):
    barrier = pltpu.get_barrier_semaphore()
    for device in devices:
        pl.semaphore_signal(barrier, inc=1, device_id=device, device_id_type=MESH)
    pl.semaphore_wait(barrier, len(devices))


def remote(src, dst, send, recv, device):
    return pltpu.make_async_remote_copy(
        src_ref=src, dst_ref=dst, send_sem=send, recv_sem=recv, device_id=device, device_id_type=MESH
    )


def params(number, vmem=56):
    return pltpu.CompilerParams(
        collective_id=number, has_side_effects=True, vmem_limit_bytes=vmem * 2**20
    )


ORDER = (1, 3, 2)
SIDE = (1, 3, 3, 1)


def gather_kernel(
    qo, kv, gain, dy, qo_all, kv_all, gain_all, dy_all, send_y, send_x, send_s, recv, recv_s, local
):
    x, y, z, c = place()
    xl = lax.rem(x, 2)
    f = 4 * xl + y
    sibling = at(x, y, z, 1 - c)
    greet([at(x, y + j, z, c) for j in (1, 2, 3)] + [at(x + j, y, z, c) for j in (1, 3)] + [sibling])
    own = (qo.at[c], kv.at[c], gain)

    def slot(item, g, core):
        if item == 2:
            return gain_all.at[g]
        return (qo_all, kv_all)[item].at[core, g]

    def wait_slot(item, g):
        ref = slot(item, g, c)
        remote(ref, ref, send_s.at[0, 0], recv.at[item, g], sibling).wait_recv()

    def send_row(item, j):
        return remote(own[item], slot(item, f, c), send_y.at[item, j - 1], recv.at[item, f], at(x, y + j, z, c))

    def send_side(item, j):
        g = 4 * xl + lax.rem(y + j, 4)
        return remote(
            own[item] if j == 0 else slot(item, g, c),
            slot(item, g, c),
            send_x.at[item, j],
            recv.at[item, g],
            at(x + SIDE[j], y, z, c),
        )

    def column(k):
        return 4 * xl + lax.rem(y + k + 1, 4) if k < 3 else 4 * (1 - xl) + lax.rem(y + k - 3, 4)

    def send_sib(item, k):
        ref = slot(item, column(k), c)
        return remote(ref, ref, send_s.at[item, k], recv_s.at[item, column(k)], sibling)

    items = (2, 0, 1)
    for item in items:
        send_side(item, 0).start()
        for j in ORDER:
            send_row(item, j).start()
    exchange = remote(dy, dy_all.at[1], send_s.at[2, 0], recv_s.at[2, 0], sibling)
    exchange.start()
    copies = [
        pltpu.make_async_copy(qo, qo_all.at[:, f], local.at[0]),
        pltpu.make_async_copy(kv, kv_all.at[:, f], local.at[1]),
        pltpu.make_async_copy(gain, gain_all.at[f], local.at[2]),
        pltpu.make_async_copy(dy, dy_all.at[0], local.at[3]),
    ]
    for copy in copies:
        copy.start()
    for item in items:
        for j in (1, 3):
            wait_slot(item, 4 * xl + lax.rem(y + j, 4))
            send_side(item, j).start()
            if item < 2:
                send_sib(item, j - 1).start()
    for item in (0, 1):
        wait_slot(item, column(3))
        send_sib(item, 3).start()
    for item in items:
        wait_slot(item, column(1))
        send_side(item, 2).start()
        if item < 2:
            send_sib(item, 1).start()
    for k in (4, 6, 5):
        for item in (0, 1):
            wait_slot(item, column(k))
            send_sib(item, k).start()
    for k in (3, 4, 6, 5):
        wait_slot(2, column(k))
    for copy in copies:
        copy.wait()
    exchange.wait()
    for item in (0, 1):
        for k in range(7):
            ref = slot(item, column(k), 1 - c)
            remote(ref, ref, send_s.at[0, 0], recv_s.at[item, column(k)], sibling).wait_recv()
            send_sib(item, k).wait_send()
    for item in items:
        for j in ORDER:
            send_row(item, j).wait_send()
        for j in range(4):
            send_side(item, j).wait_send()


def gather_weights(qo, kv, gain, dy):
    sem = pltpu.SemaphoreType.DMA
    return pl.pallas_call(
        gather_kernel,
        name="gather_weights",
        out_shape=(
            jax.ShapeDtypeStruct((2, 8, ROWS, D), BF),
            jax.ShapeDtypeStruct((2, 8, ROWS, KW), BF),
            jax.ShapeDtypeStruct((8, 8, 128), F32),
            jax.ShapeDtypeStruct((2, D, TOK), BF),
        ),
        in_specs=[ANY] * 4,
        out_specs=(ANY,) * 4,
        scratch_shapes=[sem((3, 3)), sem((3, 4)), sem((3, 7)), sem((3, 8)), sem((3, 8)), sem((4,))],
        compiler_params=params(0),
    )(qo, kv, gain, dy)


def swap_kernel(count, *refs):
    ins, outs = refs[:count], refs[count : 2 * count]
    send, recv = refs[2 * count :]
    x, y, z, c = place()
    sibling = at(x, y, z, 1 - c)
    greet([sibling])
    copies = [
        remote(ins[i], outs[i], send.at[i], recv.at[i], sibling) for i in range(count)
    ]
    for copy in copies:
        copy.start()
    for copy in copies:
        copy.wait()


def swap(number, *arrays):
    count = len(arrays)
    return pl.pallas_call(
        functools.partial(swap_kernel, count),
        name="swap_%d" % number,
        out_shape=tuple(jax.ShapeDtypeStruct(a.shape, a.dtype) for a in arrays),
        in_specs=[ANY] * count,
        out_specs=(ANY,) * count,
        scratch_shapes=[pltpu.SemaphoreType.DMA((count,)), pltpu.SemaphoreType.DMA((count,))],
        compiler_params=params(number),
    )(*arrays)


def dot(a, b, ca, cb):
    return lax.dot_general(a, b, (((ca,), (cb,)), ((), ())), preferred_element_type=F32)


def forward_kernel(
    stream, wq, wk, wv, wo, gains, cos, sin, gu, dn,
    q_low, att, lse, kv_out, one, mid, two_all, gu_all, dn_all,
    keys, wide, two, send, recv, send_y, send_x, recv_w, local,
):
    x, y, z, c = place()
    xl = lax.rem(x, 2)
    f = 4 * xl + y
    holds = c == xl
    me = 2 * (x // 2) + c
    sib_slot, far_slot, diag_slot = me + 1 - 2 * c, lax.rem(me + 2, 4), lax.rem(me + 2, 4) + 1 - 2 * c
    sibling, far = at(x, y, z, 1 - c), at(x + 2, y, z, c)
    greet([at(x, y + j, z, c) for j in (1, 2, 3)] + [at(x + j, y, z, c) for j in (1, 2, 3)] + [sibling])

    lanes = pl.ds(pl.multiple_of(c * FH, 128), FH)
    own = (gu.at[0, :, lanes], gu.at[1, :, lanes], dn.at[0:160], dn.at[160:320])

    def slot(item, g):
        if item < 2:
            return gu_all.at[item, g]
        return dn_all.at[lax.rem(g, 4), 160 * (item - 2) : 160 * (item - 1)]

    def wait_slot(item, g):
        remote(slot(item, g), slot(item, g), send_x.at[0, 0], recv_w.at[item, g], sibling).wait_recv()

    def send_row(item, j):
        return remote(own[item], slot(item, f), send_y.at[item, j - 1], recv_w.at[item, f], at(x, y + j, z, c))

    def send_side(item, j):
        g = 4 * xl + lax.rem(y + j, 4)
        return remote(
            own[item] if j == 0 else slot(item, g),
            slot(item, g),
            send_x.at[item, j],
            recv_w.at[item, g],
            at(x + (1, 3, 1, 3)[item], y, z, c),
        )

    def pass_on(items, offsets):
        for item in items:
            for j in offsets:
                wait_slot(item, 4 * xl + lax.rem(y + j, 4))
                send_side(item, j).start()

    def pass_down(offsets):
        pl.when(holds)(lambda: pass_on((2, 3), offsets))

    for j in ORDER:
        for item in (0, 1):
            send_row(item, j).start()

        @pl.when(holds)
        def _():
            for item in (2, 3):
                send_row(item, j).start()

    own_copies = [pltpu.make_async_copy(gu.at[:, :, lanes], gu_all.at[:, f], local.at[0])]
    own_copies[0].start()
    own_down = pltpu.make_async_copy(dn, dn_all.at[y], local.at[1])
    pl.when(holds)(own_down.start)

    co, si = cos[...], sin[...]
    scale = lax.rsqrt(jnp.sum(stream[...].astype(F32) ** 2, axis=0, keepdims=True) / D + norm_epsilon)
    one[...] = (stream[...].astype(F32) * scale * gains[0]).astype(BF)
    wide[:KW, :] = dot(wk[...], one[...], 0, 0)
    wide[KW : 2 * KW, :] = dot(wv[...], one[...], 0, 0)
    for h in range(KEY_VALUE_HEADS):
        a, b = wide[64 * h : 64 * h + 32, :], wide[64 * h + 32 : 64 * h + 64, :]
        keys[me, 64 * h : 64 * h + 32, :] = (a * co - b * si).astype(BF)
        keys[me, 64 * h + 32 : 64 * h + 64, :] = (b * co + a * si).astype(BF)
    keys[me, KW:, :] = wide[KW : 2 * KW, :].astype(BF)
    to_far = remote(keys.at[me], keys.at[me], send.at[0], recv.at[0], far)
    to_sib = remote(keys.at[me], keys.at[me], send.at[1], recv.at[1], sibling)
    to_far.start()
    to_sib.start()
    for item in (0, 1):
        send_side(item, 0).start()

    @pl.when(holds)
    def _():
        for item in (2, 3):
            send_side(item, 0).start()

    for start in range(0, D, 256):
        stop = min(start + 256, D)
        wide[start:stop, :] = dot(wq[:, start:stop], one[...], 0, 0)
    for h in range(QUERY_HEADS):
        a, b = wide[64 * h : 64 * h + 32, :], wide[64 * h + 32 : 64 * h + 64, :]
        q_low[64 * h : 64 * h + 32, :] = ((a * co - b * si).astype(BF) * score_scale).astype(BF)
        q_low[64 * h + 32 : 64 * h + 64, :] = ((b * co + a * si).astype(BF) * score_scale).astype(BF)
    pass_on((0,), (1, 3))
    remote(keys.at[far_slot], keys.at[far_slot], send.at[0], recv.at[0], far).wait_recv()
    on = remote(keys.at[far_slot], keys.at[far_slot], send.at[2], recv.at[2], sibling)
    on.start()
    remote(keys.at[sib_slot], keys.at[sib_slot], send.at[1], recv.at[1], sibling).wait_recv()
    remote(keys.at[diag_slot], keys.at[diag_slot], send.at[2], recv.at[2], sibling).wait_recv()
    gap = lax.broadcasted_iota(jnp.int32, (TOK, TOK), 0) - lax.broadcasted_iota(jnp.int32, (TOK, TOK), 1)

    def head(h, carry):
        rows = pl.ds(pl.multiple_of(h * 64, 64), 64)
        g = h // GROUP
        krows = pl.ds(pl.multiple_of(g * 64, 64), 64)
        vrows = pl.ds(pl.multiple_of(KW + g * 64, 64), 64)
        qh = q_low[rows, :]
        s = []
        for j in range(4):
            part = dot(keys[j, krows, :], qh, 0, 0)
            s.append(jnp.where(gap <= 256 * (me - j), part, -1e30))
        top = jnp.max(jnp.maximum(jnp.maximum(s[0], s[1]), jnp.maximum(s[2], s[3])), axis=0, keepdims=True)
        e = [jnp.exp(part - top) for part in s]
        total = jnp.sum(e[0] + e[1] + (e[2] + e[3]), axis=0, keepdims=True)
        acc = dot(keys[0, vrows, :], e[0].astype(BF), 1, 0)
        for j in range(1, 4):
            acc += dot(keys[j, vrows, :], e[j].astype(BF), 1, 0)
        att[rows, :] = (acc / total).astype(BF)
        lse[pl.ds(h, 1), 0, :] = top + jnp.log(total)
        pl.when(h == 1)(lambda: pass_on((1,), (1, 3)))
        pl.when(h == 5)(lambda: pass_down((1, 3)))
        pl.when(h == 9)(lambda: pass_on((0,), (2,)))
        pl.when(h == 13)(lambda: pass_on((1,), (2,)))
        return carry

    lax.fori_loop(0, QUERY_HEADS, head, 0)
    kv_out[...] = keys[...]

    square = jnp.zeros((1, TOK), F32)
    for start in range(0, D, 256):
        stop = min(start + 256, D)
        part = stream[start:stop, :].astype(F32) + dot(wo[:, start:stop], att[...], 0, 0)
        mid[start:stop, :] = part
        square += jnp.sum(part * part, axis=0, keepdims=True)
    scale = lax.rsqrt(square / D + norm_epsilon)
    two[...] = (mid[...] * scale * gains[1]).astype(BF)
    keep = pltpu.make_async_copy(two, two_all.at[0], local.at[2])
    keep.start()
    trade = remote(two, two_all.at[1], send.at[3], recv.at[3], sibling)
    trade.start()
    pass_down((2,))

    for k in range(4):
        g = 4 * (1 - xl) + lax.rem(y + k, 4)
        for item in (0, 1):
            wait_slot(item, g)

        @pl.when(jnp.logical_not(holds))
        def _():
            for item in (2, 3):
                wait_slot(item, g)

    own_copies[0].wait()
    keep.wait()
    trade.wait()
    to_far.wait_send()
    to_sib.wait_send()
    on.wait_send()

    def sent(items):
        for item in items:
            for j in ORDER:
                send_row(item, j).wait_send()
            for j in range(4):
                send_side(item, j).wait_send()

    sent((0, 1))

    @pl.when(holds)
    def _():
        own_down.wait()
        sent((2, 3))


def forward(stream, wq, wk, wv, wo, gains, cos, sin, gu, dn):
    sem = pltpu.SemaphoreType.DMA
    return pl.pallas_call(
        forward_kernel,
        name="forward",
        out_shape=(
            jax.ShapeDtypeStruct((D, TOK), BF),
            jax.ShapeDtypeStruct((D, TOK), BF),
            jax.ShapeDtypeStruct((16, 1, TOK), F32),
            jax.ShapeDtypeStruct((4, 2 * KW, TOK), BF),
            jax.ShapeDtypeStruct((D, TOK), BF),
            jax.ShapeDtypeStruct((D, TOK), F32),
            jax.ShapeDtypeStruct((2, D, TOK), BF),
            jax.ShapeDtypeStruct((2, 8, ROWS, FH), BF),
            jax.ShapeDtypeStruct((4, KW, D), BF),
        ),
        in_specs=[VM] * 8 + [ANY] * 2,
        out_specs=(VM,) * 6 + (ANY,) * 3,
        scratch_shapes=[
            pltpu.VMEM((4, 2 * KW, TOK), BF),
            pltpu.VMEM((D, TOK), F32),
            pltpu.VMEM((D, TOK), BF),
            sem((4,)),
            sem((4,)),
            sem((4, 3)),
            sem((4, 4)),
            sem((4, 8)),
            sem((3,)),
        ],
        compiler_params=params(1),
    )(stream, wq, wk, wv, wo, gains, cos, sin, gu, dn)


def summed(own, got, count=3):
    total = own.astype(F32)
    for i in range(count):
        total += got[i].astype(F32)
    return total.astype(BF)


def ring(x, y, z, c):
    along_x = [at(x + j, y, z, c) for j in (1, 2, 3)]
    along_y = [at(x, y + j, z, c) for j in (1, 2, 3)]
    along_z = [at(x, y, z + j, c) for j in (1, 2, 3)]
    return along_x, along_y, along_z


def quarter(index, size):
    return pl.ds(pl.multiple_of(lax.rem(index, 4) * size, 16), size)


def planes(value, extra):
    return [
        jnp.concatenate([value[ROWS * f : ROWS * (f + 1)], extra[f]], axis=0).astype(BF)
        for f in range(8)
    ]


def columns(total):
    return [(start, min(start + 256, total)) for start in range(0, total, 256)]


def backward_kernel(
    q_low, keys, lse, att, grad, cos, sin, two, gate_grad, up_grad, hidden, dy,
    q_back, kv_back, c0_out, c1_out, d_out,
    mine, got, far_got, acc, c0, c0r, c1, c1r, c1s, c1t, d, dr, ds_, dt,
    send, recv, send_z, recv_z, send_x, recv_x, send_t, recv_t, send_y, recv_y, send_d, recv_d,
):
    x, y, z, c = place()
    xl = lax.rem(x, 2)
    holds = c == xl
    me = 2 * (x // 2) + c
    far_slot = lax.rem(me + 2, 4)
    sib_slot = me + 1 - 2 * c
    diag_slot = far_slot + 1 - 2 * c
    sibling, far = at(x, y, z, 1 - c), at(x + 2, y, z, c)
    along_x, along_y, along_z = ring(x, y, z, c)
    greet(along_x + along_y + along_z + [sibling])
    co, si = cos[...], sin[...]
    nothing = [jnp.zeros((8, 256), F32)] * 8

    def c0_z(j):
        return remote(c0.at[:, :, quarter(z + j, 32)], c0r.at[j - 1], send_z.at[j - 1], recv_z.at[j - 1], along_z[j - 1])

    def c1_x(i):
        return remote(
            c1.at[1 - xl, :, :, 640 * i : 640 * (i + 1)], c1r.at[i], send_x.at[i], recv_x.at[i], along_x[2 * i]
        )

    def c1_z(j):
        return remote(c1s.at[:, quarter(z + j, 32)], c1t.at[j - 1], send_t.at[j - 1], recv_t.at[j - 1], along_z[j - 1])

    def d_y(j):
        return remote(d.at[lax.rem(y + j, 4)], dr.at[j - 1], send_y.at[j - 1], recv_y.at[j - 1], along_y[j - 1])

    def d_x(j):
        return remote(ds_, dt.at[j - 1], send_d.at[j - 1], recv_d.at[j - 1], along_x[j - 1])

    for start, stop in columns(FH):
        part = planes(dot(two[...], gate_grad[start:stop, :], 1, 1), nothing)
        for f in range(8):
            c0[f // 4, f % 4, :, start:stop] = part[f]
    for j in ORDER:
        c0_z(j).start()
    for start, stop in columns(D):
        part = dot(hidden[...], dy[start:stop, :], 1, 1).astype(BF)
        for k in range(4):
            d[k, :, start:stop] = part[KW * k : KW * (k + 1)]
    for j in ORDER:
        d_y(j).start()
    for start, stop in columns(FH):
        part = planes(dot(two[...], up_grad[start:stop, :], 1, 1), nothing)
        for f in range(8):
            c1[f // 4, f % 4, :, start:stop] = part[f]
    for i in (0, 1):
        c1_x(i).start()

    def step_c1():
        for i in (0, 1):
            c1_x(i).wait_recv()
        for k in range(4):
            for i in (0, 1):
                lanes = slice(640 * i, 640 * (i + 1))
                c1s[k, :, lanes] = (c1[xl, k, :, lanes].astype(F32) + c1r[i, k].astype(F32)).astype(BF)
        for j in ORDER:
            c1_z(j).start()

    def step_d():
        for j in (1, 2, 3):
            d_y(j).wait_recv()
        ds_[...] = summed(d[y], dr)
        pl.when(holds)(lambda: d_x(2).start())

        @pl.when(jnp.logical_not(holds))
        def _():
            d_x(1).start()
            d_x(3).start()

    gap = lax.broadcasted_iota(jnp.int32, (TOK, TOK), 0) - lax.broadcasted_iota(jnp.int32, (TOK, TOK), 1)

    def group(g, carry):
        krows = pl.ds(pl.multiple_of(g * 64, 64), 64)
        vrows = pl.ds(pl.multiple_of(KW + g * 64, 64), 64)

        def head(t, inner):
            h = g * GROUP + t
            rows = pl.ds(pl.multiple_of(h * 64, 64), 64)
            qh, gh = q_low[rows, :], grad[rows, :]
            row_dot = jnp.sum(gh.astype(F32) * att[rows, :].astype(F32), axis=0, keepdims=True)
            level = lse[pl.ds(h, 1), 0, :]
            dq = jnp.zeros((64, TOK), F32)
            for j in range(4):
                s = dot(keys[j, krows, :], qh, 0, 0)
                s = jnp.where(gap <= 256 * (me - j), s, -1e30)
                p = jnp.exp(s - level)
                dp = dot(keys[j, vrows, :], gh, 0, 0)
                ds = (p * (dp - row_dot)).astype(BF)
                pb = p.astype(BF)
                dq += dot(keys[j, krows, :], ds, 1, 0)
                dk = dot(qh, ds, 1, 1)
                dv = dot(gh, pb, 1, 1)
                first = t == 0
                acc[j, 0] = jnp.where(first, dk, acc[j, 0] + dk)
                acc[j, 1] = jnp.where(first, dv, acc[j, 1] + dv)
            dq = dq * score_scale
            a, b = dq[:32], dq[32:]
            q_back[pl.ds(pl.multiple_of(h * 64, 32), 32), :] = (a * co + b * si).astype(BF)
            q_back[pl.ds(pl.multiple_of(h * 64 + 32, 32), 32), :] = (b * co - a * si).astype(BF)
            return inner

        lax.fori_loop(0, GROUP, head, 0)
        for j in range(4):
            mine[j, krows, :] = acc[j, 0].astype(BF)
            mine[j, vrows, :] = acc[j, 1].astype(BF)
        pl.when(g == 1)(step_c1)
        pl.when(g == 3)(step_d)
        return carry

    acc[...] = jnp.zeros_like(acc)
    lax.fori_loop(0, KEY_VALUE_HEADS, group, 0)
    to_sib_far = remote(mine.at[diag_slot], got.at[1], send.at[0], recv.at[0], sibling)
    to_sib = remote(mine.at[sib_slot], got.at[0], send.at[1], recv.at[1], sibling)
    to_sib_far.start()
    to_sib.start()
    to_sib_far.wait_recv()
    got[1] = (mine[far_slot].astype(F32) + got[1].astype(F32)).astype(BF)
    to_far = remote(got.at[1], far_got, send.at[2], recv.at[2], far)
    to_far.start()
    to_sib.wait_recv()

    @pl.when(holds)
    def _():
        for j in (1, 2, 3):
            d_x(j).wait_recv()
        d_out[...] = summed(ds_[...], dt)

    @pl.when(jnp.logical_not(holds))
    def _():
        d_out[...] = jnp.zeros_like(d_out)

    near = mine[me].astype(F32) + got[0].astype(F32)
    to_far.wait_recv()
    total = near + far_got[...].astype(F32)
    for h in range(KEY_VALUE_HEADS):
        a, b = total[64 * h : 64 * h + 32, :], total[64 * h + 32 : 64 * h + 64, :]
        kv_back[64 * h : 64 * h + 32, :] = (a * co + b * si).astype(BF)
        kv_back[64 * h + 32 : 64 * h + 64, :] = (b * co - a * si).astype(BF)
    kv_back[KW:, :] = total[KW:, :].astype(BF)
    for j in (1, 2, 3):
        c0_z(j).wait_recv()
    for i in (0, 1):
        for k in range(4):
            c0_out[i, k] = summed(c0[i, k, quarter(z, 32)], [c0r[j, i, k] for j in range(3)])
    for j in (1, 2, 3):
        c1_z(j).wait_recv()
    for k in range(4):
        c1_out[k] = summed(c1s[k, quarter(z, 32)], [c1t[j, k] for j in range(3)])

    to_sib_far.wait_send()
    to_sib.wait_send()
    to_far.wait_send()
    for j in (1, 2, 3):
        c0_z(j).wait_send()
        c1_z(j).wait_send()
        d_y(j).wait_send()
    for i in (0, 1):
        c1_x(i).wait_send()
    pl.when(holds)(lambda: d_x(2).wait_send())

    @pl.when(jnp.logical_not(holds))
    def _():
        d_x(1).wait_send()
        d_x(3).wait_send()


def backward(*args):
    sem = pltpu.SemaphoreType.DMA
    vm = lambda *shape: pltpu.VMEM(shape, BF)
    return pl.pallas_call(
        backward_kernel,
        name="backward",
        out_shape=(
            jax.ShapeDtypeStruct((D, TOK), BF),
            jax.ShapeDtypeStruct((2 * KW, TOK), BF),
            jax.ShapeDtypeStruct((2, 4, 32, FH), BF),
            jax.ShapeDtypeStruct((4, 32, FH), BF),
            jax.ShapeDtypeStruct((KW, D), BF),
        ),
        in_specs=[VM] * 12,
        out_specs=(VM,) * 5,
        scratch_shapes=[
            vm(4, 2 * KW, TOK), vm(2, 2 * KW, TOK), vm(2 * KW, TOK), pltpu.VMEM((4, 2, 64, TOK), F32),
            vm(2, 4, PAD, FH), vm(3, 2, 4, 32, FH),
            vm(2, 4, PAD, FH), vm(2, 4, PAD, 640), vm(4, PAD, FH), vm(3, 4, 32, FH),
            vm(4, KW, D), vm(3, KW, D), vm(KW, D), vm(3, KW, D),
        ]
        + [sem((3,))] * 4
        + [sem((2,))] * 2
        + [sem((3,))] * 6,
        compiler_params=params(2),
    )(*args)


WIDE, NARROW = 512, D - 512


def finish_kernel(
    one, att, mid, q_back, kv_back, gain, c0, c1, dd,
    lo_sum, hi_sum, kv_sum, c0_sum, c1_sum, d_sum,
    left, right, thin, both, lo, hi, kv,
    lo1, lo1r, lo2, lo2r, lo3, lo3r,
    kv1, kv1r, kv2, kv2r, kv3, kv3r,
    hi1, hi1r, hi2, hi2r, hi3, hi3r,
    c02r, c02, c03r, c03,
    c1r, c1s, c1t, c1u,
    dr, ds_,
    send, recv, send_s, recv_s, send_g, recv_g, send_o, recv_o, local,
):
    x, y, z, c = place()
    xl = lax.rem(x, 2)
    holds = c == xl
    sibling = at(x, y, z, 1 - c)
    along_x, along_y, along_z = ring(x, y, z, c)
    greet(along_x + along_y + along_z + [sibling])
    LO, HI, KV, C0, C1, DN = range(6)

    def trade(i, src, dst):
        return remote(src, dst, send_s.at[i], recv_s.at[i], sibling)

    far = slice(TOK, 2 * TOK)

    def trades(core):
        return [
            trade(0, att if core == 0 else one, left.at[:, far]),
            trade(1, mid if core == 0 else q_back, right.at[:, far]),
            trade(2, kv_back.at[KW:] if core == 0 else kv_back.at[:KW], thin.at[:, far]),
            trade(3, one, both.at[:, far]),
        ]

    def move(item, phase, j, src, dst, along):
        return remote(src, dst.at[j - 1], send.at[item, phase, j - 1], recv.at[item, phase, j - 1], along[j - 1])

    def y1(item, j):
        src, dst = {LO: (lo, lo1r), KV: (kv, kv1r)}[item]
        return move(item, 0, j, src.at[:, lax.rem(y + j, 4)], dst, along_y)

    def x2(item, j):
        src, dst = {LO: (lo1, lo2r), KV: (kv1, kv2r)}[item]
        return move(item, 1, j, src.at[xl if j == 2 else 1 - xl], dst, along_x)

    def z3(item, j):
        if item == DN:
            return move(item, 2, j, dd.at[quarter(z + j, 80)], dr, along_z)
        src, dst = {LO: (lo2, lo3r), KV: (kv2, kv3r)}[item]
        return move(item, 2, j, src.at[quarter(z + j, 32)], dst, along_z)

    def z1(j):
        return move(HI, 0, j, hi.at[:, :, quarter(z + j, 32)], hi1r, along_z)

    def y2(item, j):
        src, dst = {HI: (hi1, hi2r), C0: (c0, c02r)}[item]
        return move(item, 1, j, src.at[:, lax.rem(y + j, 4)], dst, along_y)

    def x3(item, j):
        src, dst = {HI: (hi2, hi3r), C0: (c02, c03r)}[item]
        return move(item, 2, j, src.at[xl if j == 2 else 1 - xl], dst, along_x)

    def y_up(j):
        return move(C1, 0, j, c1.at[lax.rem(y + j, 4)], c1r, along_y)

    def x_up():
        return remote(c1s, c1t, send.at[C1, 1, 0], recv.at[C1, 1, 0], along_x[1])

    for core in (0, 1):

        @pl.when(c == core)
        def _(core=core):
            for copy in trades(core):
                copy.start()

    for j in ORDER:
        y2(C0, j).start()
        y_up(j).start()

    @pl.when(holds)
    def _():
        for j in ORDER:
            z3(DN, j).start()

    near = slice(0, TOK)

    @pl.when(c == 0)
    def _():
        left[:, near] = one[...]
        right[:, near] = q_back[...]
        thin[:, near] = kv_back[:KW, :]

    @pl.when(c == 1)
    def _():
        left[:, near] = att[...]
        right[:, near] = mid[...]
        thin[:, near] = kv_back[KW:, :]

    both[:, near] = one[...]
    trade(3, one, both.at[:, far]).wait_recv()
    trade(2, kv_back.at[:KW], thin.at[:, far]).wait_recv()
    nothing = [jnp.zeros((8, KW), F32)] * 8
    part = planes(dot(both[...], thin[...], 1, 1), nothing)
    for f in range(8):
        kv[f // 4, f % 4] = part[f]
    for j in ORDER:
        y1(KV, j).start()
    trade(0, one, left.at[:, far]).wait_recv()
    trade(1, one, right.at[:, far]).wait_recv()
    for start, stop in ((256, 512), (0, 256), (512, 768), (768, D)):
        size = stop - start
        extra = [gain[f] if start == 0 else jnp.zeros((8, size), F32) for f in range(8)]
        part = planes(dot(left[...], right[start:stop, :], 1, 1), extra)
        for f in range(8):
            if start < WIDE:
                lo[f // 4, f % 4, :, start:stop] = part[f]
            else:
                hi[f // 4, f % 4, :, start - WIDE : stop - WIDE] = part[f]
        if start == 0:
            for j in ORDER:
                y1(LO, j).start()
    for j in ORDER:
        z1(j).start()

    def arrived(make, *key):
        for j in (1, 2, 3):
            make(*key, j).wait_recv()

    arrived(y2, C0)
    for i in range(2):
        c02[i] = summed(c0[i, y], [c02r[j, i] for j in range(3)])
    for j in ORDER:
        x3(C0, j).start()
    arrived(y_up)
    c1s[...] = summed(c1[y], c1r)
    x_up().start()

    part_of = {LO: lo3, HI: hi3, KV: kv3, C0: c03, C1: c1u, DN: ds_}

    def place_of(item, index, core):
        if item == DN:
            return d_sum.at[quarter(index, 80)]
        if item in (C0, C1):
            lanes = pl.ds(pl.multiple_of(FH * core, 128), FH)
            return (c0_sum if item == C0 else c1_sum).at[quarter(index, 32), lanes]
        return {LO: lo_sum, HI: hi_sum, KV: kv_sum}[item].at[core, quarter(index, 32)]

    def spread(item, j):
        return remote(
            part_of[item], place_of(item, z, c), send_g.at[item, j - 1], recv_g.at[item, j - 1], along_z[j - 1]
        )

    def keep(item):
        return pltpu.make_async_copy(part_of[item], place_of(item, z, c), local.at[item])

    def across(item, k):
        index = lax.rem(z + 4 - k, 4)
        src = part_of[item] if k == 0 else place_of(item, index, c)
        return remote(src, place_of(item, index, c), send_o.at[item, k], recv_o.at[item, k], sibling)

    def publish(item):
        keep(item).start()
        for j in ORDER:
            spread(item, j).start()
        across(item, 0).start()

    def landed(item, j):
        ref = place_of(item, lax.rem(z + 4 - j, 4), c)
        remote(ref, ref, send_g.at[item, j - 1], recv_g.at[item, j - 1], sibling).wait_recv()

    def collect(item):
        for j in ORDER:
            landed(item, j)
            across(item, j).start()

    def arrive(item):
        for k in range(4):
            ref = place_of(item, lax.rem(z + 4 - k, 4), 1 - c)
            remote(ref, ref, send_o.at[item, k], recv_o.at[item, k], sibling).wait_recv()

    @pl.when(holds)
    def _():
        arrived(z3, DN)
        ds_[...] = summed(dd[quarter(z, 80)], dr)
        publish(DN)

    x_up().wait_recv()
    c1u[...] = (c1s[...].astype(F32) + c1t[...].astype(F32)).astype(BF)
    publish(C1)
    arrived(x3, C0)
    c03[...] = summed(c02[xl], c03r)
    publish(C0)

    arrived(y1, KV)
    for i in range(2):
        kv1[i] = summed(kv[i, y], [kv1r[j, i] for j in range(3)])
    for j in ORDER:
        x2(KV, j).start()
    arrived(y1, LO)
    for i in range(2):
        lo1[i] = summed(lo[i, y], [lo1r[j, i] for j in range(3)])
    for j in ORDER:
        x2(LO, j).start()
    arrived(z1)
    for i in range(2):
        for k in range(4):
            hi1[i, k] = summed(hi[i, k, quarter(z, 32)], [hi1r[j, i, k] for j in range(3)])
    for j in ORDER:
        y2(HI, j).start()
    arrived(x2, KV)
    kv2[...] = summed(kv1[xl], kv2r)
    for j in ORDER:
        z3(KV, j).start()
    arrived(x2, LO)
    lo2[...] = summed(lo1[xl], lo2r)
    for j in ORDER:
        z3(LO, j).start()
    arrived(y2, HI)
    for i in range(2):
        hi2[i] = summed(hi1[i, y], [hi2r[j, i] for j in range(3)])
    for j in ORDER:
        x3(HI, j).start()
    arrived(z3, KV)
    kv3[...] = summed(kv2[quarter(z, 32)], kv3r)
    publish(KV)
    arrived(z3, LO)
    lo3[...] = summed(lo2[quarter(z, 32)], lo3r)
    publish(LO)
    arrived(x3, HI)
    hi3[...] = summed(hi2[xl], hi3r)
    publish(HI)

    pl.when(holds)(lambda: collect(DN))
    for item in (C1, C0, KV, LO, HI):
        collect(item)
    pl.when(jnp.logical_not(holds))(lambda: arrive(DN))
    for item in (C1, C0, KV, LO, HI):
        arrive(item)

    for core in (0, 1):

        @pl.when(c == core)
        def _(core=core):
            for copy in trades(core):
                copy.wait_send()

    def settled(item):
        keep(item).wait()
        for j in (1, 2, 3):
            spread(item, j).wait_send()
        for k in range(4):
            across(item, k).wait_send()

    for j in (1, 2, 3):
        for make, key in (
            (y1, LO), (x2, LO), (z3, LO), (y1, KV), (x2, KV), (z3, KV), (y2, HI), (x3, HI), (y2, C0), (x3, C0),
        ):
            make(key, j).wait_send()
        z1(j).wait_send()
        y_up(j).wait_send()
    x_up().wait_send()
    for item in (LO, HI, KV, C0, C1):
        settled(item)

    @pl.when(holds)
    def _():
        for j in (1, 2, 3):
            z3(DN, j).wait_send()
        settled(DN)


def finish(*args):
    sem = pltpu.SemaphoreType.DMA
    vm = lambda *shape: pltpu.VMEM(shape, BF)

    def yxz(width):
        return [
            vm(2, PAD, width), vm(3, 2, PAD, width), vm(PAD, width), vm(3, PAD, width),
            vm(32, width), vm(3, 32, width),
        ]

    return pl.pallas_call(
        finish_kernel,
        name="finish",
        out_shape=(
            jax.ShapeDtypeStruct((2, PAD, WIDE), BF),
            jax.ShapeDtypeStruct((2, PAD, NARROW), BF),
            jax.ShapeDtypeStruct((2, PAD, KW), BF),
            jax.ShapeDtypeStruct((PAD, FF), BF),
            jax.ShapeDtypeStruct((PAD, FF), BF),
            jax.ShapeDtypeStruct((KW, D), BF),
        ),
        in_specs=[VM] * 9,
        out_specs=(ANY,) * 6,
        scratch_shapes=[
            vm(D, 2 * TOK), vm(D, 2 * TOK), vm(KW, 2 * TOK), vm(D, 2 * TOK),
            vm(2, 4, PAD, WIDE), vm(2, 4, PAD, NARROW), vm(2, 4, PAD, KW),
        ]
        + yxz(WIDE)
        + yxz(KW)
        + [
            vm(2, 4, 32, NARROW), vm(3, 2, 4, 32, NARROW), vm(2, 32, NARROW), vm(3, 2, 32, NARROW),
            vm(32, NARROW), vm(3, 32, NARROW),
        ]
        + [vm(3, 2, 32, FH), vm(2, 32, FH), vm(3, 32, FH), vm(32, FH)]
        + [vm(3, 32, FH), vm(32, FH), vm(32, FH), vm(32, FH)]
        + [vm(3, 80, D), vm(80, D)]
        + [sem((6, 3, 3)), sem((6, 3, 3)), sem((4,)), sem((4,)), sem((6, 3)), sem((6, 3)), sem((6, 4)), sem((6, 4)), sem((6,))],
        compiler_params=params(3),
    )(*args)


def norm_backward(stream, gain, incoming):
    scale = lax.rsqrt(jnp.mean(stream * stream, axis=0, keepdims=True) + norm_epsilon)
    normal = stream * scale
    gain_grad = jnp.sum(incoming * normal, axis=1)
    scaled = incoming * gain
    stream_grad = scale * (scaled - normal * jnp.mean(scaled * normal, axis=0, keepdims=True))
    return (stream_grad, gain_grad)


def adamw_update(weight, gradient, first, second, rate, decay):
    weight = weight.astype(F32)
    first_new = beta_first * first.astype(F32) + (1.0 - beta_first) * gradient
    second_new = beta_second * second.astype(F32) + (1.0 - beta_second) * gradient * gradient
    first_hat = first_new / (1.0 - beta_first**STEP)
    second_hat = second_new / (1.0 - beta_second**STEP)
    weight_new = weight - rate * (
        first_hat / (jnp.sqrt(second_hat) + adam_epsilon) + decay * weight
    )
    return (weight_new, first_new, second_new)


def body(
    tokens,
    cotangent,
    query_weight,
    keyval_weight,
    output_weight,
    gateup_weight,
    down_weight,
    norm_gains,
    query_first,
    keyval_first,
    output_first,
    gateup_first,
    down_first,
    gains_first,
    query_second,
    keyval_second,
    output_second,
    gateup_second,
    down_second,
    gains_second,
):
    ctx = lax.axis_index("ctx")
    core = lax.rem(ctx, 2)
    stream_t, dy_t = tokens[0].T, cotangent[0].T
    gain_tile = jnp.pad(norm_gains.astype(F32), ((0, 6), (0, 8)))
    qo_all, kv_all, gain_all, dy_all = gather_weights(
        jnp.stack([query_weight, output_weight]), keyval_weight, gain_tile, dy_t
    )
    gains = gain_all[:, :2, :ROWS].transpose(1, 0, 2).reshape(2, D, 1)
    query_full, output_full = qo_all[0].reshape(D, D), qo_all[1].reshape(D, D)
    key_full, value_full = kv_all[0].reshape(D, KW), kv_all[1].reshape(D, KW)

    positions = (ctx * TOK + jnp.arange(TOK, dtype=jnp.int32)).astype(F32)
    counter = jnp.arange(HALF, dtype=F32)
    frequency = 1.0 / rotary_base ** (counter * (2.0 / HEAD_WIDTH))
    angles = frequency[:, None] * positions[None, :]
    cosine, sine = jnp.cos(angles), jnp.sin(angles)

    query_low, attended_t, level, keys, one_t, middle_t, two_all, gu_all, dn_all = forward(
        stream_t, query_full, key_full, value_full, output_full, gains, cosine, sine, gateup_weight, down_weight
    )
    gate_full, up_full = gu_all[0].reshape(D, FH), gu_all[1].reshape(D, FH)
    down_full = dn_all.reshape(FH, D)
    both_dy = jnp.concatenate([dy_all[0], dy_all[1]], axis=1)
    both_two = jnp.concatenate([two_all[0], two_all[1]], axis=1)

    def dg(a, b, ca, cb):
        return lax.dot_general(a, b, (((ca,), (cb,)), ((), ())), preferred_element_type=F32)

    gate = dg(gate_full, both_two, 0, 0)
    upward = dg(up_full, both_two, 0, 0)
    sigmoid_gate = jax.nn.sigmoid(gate)
    hidden = (gate * sigmoid_gate * upward).astype(BF)
    down_part = dg(down_full, hidden, 0, 0)
    hidden_grad = dg(down_full, both_dy, 1, 0)
    gate_grad = (hidden_grad * upward * sigmoid_gate * (1.0 + gate * (1.0 - sigmoid_gate))).astype(BF)
    up_grad = (hidden_grad * gate * sigmoid_gate).astype(BF)
    two_part = dg(gate_full, gate_grad, 1, 0) + dg(up_full, up_grad, 1, 0)
    down_other, two_other = swap(5, down_part[:, TOK:], two_part[:, TOK:])
    result_t = (middle_t + down_part[:, :TOK] + down_other).astype(BF)
    two_grad = two_part[:, :TOK] + two_other
    incoming = dy_t.astype(F32)
    middle_norm_grad, gain_two_grad = norm_backward(middle_t, gains[1], two_grad)
    middle_grad = incoming + middle_norm_grad
    middle_low = middle_grad.astype(BF)
    attended_grad_t = dg(output_full, middle_low, 1, 0).astype(BF)
    query_back, keyval_back, gate_part, up_part, down_sum = backward(
        query_low, keys, level, attended_t, attended_grad_t, cosine, sine,
        both_two, gate_grad, up_grad, hidden, both_dy,
    )
    key_back, value_back = keyval_back[:KW], keyval_back[KW:]

    one_grad = dg(query_full, query_back, 1, 0) + dg(key_full, key_back, 1, 0) + dg(value_full, value_back, 1, 0)
    stream_norm_grad, gain_one_grad = norm_backward(stream_t.astype(F32), gains[0], one_grad)
    input_grad = middle_grad + stream_norm_grad
    grad_gains = jnp.stack([gain_one_grad, gain_two_grad]).reshape(2, 8, ROWS).transpose(1, 0, 2)
    gain_rows = jnp.pad(grad_gains, ((0, 0), (0, 6), (0, 256 - ROWS)))
    low, high, narrow, gate_sum, up_sum, down = finish(
        one_t, attended_t, middle_low, query_back, keyval_back, gain_rows, gate_part, up_part, down_sum
    )
    wide = jnp.concatenate([low, high], axis=2)
    gains_sum = low[0, ROWS : ROWS + 2, :ROWS].astype(F32) + low[1, ROWS : ROWS + 2, :ROWS].astype(F32)
    summed_rows = (
        wide[0, :ROWS].astype(F32),
        narrow[:, :ROWS].astype(F32),
        wide[1, :ROWS].astype(F32),
        jnp.stack([gate_sum[:ROWS], up_sum[:ROWS]]).astype(F32),
        down.astype(F32),
        gains_sum,
    )
    shards = (query_weight, keyval_weight, output_weight, gateup_weight, down_weight, norm_gains)
    firsts = (query_first, keyval_first, output_first, gateup_first, down_first, gains_first)
    seconds = (query_second, keyval_second, output_second, gateup_second, down_second, gains_second)
    rates = (matrix_rate,) * 5 + (gain_rate,)
    decays = (matrix_decay,) * 5 + (0.0,)
    updated = [
        adamw_update(shards[i], summed_rows[i], firsts[i], seconds[i], rates[i], decays[i])
        for i in range(6)
    ]
    return (
        result_t.T[None],
        input_grad.T[None],
        *[updated[i][0] for i in range(6)],
        *[updated[i][1] for i in range(6)],
        *[updated[i][2] for i in range(6)],
    )


def solution(mesh):
    row, mid = P("fsdp", None), P(None, "fsdp", None)
    weights = (row, mid, row, mid, row, P(None, "fsdp"))
    stream = P(("rep", "fsdp"), "ctx", None)
    return jax.shard_map(
        body,
        mesh=mesh,
        in_specs=(stream, stream) + weights * 3,
        out_specs=(stream, stream) + weights * 3,
        check_vma=False,
    )
```

time: 396 us -> 297 us (0.75); the launches traced: 392 us -> 297 us
  Pallas kernels: 265 us -> 228 us
  matrix products: 34.9 us -> 14.6 us
  blocking collectives: 14.8 us -> 0 us
  local copies, waits for them, and re-layouts: 42.9 us -> 29.5 us
  other arithmetic: 32 us -> 23.3 us
    pallas_call x1, Pallas kernels: 82 us -> 41.3 us  [gather_weights(): pl.pallas_call(gather_kernel, name='gather_weights', out_shape=(jax.Shape...]
    dot_general x19 -> x10, matrix products: 34.9 us -> 14.6 us  [dg(): lax.dot_general(a, b, (((ca,), (cb,)), ((), ())), preferred_element_type=...]
    all_gather x1 -> x0, blocking collectives: 14.8 us -> none  [body(): gains = lax.all_gather(norm_gains, 'fsdp', axis=1, tiled=True).astype(F32)]
    pallas_call x3, Pallas kernels: 172 us -> 182 us  [the longest x1 66.3 us: backward(): pl.pallas_call(backward_kernel, name='backward', out_shape=(jax.ShapeDtyp...]
    unnamed x122 -> x103, local copies, waits for them, and re-layouts: 18.4 us -> 10.3 us
    pallas_call x3 -> x1, Pallas kernels: 11.2 us -> 4.35 us  [swap(): pl.pallas_call(functools.partial(swap_kernel, count), name='swap_%d' % nu...]
    convert_element_type x4 -> x0, local copies, waits for them, and re-layouts: 4.86 us -> none  [the longest x1 3.61 us: body(): grad_down = matmul(hidden.T, both_dy).astype(BF)]
where the time goes in v2:
time: 297 us
  Pallas kernels  228 us (77%)
  local copies, waits for them, and re-layouts  29.5 us (10%)
  other arithmetic  23.3 us (8%)
  matrix products  14.6 us (5%)
    pallas_call x1, Pallas kernels, backward(): pl.pallas_call(backward_kernel, name='backward', out_shape=(jax.ShapeDtyp...  66.3 us
    pallas_call x1, Pallas kernels, forward(): pl.pallas_call(forward_kernel, name='forward', out_shape=(jax.ShapeDtypeS...  58.6 us
    pallas_call x1, Pallas kernels, finish(): pl.pallas_call(finish_kernel, name='finish', out_shape=(jax.ShapeDtypeStr...  57.6 us
    pallas_call x1, Pallas kernels, gather_weights(): pl.pallas_call(gather_kernel, name='gather_weights', out_shape=(jax.Shape...  41.3 us
    dot_general x10, matrix products, dg(): lax.dot_general(a, b, (((ca,), (cb,)), ((), ())), preferred_element_type=...  14.6 us
    sub x4, other arithmetic, adamw_update(): weight - rate * (first_hat / (jnp.sqrt(second_hat) + adam_epsilon) + deca...  10.7 us
    unnamed x103, local copies, waits for them, and re-layouts  10.3 us

profile of v2, /device:TPU:1, one launch (start us, length us, event | category | flops | bytes accessed | tf_op | source)
XLA Modules:
  0.0 296.7 jit_solution(9131390010191438142)
XLA Ops:
  0.7 1.7 copy.48.kv
  2.4 1.9 pad_maximum_fusion.3.qo
  5.5 41.3 %gather_weights.1 = (bf16[2,8,120,960]{3,2,1,0:T(8,128)(2,1)}, bf16[2,8,120,320]{3,2,1,0:T(8,128)(2,1)}, f32[8,8,128]{2,1,0:T(8,128)}, bf16[2,960,256]{2,1,0:T(8,128)(2,1)}) custom-call(bf16[2,120,960]{2,1,0:T(8,128)(2,1)} %pad_maximum_fusion.3.qo, bf16[2,120,320]{2,1,0:T(8,128)(2,1)} %copy.48.kv, f32[8,128]{1,0:T(8,128)} %pad.8.gain, bf16[960,256]{1,0:T(8,128)(2,1)} %bitcast.98), custom_call_target="tpu_custom_call" | custom-call | tf_op jit(solution)/shard_map/gather_weights/pallas_call | solution.py:167
  46.8 4.7 %fusion.52 = (bf16[1,8,120,960]{3,2,1,0:T(8,128)(2,1)}, bf16[1,8,120,960]{3,2,1,0:T(8,128)(2,1)}) fusion(bf16[2,8,120,960]{3,2,1,0:T(8,128)(2,1)} %get-tuple-element.46), kind=kLoop, calls=%fused_computation.110 | loop fusion | bytes 7372800 | tf_op jit(solution)/shard_map/slice | solution.py:1014
  55.7 58.6 %forward.1 = (bf16[960,256]{1,0:T(8,128)(2,1)}, bf16[960,256]{1,0:T(8,128)(2,1)}, f32[16,1,256]{2,1,0:T(1,128)}, bf16[4,640,256]{2,1,0:T(8,128)(2,1)}, bf16[960,...) custom-call(bf16[960,256]{1,0:T(8,128)(2,1)} %bitcast.85, ...), custom_call_target="tpu_custom_call" | custom-call | tf_op jit(solution)/shard_map/forward/pallas_call | solution.py:388
  115.5 3.1 %fusion.51 = (bf16[1,8,120,1280]{3,2,1,0:T(8,128)(2,1)S(1)}, bf16[1,8,120,1280]{3,2,1,0:T(8,128)(2,1)S(1)}) fusion(bf16[2,8,120,1280]{3,2,1,0:T(8,128)(2,1)} %get-tuple-element.51), kind=kLoop, calls=%fused_computation.109 | loop fusion | bytes 9830400 | tf_op jit(solution)/shard_map/slice | solution.py:1026
  118.6 1.6 fusion.38
  120.3 1.6 fusion.39
  122.3 3.0 %multiply_convert_fusion = (bf16[1280,512]{1,0:T(8,128)(2,1)S(1)}, bf16[1280,512]{1,0:T(8,128)(2,1)S(1)}, bf16[1280,512]{1,0:T(8,128)(2,1)S(1)}) fusion(f32[1280,512]{1,0:T(8,128)S(1)} %fusion.39, f32[1280,512]{1,0:T(8,128)S(1)} %fusion.38, bf16[1280,960]{1,0:T(8,128)(2,1)S(1)} %bitcast.101, bf16[960,256]{1,0:T(8,128)(2,1)S(1)} %get-tuple-element.146, ...), kind=kOutput, calls=%fused_computation.4 | convolution fusion | flops 1270743040 | bytes 12615680 | tf_op jit(solution)/shard_map/dot_general | solution.py:1032
  125.3 1.4 fusion.55
  126.8 1.4 convolution_add_fusion
  129.3 1.5 fusion.54
  133.1 4.3 %swap_5.1 = (f32[960,256]{1,0:T(8,128)}, f32[960,256]{1,0:T(8,128)}) custom-call(f32[960,256]{1,0:T(8,128)} %slice.107.refs_0_, f32[960,256]{1,0:T(8,128)} %slice.108.refs_1_), custom_call_target="tpu_custom_call" | custom-call | tf_op jit(solution)/shard_map/swap_5/pallas_call | solution.py:200
  137.7 1.8 multiply_reduce_fusion
  139.9 2.9 fusion.50
  142.9 1.5 convolution_convert_fusion.grad
  146.0 66.3 %backward.1 = (bf16[960,256]{1,0:T(8,128)(2,1)}, bf16[640,256]{1,0:T(8,128)(2,1)}, bf16[2,4,32,1280]{3,2,1,0:T(8,128)(2,1)}, bf16[4,32,1280]{2,1,0:T(8,128)(2,1)}, bf16[320,960]{1,0:T(8,128)(2,1)}) custom-call(bf16[960,256]{1,0:T(8,128)(2,1)} %get-tuple-element.56.q_low, bf16[4,640,256]{2,1,0:T(8,128)(2,1)} %get-tuple-element.57.keys, ...), custom_call_target="tpu_custom_call" | custom-call | tf_op jit(solution)/shard_map/backward/pallas_call | solution.py:624
  212.3 1.8 fusion.56
  216.7 57.6 %finish.1 = (bf16[2,128,512]{2,1,0:T(8,128)(2,1)}, bf16[2,128,448]{2,1,0:T(8,128)(2,1)}, bf16[2,128,320]{2,1,0:T(8,128)(2,1)}, bf16[128,2560]{1,0:T(8,128)(2,1)}...) custom-call(bf16[960,256]{1,0:T(8,128)(2,1)} %get-tuple-element.62.one, bf16[960,256]{1,0:T(8,128)(2,1)} %get-tuple-element.59.att, ...), custom_call_target="tpu_custom_call" | custom-call | tf_op jit(solution)/shard_map/finish/pallas_call | solution.py:932
  276.8 4.5 %convert_subtract_fusion = (f32[2,120,2560]{2,1,0:T(8,128)}, f32[2,120,2560]{2,1,0:T(8,128)}, f32[2,120,2560]{2,1,0:T(8,128)}) fusion(bf16[2,120,2560]{2,1,0:T(8,128)(2,1)S(1)} %copy-done.6, bf16[1,120,2560]{2,1,0:T(8,128)(2,1)S(1)} %slice_bitcast_fusion, bf16[1,120,2560]{2,1,0:T(8,128)(2,1)S(1)} %slice_bitcast_fusion.1, ...), kind=kLoop, calls=%fused_computation.2 | loop fusion | flops 12288000 | bytes 12288000 | tf_op jit(solution)/shard_map/sub | solution.py:978
  281.5 2.2 convert_subtract_fusion.2
  283.9 2.8 convert_subtract_fusion.1
  288.3 2.3 fusion.32
  290.6 1.9 copy.54
  (134 shorter events, 24.2 us)
Async XLA Ops:
  46.8 4.7 %copy-start.23 = (bf16[2,8,120,320]{3,2,1,0:T(8,128)(2,1)S(1)}, bf16[2,8,120,320]{3,2,1,0:T(8,128)(2,1)}, u32[]{:S(2)}) copy-start(bf16[2,8,120,320]{3,2,1,0:T(8,128)(2,1)} %get-tuple-element.47) | copy-start | bytes 3686404
  115.5 4.7 %copy-start.12 = (bf16[960,256]{1,0:T(8,128)(2,1)}, bf16[960,256]{1,0:T(8,128)(2,1)S(1)}, u32[]{:S(2)}) copy-start(bf16[960,256]{1,0:T(8,128)(2,1)S(1)} %get-tuple-element.147) | copy-start | bytes 1474564
  115.5 4.7 %copy-start.14 = (bf16[960,256]{1,0:T(8,128)(2,1)}, bf16[960,256]{1,0:T(8,128)(2,1)S(1)}, u32[]{:S(2)}) copy-start(bf16[960,256]{1,0:T(8,128)(2,1)S(1)} %get-tuple-element.148) | copy-start | bytes 1474564
  121.9 3.4 %copy-start.16 = (bf16[960,256]{1,0:T(8,128)(2,1)}, bf16[960,256]{1,0:T(8,128)(2,1)S(1)}, u32[]{:S(2)}) copy-start(bf16[960,256]{1,0:T(8,128)(2,1)S(1)} %get-tuple-element.145) | copy-start | bytes 1474564
  121.9 3.4 %copy-start.18 = (bf16[960,256]{1,0:T(8,128)(2,1)}, bf16[960,256]{1,0:T(8,128)(2,1)S(1)}, u32[]{:S(2)}) copy-start(bf16[960,256]{1,0:T(8,128)(2,1)S(1)} %get-tuple-element.146) | copy-start | bytes 1474564
  125.3 4.0 %copy-start.27 = (bf16[1280,512]{1,0:T(8,128)(2,1)}, bf16[1280,512]{1,0:T(8,128)(2,1)S(1)}, u32[]{:S(2)}) copy-start(bf16[1280,512]{1,0:T(8,128)(2,1)S(1)} %get-tuple-element.137.hidden) | copy-start | bytes 3932164
  132.0 5.4 %copy-start = (f32[960,256]{1,0:T(8,128)S(1)}, f32[960,256]{1,0:T(8,128)}, u32[]{:S(2)}) copy-start(f32[960,256]{1,0:T(8,128)} %get-tuple-element.49) | copy-start | bytes 2949124
  139.9 2.9 copy-start.3
  146.0 66.3 %copy-start.2 = (bf16[1,8,120,960]{3,2,1,0:T(8,128)(2,1)S(1)}, bf16[1,8,120,960]{3,2,1,0:T(8,128)(2,1)}, u32[]{:S(2)}) copy-start(bf16[1,8,120,960]{3,2,1,0:T(8,128)(2,1)} %get-tuple-element.141) | copy-start | bytes 5529604
  216.7 60.0 %copy-start.29 = (bf16[2,120,2560]{2,1,0:T(8,128)(2,1)S(1)}, bf16[2,120,2560]{2,1,0:T(8,128)(2,1)}, u32[]{:S(2)}) copy-start(bf16[2,120,2560]{2,1,0:T(8,128)(2,1)} %param.37) | copy-start | bytes 3686404
  276.7 4.6 %copy-start.36 = (bf16[2,128,512]{2,1,0:T(8,128)(2,1)S(1)}, bf16[2,128,512]{2,1,0:T(8,128)(2,1)}, u32[]{:S(2)}) copy-start(bf16[2,128,512]{2,1,0:T(8,128)(2,1)} %get-tuple-element.66) | copy-start | bytes 786436
  276.7 4.6 %copy-start.37 = (bf16[2,128,448]{2,1,0:T(8,128)(2,1)S(1)}, bf16[2,128,448]{2,1,0:T(8,128)(2,1)}, u32[]{:S(2)}) copy-start(bf16[2,128,448]{2,1,0:T(8,128)(2,1)} %get-tuple-element.67) | copy-start | bytes 688132
  276.7 4.6 %copy-start.31 = (bf16[120,960]{1,0:T(8,128)(2,1)S(1)}, bf16[120,960]{1,0:T(8,128)(2,1)}, u32[]{:S(2)}) copy-start(bf16[120,960]{1,0:T(8,128)(2,1)} %param.24) | copy-start | bytes 691204
  276.7 4.6 %copy-start.32 = (bf16[120,960]{1,0:T(8,128)(2,1)S(1)}, bf16[120,960]{1,0:T(8,128)(2,1)}, u32[]{:S(2)}) copy-start(bf16[120,960]{1,0:T(8,128)(2,1)} %param.22) | copy-start | bytes 691204
  276.7 4.6 %copy-start.38 = (bf16[120,960]{1,0:T(8,128)(2,1)S(1)}, bf16[120,960]{1,0:T(8,128)(2,1)}, u32[]{:S(2)}) copy-start(bf16[120,960]{1,0:T(8,128)(2,1)} %param.30) | copy-start | bytes 691204
  276.8 4.6 %copy-start.39 = (bf16[120,960]{1,0:T(8,128)(2,1)S(1)}, bf16[120,960]{1,0:T(8,128)(2,1)}, u32[]{:S(2)}) copy-start(bf16[120,960]{1,0:T(8,128)(2,1)} %param.36) | copy-start | bytes 691204
  276.8 4.6 %copy-start.40 = (bf16[120,960]{1,0:T(8,128)(2,1)S(1)}, bf16[120,960]{1,0:T(8,128)(2,1)}, u32[]{:S(2)}) copy-start(bf16[120,960]{1,0:T(8,128)(2,1)} %param.34) | copy-start | bytes 691204
  276.8 4.6 %copy-start.41 = (bf16[120,960]{1,0:T(8,128)(2,1)S(1)}, bf16[120,960]{1,0:T(8,128)(2,1)}, u32[]{:S(2)}) copy-start(bf16[120,960]{1,0:T(8,128)(2,1)} %param.28) | copy-start | bytes 691204
  283.9 3.6 %copy-start.43 = (bf16[2,120,320]{1,2,0:T(8,128)(2,1)S(1)}, bf16[2,120,320]{1,2,0:T(8,128)(2,1)}, u32[]{:S(2)}) copy-start(bf16[2,120,320]{1,2,0:T(8,128)(2,1)} %param.35) | copy-start | bytes 460804
  283.9 4.4 %copy-start.22 = (bf16[2,120,320]{2,1,0:T(8,128)(2,1)S(1)}, bf16[2,120,320]{2,1,0:T(8,128)(2,1)}, u32[]{:S(2)}) copy-start(bf16[2,120,320]{2,1,0:T(8,128)(2,1)} %copy.48.kv) | copy-start | bytes 460804
  288.3 5.9 %copy-start.44 = (bf16[2,120]{1,0:T(2,128)(2,1)S(1)}, bf16[2,120]{1,0:T(2,128)(2,1)}, u32[]{:S(2)}) copy-start(bf16[2,120]{1,0:T(2,128)(2,1)} %param.27) | copy-start | bytes 1444
  288.3 5.9 %copy-start.45 = (bf16[2,120]{1,0:T(2,128)(2,1)S(1)}, bf16[2,120]{1,0:T(2,128)(2,1)}, u32[]{:S(2)}) copy-start(bf16[2,120]{1,0:T(2,128)(2,1)} %param.33) | copy-start | bytes 1444
  288.3 5.9 %copy-start.46 = (bf16[2,120]{1,0:T(2,128)(2,1)S(1)}, bf16[2,120]{1,0:T(2,128)(2,1)}, u32[]{:S(2)}) copy-start(bf16[2,120]{1,0:T(2,128)(2,1)} %param.39) | copy-start | bytes 1444
  288.3 7.2 %copy-start.7 = (f32[960,256]{1,0:T(8,128)S(1)}, f32[960,256]{1,0:T(8,128)}, u32[]{:S(2)}) copy-start(f32[960,256]{1,0:T(8,128)} %get-tuple-element.134) | copy-start | bytes 2949124
  (24 other events, 44.3 us)

commit v3 on v2

--- a/solution.py
+++ b/solution.py
@@ -69,153 +69,23 @@
     )
 
 
+def columns(total):
+    return [(start, min(start + 256, total)) for start in range(0, total, 256)]
+
+
 ORDER = (1, 3, 2)
 SIDE = (1, 3, 3, 1)
 
 
-def gather_kernel(
-    qo, kv, gain, dy, qo_all, kv_all, gain_all, dy_all, send_y, send_x, send_s, recv, recv_s, local
-):
-    x, y, z, c = place()
-    xl = lax.rem(x, 2)
-    f = 4 * xl + y
-    sibling = at(x, y, z, 1 - c)
-    greet([at(x, y + j, z, c) for j in (1, 2, 3)] + [at(x + j, y, z, c) for j in (1, 3)] + [sibling])
-    own = (qo.at[c], kv.at[c], gain)
-
-    def slot(item, g, core):
-        if item == 2:
-            return gain_all.at[g]
-        return (qo_all, kv_all)[item].at[core, g]
-
-    def wait_slot(item, g):
-        ref = slot(item, g, c)
-        remote(ref, ref, send_s.at[0, 0], recv.at[item, g], sibling).wait_recv()
-
-    def send_row(item, j):
-        return remote(own[item], slot(item, f, c), send_y.at[item, j - 1], recv.at[item, f], at(x, y + j, z, c))
-
-    def send_side(item, j):
-        g = 4 * xl + lax.rem(y + j, 4)
-        return remote(
-            own[item] if j == 0 else slot(item, g, c),
-            slot(item, g, c),
-            send_x.at[item, j],
-            recv.at[item, g],
-            at(x + SIDE[j], y, z, c),
-        )
-
-    def column(k):
-        return 4 * xl + lax.rem(y + k + 1, 4) if k < 3 else 4 * (1 - xl) + lax.rem(y + k - 3, 4)
-
-    def send_sib(item, k):
-        ref = slot(item, column(k), c)
-        return remote(ref, ref, send_s.at[item, k], recv_s.at[item, column(k)], sibling)
-
-    items = (2, 0, 1)
-    for item in items:
-        send_side(item, 0).start()
-        for j in ORDER:
-            send_row(item, j).start()
-    exchange = remote(dy, dy_all.at[1], send_s.at[2, 0], recv_s.at[2, 0], sibling)
-    exchange.start()
-    copies = [
-        pltpu.make_async_copy(qo, qo_all.at[:, f], local.at[0]),
-        pltpu.make_async_copy(kv, kv_all.at[:, f], local.at[1]),
-        pltpu.make_async_copy(gain, gain_all.at[f], local.at[2]),
-        pltpu.make_async_copy(dy, dy_all.at[0], local.at[3]),
-    ]
-    for copy in copies:
-        copy.start()
-    for item in items:
-        for j in (1, 3):
-            wait_slot(item, 4 * xl + lax.rem(y + j, 4))
-            send_side(item, j).start()
-            if item < 2:
-                send_sib(item, j - 1).start()
-    for item in (0, 1):
-        wait_slot(item, column(3))
-        send_sib(item, 3).start()
-    for item in items:
-        wait_slot(item, column(1))
-        send_side(item, 2).start()
-        if item < 2:
-            send_sib(item, 1).start()
-    for k in (4, 6, 5):
-        for item in (0, 1):
-            wait_slot(item, column(k))
-            send_sib(item, k).start()
-    for k in (3, 4, 6, 5):
-        wait_slot(2, column(k))
-    for copy in copies:
-        copy.wait()
-    exchange.wait()
-    for item in (0, 1):
-        for k in range(7):
-            ref = slot(item, column(k), 1 - c)
-            remote(ref, ref, send_s.at[0, 0], recv_s.at[item, column(k)], sibling).wait_recv()
-            send_sib(item, k).wait_send()
-    for item in items:
-        for j in ORDER:
-            send_row(item, j).wait_send()
-        for j in range(4):
-            send_side(item, j).wait_send()
-
-
-def gather_weights(qo, kv, gain, dy):
-    sem = pltpu.SemaphoreType.DMA
-    return pl.pallas_call(
-        gather_kernel,
-        name="gather_weights",
-        out_shape=(
-            jax.ShapeDtypeStruct((2, 8, ROWS, D), BF),
-            jax.ShapeDtypeStruct((2, 8, ROWS, KW), BF),
-            jax.ShapeDtypeStruct((8, 8, 128), F32),
-            jax.ShapeDtypeStruct((2, D, TOK), BF),
-        ),
-        in_specs=[ANY] * 4,
-        out_specs=(ANY,) * 4,
-        scratch_shapes=[sem((3, 3)), sem((3, 4)), sem((3, 7)), sem((3, 8)), sem((3, 8)), sem((4,))],
-        compiler_params=params(0),
-    )(qo, kv, gain, dy)
-
-
-def swap_kernel(count, *refs):
-    ins, outs = refs[:count], refs[count : 2 * count]
-    send, recv = refs[2 * count :]
-    x, y, z, c = place()
-    sibling = at(x, y, z, 1 - c)
-    greet([sibling])
-    copies = [
-        remote(ins[i], outs[i], send.at[i], recv.at[i], sibling) for i in range(count)
-    ]
-    for copy in copies:
-        copy.start()
-    for copy in copies:
-        copy.wait()
-
-
-def swap(number, *arrays):
-    count = len(arrays)
-    return pl.pallas_call(
-        functools.partial(swap_kernel, count),
-        name="swap_%d" % number,
-        out_shape=tuple(jax.ShapeDtypeStruct(a.shape, a.dtype) for a in arrays),
-        in_specs=[ANY] * count,
-        out_specs=(ANY,) * count,
-        scratch_shapes=[pltpu.SemaphoreType.DMA((count,)), pltpu.SemaphoreType.DMA((count,))],
-        compiler_params=params(number),
-    )(*arrays)
-
-
 def dot(a, b, ca, cb):
     return lax.dot_general(a, b, (((ca,), (cb,)), ((), ())), preferred_element_type=F32)
 
 
 def forward_kernel(
-    stream, wq, wk, wv, wo, gains, cos, sin, gu, dn,
-    q_low, att, lse, kv_out, one, mid, two_all, gu_all, dn_all,
-    keys, wide, two, send, recv, send_y, send_x, recv_w, local,
+    stream, cos, sin, qo, kv, gain, dy, gu, dn,
+    q_low, att, lse, kv_out, one, mid, two_all, dy_all, gains_out, q_all, o_all, k_all, v_all, gate_all, up_all, dn_all,
+    keys, wide, ones, two, qo_land, kv_land, gain_land,
+    send, recv, send_y, send_x, recv_w, send_ay, send_ax, send_as, recv_a, recv_as, local,
 ):
     x, y, z, c = place()
     xl = lax.rem(x, 2)
@@ -226,12 +96,55 @@
     sibling, far = at(x, y, z, 1 - c), at(x + 2, y, z, c)
     greet([at(x, y + j, z, c) for j in (1, 2, 3)] + [at(x + j, y, z, c) for j in (1, 2, 3)] + [sibling])
 
+    def column(k):
+        return 4 * xl + lax.rem(y + k + 1, 4) if k < 3 else 4 * (1 - xl) + lax.rem(y + k - 3, 4)
+
+    own_a = (qo.at[c], kv.at[c], gain)
+
+    def slot_a(item, g, core):
+        if item == 2:
+            return gain_land.at[g]
+        return (qo_land, kv_land)[item].at[core, g]
+
+    def wait_a(item, k):
+        ref = slot_a(item, column(k), c)
+        remote(ref, ref, send_as.at[0, 0], recv_a.at[item, column(k)], sibling).wait_recv()
+
+    def row_a(item, j):
+        return remote(own_a[item], slot_a(item, f, c), send_ay.at[item, j - 1], recv_a.at[item, f], at(x, y + j, z, c))
+
+    def side_a(item, j):
+        g = 4 * xl + lax.rem(y + j, 4)
+        return remote(
+            own_a[item] if j == 0 else slot_a(item, g, c),
+            slot_a(item, g, c),
+            send_ax.at[item, j],
+            recv_a.at[item, g],
+            at(x + SIDE[j], y, z, c),
+        )
+
+    def sib_a(item, k):
+        ref = slot_a(item, column(k), c)
+        return remote(ref, ref, send_as.at[item, k], recv_as.at[item, column(k)], sibling)
+
+    def take(item, k):
+        wait_a(item, k)
+        if k < 3:
+            side_a(item, k + 1).start()
+        if item < 2:
+            sib_a(item, k).start()
+
+    def taken(item):
+        for k in range(7):
+            ref = slot_a(item, column(k), 1 - c)
+            remote(ref, ref, send_as.at[0, 0], recv_as.at[item, column(k)], sibling).wait_recv()
+
     lanes = pl.ds(pl.multiple_of(c * FH, 128), FH)
     own = (gu.at[0, :, lanes], gu.at[1, :, lanes], dn.at[0:160], dn.at[160:320])
 
     def slot(item, g):
         if item < 2:
-            return gu_all.at[item, g]
+            return (gate_all, up_all)[item].at[g]
         return dn_all.at[lax.rem(g, 4), 160 * (item - 2) : 160 * (item - 1)]
 
     def wait_slot(item, g):
@@ -259,6 +172,34 @@
     def pass_down(offsets):
         pl.when(holds)(lambda: pass_on((2, 3), offsets))
 
+    for item in (2, 1, 0):
+        side_a(item, 0).start()
+        for j in ORDER:
+            row_a(item, j).start()
+    copies = [
+        pltpu.make_async_copy(gain, gain_land.at[f], local.at[0]),
+        pltpu.make_async_copy(kv, kv_land.at[:, f], local.at[1]),
+        pltpu.make_async_copy(qo, qo_land.at[:, f], local.at[2]),
+        pltpu.make_async_copy(own[0], gate_all.at[f], local.at[3]),
+        pltpu.make_async_copy(own[1], up_all.at[f], local.at[8]),
+        pltpu.make_async_copy(dy, dy_all.at[0], local.at[4]),
+    ]
+    for copy in copies:
+        copy.start()
+    own_down = pltpu.make_async_copy(dn, dn_all.at[y], local.at[5])
+    pl.when(holds)(own_down.start)
+
+    co, si = cos[...], sin[...]
+    wide[...] = stream[...].astype(F32)
+    scale = lax.rsqrt(jnp.sum(wide[...] ** 2, axis=0, keepdims=True) / D + norm_epsilon)
+
+    for k in (0, 2):
+        take(2, k)
+        take(1, k)
+    take(1, 3)
+    wait_a(2, 3)
+    for k in (0, 2):
+        take(0, k)
     for j in ORDER:
         for item in (0, 1):
             send_row(item, j).start()
@@ -268,25 +209,45 @@
             for item in (2, 3):
                 send_row(item, j).start()
 
-    own_copies = [pltpu.make_async_copy(gu.at[:, :, lanes], gu_all.at[:, f], local.at[0])]
-    own_copies[0].start()
-    own_down = pltpu.make_async_copy(dn, dn_all.at[y], local.at[1])
-    pl.when(holds)(own_down.start)
-
-    co, si = cos[...], sin[...]
-    scale = lax.rsqrt(jnp.sum(stream[...].astype(F32) ** 2, axis=0, keepdims=True) / D + norm_epsilon)
-    one[...] = (stream[...].astype(F32) * scale * gains[0]).astype(BF)
-    wide[:KW, :] = dot(wk[...], one[...], 0, 0)
-    wide[KW : 2 * KW, :] = dot(wv[...], one[...], 0, 0)
+    take(2, 1)
+    take(1, 1)
+    take(0, 3)
+    for k in (4, 6, 5):
+        wait_a(2, k)
+        take(1, k)
+    take(0, 1)
+
+    for copy in copies[:3]:
+        copy.wait()
+    for g in range(8):
+        tile = gain_land[g].T
+        gains_out[0, ROWS * g : ROWS * (g + 1), :] = tile[:ROWS, 0:1]
+        gains_out[1, ROWS * g : ROWS * (g + 1), :] = tile[:ROWS, 1:2]
+    ones[...] = wide[...] * scale * gains_out[0]
+    one[...] = ones[...].astype(BF)
+    taken(1)
+
+    def block(ref, g):
+        return ref[ROWS * g : ROWS * (g + 1), :].astype(BF)
+
+    def project(land, which, cols, source):
+        total = dot(land[which, 0, :, cols], block(source, 0), 0, 0)
+        for g in range(1, 8):
+            total += dot(land[which, g, :, cols], block(source, g), 0, 0)
+        return total
+
+    key = project(kv_land, 0, slice(0, KW), ones)
     for h in range(KEY_VALUE_HEADS):
-        a, b = wide[64 * h : 64 * h + 32, :], wide[64 * h + 32 : 64 * h + 64, :]
+        a, b = key[64 * h : 64 * h + 32, :], key[64 * h + 32 : 64 * h + 64, :]
         keys[me, 64 * h : 64 * h + 32, :] = (a * co - b * si).astype(BF)
         keys[me, 64 * h + 32 : 64 * h + 64, :] = (b * co + a * si).astype(BF)
-    keys[me, KW:, :] = wide[KW : 2 * KW, :].astype(BF)
+    keys[me, KW:, :] = project(kv_land, 1, slice(0, KW), ones).astype(BF)
     to_far = remote(keys.at[me], keys.at[me], send.at[0], recv.at[0], far)
     to_sib = remote(keys.at[me], keys.at[me], send.at[1], recv.at[1], sibling)
     to_far.start()
     to_sib.start()
+    for k in (4, 6, 5):
+        take(0, k)
     for item in (0, 1):
         send_side(item, 0).start()
 
@@ -295,13 +256,24 @@
         for item in (2, 3):
             send_side(item, 0).start()
 
-    for start in range(0, D, 256):
-        stop = min(start + 256, D)
-        wide[start:stop, :] = dot(wq[:, start:stop], one[...], 0, 0)
-    for h in range(QUERY_HEADS):
-        a, b = wide[64 * h : 64 * h + 32, :], wide[64 * h + 32 : 64 * h + 64, :]
-        q_low[64 * h : 64 * h + 32, :] = ((a * co - b * si).astype(BF) * score_scale).astype(BF)
-        q_low[64 * h + 32 : 64 * h + 64, :] = ((b * co + a * si).astype(BF) * score_scale).astype(BF)
+    taken(0)
+    exchange = remote(dy, dy_all.at[1], send.at[4], recv.at[4], sibling)
+    exchange.start()
+    keep_a = [
+        pltpu.make_async_copy(qo_land.at[0], q_all, local.at[0]),
+        pltpu.make_async_copy(qo_land.at[1], o_all, local.at[1]),
+        pltpu.make_async_copy(kv_land.at[0], k_all, local.at[2]),
+        pltpu.make_async_copy(kv_land.at[1], v_all, local.at[6]),
+    ]
+    for copy in keep_a:
+        copy.start()
+    for start, stop in columns(D):
+        query = project(qo_land, 0, slice(start, stop), ones)
+        for h in range(0, stop - start, 64):
+            a, b = query[h : h + 32, :], query[h + 32 : h + 64, :]
+            rows = start + h
+            q_low[rows : rows + 32, :] = ((a * co - b * si).astype(BF) * score_scale).astype(BF)
+            q_low[rows + 32 : rows + 64, :] = ((b * co + a * si).astype(BF) * score_scale).astype(BF)
     pass_on((0,), (1, 3))
     remote(keys.at[far_slot], keys.at[far_slot], send.at[0], recv.at[0], far).wait_recv()
     on = remote(keys.at[far_slot], keys.at[far_slot], send.at[2], recv.at[2], sibling)
@@ -326,26 +298,26 @@
         acc = dot(keys[0, vrows, :], e[0].astype(BF), 1, 0)
         for j in range(1, 4):
             acc += dot(keys[j, vrows, :], e[j].astype(BF), 1, 0)
-        att[rows, :] = (acc / total).astype(BF)
+        ones[rows, :] = acc / total
         lse[pl.ds(h, 1), 0, :] = top + jnp.log(total)
         pl.when(h == 1)(lambda: pass_on((1,), (1, 3)))
-        pl.when(h == 5)(lambda: pass_down((1, 3)))
+        pl.when(h == 4)(lambda: pass_down((1, 3)))
         pl.when(h == 9)(lambda: pass_on((0,), (2,)))
         pl.when(h == 13)(lambda: pass_on((1,), (2,)))
         return carry
 
     lax.fori_loop(0, QUERY_HEADS, head, 0)
     kv_out[...] = keys[...]
+    att[...] = ones[...].astype(BF)
 
     square = jnp.zeros((1, TOK), F32)
-    for start in range(0, D, 256):
-        stop = min(start + 256, D)
-        part = stream[start:stop, :].astype(F32) + dot(wo[:, start:stop], att[...], 0, 0)
+    for start, stop in columns(D):
+        part = wide[start:stop, :] + project(qo_land, 1, slice(start, stop), ones)
         mid[start:stop, :] = part
         square += jnp.sum(part * part, axis=0, keepdims=True)
     scale = lax.rsqrt(square / D + norm_epsilon)
-    two[...] = (mid[...] * scale * gains[1]).astype(BF)
-    keep = pltpu.make_async_copy(two, two_all.at[0], local.at[2])
+    two[...] = (mid[...] * scale * gains_out[1]).astype(BF)
+    keep = pltpu.make_async_copy(two, two_all.at[0], local.at[7])
     keep.start()
     trade = remote(two, two_all.at[1], send.at[3], recv.at[3], sibling)
     trade.start()
@@ -361,12 +333,21 @@
             for item in (2, 3):
                 wait_slot(item, g)
 
-    own_copies[0].wait()
-    keep.wait()
+    for copy in copies[3:] + keep_a + [keep]:
+        copy.wait()
     trade.wait()
+    exchange.wait()
     to_far.wait_send()
     to_sib.wait_send()
     on.wait_send()
+    for item in (0, 1, 2):
+        for j in ORDER:
+            row_a(item, j).wait_send()
+        for j in range(4):
+            side_a(item, j).wait_send()
+        if item < 2:
+            for k in range(7):
+                sib_a(item, k).wait_send()
 
     def sent(items):
         for item in items:
@@ -383,37 +364,54 @@
         sent((2, 3))
 
 
-def forward(stream, wq, wk, wv, wo, gains, cos, sin, gu, dn):
+def forward(*args):
     sem = pltpu.SemaphoreType.DMA
+    low = lambda *shape: jax.ShapeDtypeStruct(shape, BF)
     return pl.pallas_call(
         forward_kernel,
         name="forward",
         out_shape=(
-            jax.ShapeDtypeStruct((D, TOK), BF),
-            jax.ShapeDtypeStruct((D, TOK), BF),
+            low(D, TOK),
+            low(D, TOK),
             jax.ShapeDtypeStruct((16, 1, TOK), F32),
-            jax.ShapeDtypeStruct((4, 2 * KW, TOK), BF),
-            jax.ShapeDtypeStruct((D, TOK), BF),
+            low(4, 2 * KW, TOK),
+            low(D, TOK),
             jax.ShapeDtypeStruct((D, TOK), F32),
-            jax.ShapeDtypeStruct((2, D, TOK), BF),
-            jax.ShapeDtypeStruct((2, 8, ROWS, FH), BF),
-            jax.ShapeDtypeStruct((4, KW, D), BF),
+            low(2, D, TOK),
+            low(2, D, TOK),
+            jax.ShapeDtypeStruct((2, D, 1), F32),
+            low(8, ROWS, D),
+            low(8, ROWS, D),
+            low(8, ROWS, KW),
+            low(8, ROWS, KW),
+            low(8, ROWS, FH),
+            low(8, ROWS, FH),
+            low(4, KW, D),
         ),
-        in_specs=[VM] * 8 + [ANY] * 2,
-        out_specs=(VM,) * 6 + (ANY,) * 3,
+        in_specs=[VM] * 3 + [ANY] * 6,
+        out_specs=(VM,) * 6 + (ANY,) * 2 + (VM,) + (ANY,) * 7,
         scratch_shapes=[
             pltpu.VMEM((4, 2 * KW, TOK), BF),
             pltpu.VMEM((D, TOK), F32),
+            pltpu.VMEM((D, TOK), F32),
             pltpu.VMEM((D, TOK), BF),
-            sem((4,)),
-            sem((4,)),
+            pltpu.VMEM((2, 8, ROWS, D), BF),
+            pltpu.VMEM((2, 8, ROWS, KW), BF),
+            pltpu.VMEM((8, 8, 128), F32),
+            sem((5,)),
+            sem((5,)),
             sem((4, 3)),
             sem((4, 4)),
             sem((4, 8)),
-            sem((3,)),
+            sem((3, 3)),
+            sem((3, 4)),
+            sem((2, 7)),
+            sem((3, 8)),
+            sem((2, 8)),
+            sem((9,)),
         ],
         compiler_params=params(1),
-    )(stream, wq, wk, wv, wo, gains, cos, sin, gu, dn)
+    )(*args)
 
 
 def summed(own, got, count=3):
@@ -441,13 +439,10 @@
     ]
 
 
-def columns(total):
-    return [(start, min(start + 256, total)) for start in range(0, total, 256)]
-
-
 def backward_kernel(
-    q_low, keys, lse, att, grad, cos, sin, two, gate_grad, up_grad, hidden, dy,
-    q_back, kv_back, c0_out, c1_out, d_out,
+    q_low, keys, lse, att, cos, sin, two_all, dy_all, mid, gains, wg, wu, wd, wo,
+    q_back, kv_back, c0_out, c1_out, d_out, result, mid_grad, mid_low, gain_grad,
+    two, dy, gate_grad, up_grad, hidden, grad, down_part, down_got, two_part, two_got, send_s, recv_s,
     mine, got, far_got, acc, c0, c0r, c1, c1r, c1s, c1t, d, dr, ds_, dt,
     send, recv, send_z, recv_z, send_x, recv_x, send_t, recv_t, send_y, recv_y, send_d, recv_d,
 ):
@@ -481,6 +476,19 @@
     def d_x(j):
         return remote(ds_, dt.at[j - 1], send_d.at[j - 1], recv_d.at[j - 1], along_x[j - 1])
 
+    for i in (0, 1):
+        two[:, TOK * i : TOK * (i + 1)] = two_all[i]
+        dy[:, TOK * i : TOK * (i + 1)] = dy_all[i]
+    for start, stop in columns(FH):
+        gate = dot(wg[:, start:stop], two[...], 0, 0)
+        up = dot(wu[:, start:stop], two[...], 0, 0)
+        back = dot(wd[start:stop, :], dy[...], 1, 0)
+        sigmoid = jax.nn.sigmoid(gate)
+        silu = gate * sigmoid
+        hidden[start:stop, :] = (silu * up).astype(BF)
+        gate_grad[start:stop, :] = (back * up * sigmoid * (1.0 + gate * (1.0 - sigmoid))).astype(BF)
+        up_grad[start:stop, :] = (back * silu).astype(BF)
+
     for start, stop in columns(FH):
         part = planes(dot(two[...], gate_grad[start:stop, :], 1, 1), nothing)
         for f in range(8):
@@ -499,6 +507,30 @@
             c1[f // 4, f % 4, :, start:stop] = part[f]
     for i in (0, 1):
         c1_x(i).start()
+
+    far_half = pl.ds(TOK, TOK)
+    for start, stop in columns(D):
+        two_part[start:stop, :] = dot(wg[start:stop, :], gate_grad[...], 1, 0) + dot(wu[start:stop, :], up_grad[...], 1, 0)
+    trade_two = remote(two_part.at[:, far_half], two_got, send_s.at[0], recv_s.at[0], sibling)
+    trade_two.start()
+    for start, stop in columns(D):
+        down_part[start:stop, :] = dot(wd[:, start:stop], hidden[...], 0, 0)
+    trade_down = remote(down_part.at[:, far_half], down_got, send_s.at[1], recv_s.at[1], sibling)
+    trade_down.start()
+    middle = mid[...]
+    scale = lax.rsqrt(jnp.sum(middle * middle, axis=0, keepdims=True) / D + norm_epsilon)
+    trade_two.wait_recv()
+    normal = middle * scale
+    incoming = two_part[:, :TOK] + two_got[...]
+    gain_grad[...] = jnp.sum(incoming * normal, axis=1, keepdims=True)
+    scaled = incoming * gains[1]
+    level_two = jnp.sum(scaled * normal, axis=0, keepdims=True) / D
+    mid_grad[...] = dy_all[0].astype(F32) + scale * (scaled - normal * level_two)
+    mid_low[...] = mid_grad[...].astype(BF)
+    for start, stop in columns(D):
+        grad[start:stop, :] = dot(wo[start:stop, :], mid_low[...], 1, 0).astype(BF)
+    trade_down.wait_recv()
+    result[...] = (middle + down_part[:, :TOK] + down_got[...]).astype(BF)
 
     def step_c1():
         for i in (0, 1):
@@ -601,6 +633,8 @@
     for k in range(4):
         c1_out[k] = summed(c1s[k, quarter(z, 32)], [c1t[j, k] for j in range(3)])
 
+    trade_two.wait_send()
+    trade_down.wait_send()
     to_sib_far.wait_send()
     to_sib.wait_send()
     to_far.wait_send()
@@ -630,10 +664,18 @@
             jax.ShapeDtypeStruct((2, 4, 32, FH), BF),
             jax.ShapeDtypeStruct((4, 32, FH), BF),
             jax.ShapeDtypeStruct((KW, D), BF),
+            jax.ShapeDtypeStruct((D, TOK), BF),
+            jax.ShapeDtypeStruct((D, TOK), F32),
+            jax.ShapeDtypeStruct((D, TOK), BF),
+            jax.ShapeDtypeStruct((D, 1), F32),
         ),
-        in_specs=[VM] * 12,
-        out_specs=(VM,) * 5,
+        in_specs=[VM] * 14,
+        out_specs=(VM,) * 9,
         scratch_shapes=[
+            vm(D, 2 * TOK), vm(D, 2 * TOK), vm(FH, 2 * TOK), vm(FH, 2 * TOK), vm(FH, 2 * TOK), vm(D, TOK),
+            pltpu.VMEM((D, 2 * TOK), F32), pltpu.VMEM((D, TOK), F32),
+            pltpu.VMEM((D, 2 * TOK), F32), pltpu.VMEM((D, TOK), F32),
+            sem((2,)), sem((2,)),
             vm(4, 2 * KW, TOK), vm(2, 2 * KW, TOK), vm(2 * KW, TOK), pltpu.VMEM((4, 2, 64, TOK), F32),
             vm(2, 4, PAD, FH), vm(3, 2, 4, 32, FH),
             vm(2, 4, PAD, FH), vm(2, 4, PAD, 640), vm(4, PAD, FH), vm(3, 4, 32, FH),
@@ -650,8 +692,9 @@
 
 
 def finish_kernel(
-    one, att, mid, q_back, kv_back, gain, c0, c1, dd,
-    lo_sum, hi_sum, kv_sum, c0_sum, c1_sum, d_sum,
+    one, att, mid, q_back, kv_back, c0, c1, dd, stream, mid_grad, gains, gain_two, wq, wk, wv,
+    lo_sum, hi_sum, kv_sum, c0_sum, c1_sum, d_sum, in_grad,
+    gain_cols,
     left, right, thin, both, lo, hi, kv,
     lo1, lo1r, lo2, lo2r, lo3, lo3r,
     kv1, kv1r, kv2, kv2r, kv3, kv3r,
@@ -747,6 +790,31 @@
         thin[:, near] = kv_back[KW:, :]
 
     both[:, near] = one[...]
+
+    source = stream[...].astype(F32)
+    scale = lax.rsqrt(jnp.sum(source * source, axis=0, keepdims=True) / D + norm_epsilon)
+    normal = source * scale
+    for start, stop in columns(D):
+        in_grad[start:stop, :] = (
+            dot(wq[start:stop, :], q_back[...], 1, 0)
+            + dot(wk[start:stop, :], kv_back[:KW, :], 1, 0)
+            + dot(wv[start:stop, :], kv_back[KW:, :], 1, 0)
+        )
+    incoming = in_grad[...]
+    gain_cols[...] = jnp.sum(incoming * normal, axis=1, keepdims=True)
+    scaled = incoming * gains[0]
+    level = jnp.sum(scaled * normal, axis=0, keepdims=True) / D
+    in_grad[...] = mid_grad[...] + scale * (scaled - normal * level)
+    lane = lax.broadcasted_iota(jnp.int32, (PAD, 128), 1)
+    gain = []
+    for f in range(8):
+        rows_f = slice(ROWS * f, ROWS * (f + 1))
+        zeros = jnp.zeros((PAD - ROWS, 128), F32)
+        first_col = jnp.concatenate([jnp.broadcast_to(gain_cols[rows_f, :], (ROWS, 128)), zeros], axis=0)
+        second_col = jnp.concatenate([jnp.broadcast_to(gain_two[rows_f, :], (ROWS, 128)), zeros], axis=0)
+        tile = jnp.where(lane == 0, first_col, jnp.where(lane == 1, second_col, 0.0)).T
+        gain.append(jnp.concatenate([tile[:8], jnp.zeros((8, 128), F32)], axis=1))
+
     trade(3, one, both.at[:, far]).wait_recv()
     trade(2, kv_back.at[:KW], thin.at[:, far]).wait_recv()
     nothing = [jnp.zeros((8, KW), F32)] * 8
@@ -939,10 +1007,12 @@
             jax.ShapeDtypeStruct((PAD, FF), BF),
             jax.ShapeDtypeStruct((PAD, FF), BF),
             jax.ShapeDtypeStruct((KW, D), BF),
+            jax.ShapeDtypeStruct((D, TOK), F32),
         ),
-        in_specs=[VM] * 9,
-        out_specs=(ANY,) * 6,
+        in_specs=[VM] * 15,
+        out_specs=(ANY,) * 6 + (VM,),
         scratch_shapes=[
+            pltpu.VMEM((D, 1), F32),
             vm(D, 2 * TOK), vm(D, 2 * TOK), vm(KW, 2 * TOK), vm(D, 2 * TOK),
             vm(2, 4, PAD, WIDE), vm(2, 4, PAD, NARROW), vm(2, 4, PAD, KW),
         ]
@@ -960,15 +1030,6 @@
     )(*args)
 
 
-def norm_backward(stream, gain, incoming):
-    scale = lax.rsqrt(jnp.mean(stream * stream, axis=0, keepdims=True) + norm_epsilon)
-    normal = stream * scale
-    gain_grad = jnp.sum(incoming * normal, axis=1)
-    scaled = incoming * gain
-    stream_grad = scale * (scaled - normal * jnp.mean(scaled * normal, axis=0, keepdims=True))
-    return (stream_grad, gain_grad)
-
-
 def adamw_update(weight, gradient, first, second, rate, decay):
     weight = weight.astype(F32)
     first_new = beta_first * first.astype(F32) + (1.0 - beta_first) * gradient
@@ -979,6 +1040,49 @@
         first_hat / (jnp.sqrt(second_hat) + adam_epsilon) + decay * weight
     )
     return (weight_new, first_new, second_new)
+
+
+def update_kernel(lo, hi, narrow, gate, up, down, *refs):
+    state, new = refs[:18], refs[18:]
+
+    def update(which, index, gradient, rate=matrix_rate, decay=matrix_decay):
+        weight, first, second = (state[3 * which + i][index] for i in range(3))
+        for i, value in enumerate(adamw_update(weight, gradient, first, second, rate, decay)):
+            new[3 * which + i][index] = value
+
+    for m, source in ((0, gate), (1, up)):
+        update(3, m, source[...].astype(F32)[:ROWS])
+    update(4, slice(None), down[...].astype(F32))
+
+    @pl.when(pl.program_id(0) == 0)
+    def _():
+        for which, core in ((0, 0), (2, 1)):
+            update(which, (slice(None), slice(0, WIDE)), lo[core].astype(F32)[:ROWS])
+            update(which, (slice(None), slice(WIDE, D)), hi[core].astype(F32)[:ROWS])
+        for m in (0, 1):
+            update(1, m, narrow[m].astype(F32).T[:, :ROWS])
+        gains = lo[0, 112:, :128].astype(F32) + lo[1, 112:, :128].astype(F32)
+        update(5, slice(None), gains[8:10, :ROWS], gain_rate, 0.0)
+
+
+def update_all(lo, hi, narrow, gate, up, down, state):
+    steps = 5
+    fixed = lambda a: pl.BlockSpec(a.shape, lambda i: (0,) * len(a.shape))
+    sums = pl.BlockSpec((PAD, FF // steps), lambda i: (0, i))
+    rows = pl.BlockSpec((KW // steps, D), lambda i: (i, 0))
+    wide = pl.BlockSpec((2, ROWS, FF // steps), lambda i: (0, 0, i))
+    specs = []
+    for i, array in enumerate(state):
+        specs.append(wide if i // 3 == 3 else rows if i // 3 == 4 else fixed(array))
+    return pl.pallas_call(
+        update_kernel,
+        name="update",
+        grid=(steps,),
+        out_shape=tuple(jax.ShapeDtypeStruct(a.shape, F32) for a in state),
+        in_specs=[fixed(lo), fixed(hi), fixed(narrow), sums, sums, rows] + specs,
+        out_specs=tuple(specs),
+        compiler_params=pltpu.CompilerParams(vmem_limit_bytes=40 * 2**20),
+    )(lo, hi, narrow, gate, up, down, *state)
 
 
 def body(
@@ -1007,87 +1111,46 @@
     core = lax.rem(ctx, 2)
     stream_t, dy_t = tokens[0].T, cotangent[0].T
     gain_tile = jnp.pad(norm_gains.astype(F32), ((0, 6), (0, 8)))
-    qo_all, kv_all, gain_all, dy_all = gather_weights(
-        jnp.stack([query_weight, output_weight]), keyval_weight, gain_tile, dy_t
-    )
-    gains = gain_all[:, :2, :ROWS].transpose(1, 0, 2).reshape(2, D, 1)
-    query_full, output_full = qo_all[0].reshape(D, D), qo_all[1].reshape(D, D)
-    key_full, value_full = kv_all[0].reshape(D, KW), kv_all[1].reshape(D, KW)
-
     positions = (ctx * TOK + jnp.arange(TOK, dtype=jnp.int32)).astype(F32)
     counter = jnp.arange(HALF, dtype=F32)
     frequency = 1.0 / rotary_base ** (counter * (2.0 / HEAD_WIDTH))
     angles = frequency[:, None] * positions[None, :]
     cosine, sine = jnp.cos(angles), jnp.sin(angles)
 
-    query_low, attended_t, level, keys, one_t, middle_t, two_all, gu_all, dn_all = forward(
-        stream_t, query_full, key_full, value_full, output_full, gains, cosine, sine, gateup_weight, down_weight
+    (
+        query_low, attended_t, level, keys, one_t, middle_t, two_all, dy_all, gains,
+        query_all, output_all, key_all, value_all, gate_all, up_all, dn_all,
+    ) = forward(
+        stream_t, cosine, sine, jnp.stack([query_weight, output_weight]), keyval_weight, gain_tile, dy_t,
+        gateup_weight, down_weight,
     )
-    gate_full, up_full = gu_all[0].reshape(D, FH), gu_all[1].reshape(D, FH)
+    query_full, output_full = query_all.reshape(D, D), output_all.reshape(D, D)
+    key_full, value_full = key_all.reshape(D, KW), value_all.reshape(D, KW)
+    gate_full, up_full = gate_all.reshape(D, FH), up_all.reshape(D, FH)
     down_full = dn_all.reshape(FH, D)
-    both_dy = jnp.concatenate([dy_all[0], dy_all[1]], axis=1)
-    both_two = jnp.concatenate([two_all[0], two_all[1]], axis=1)
-
-    def dg(a, b, ca, cb):
-        return lax.dot_general(a, b, (((ca,), (cb,)), ((), ())), preferred_element_type=F32)
-
-    gate = dg(gate_full, both_two, 0, 0)
-    upward = dg(up_full, both_two, 0, 0)
-    sigmoid_gate = jax.nn.sigmoid(gate)
-    hidden = (gate * sigmoid_gate * upward).astype(BF)
-    down_part = dg(down_full, hidden, 0, 0)
-    hidden_grad = dg(down_full, both_dy, 1, 0)
-    gate_grad = (hidden_grad * upward * sigmoid_gate * (1.0 + gate * (1.0 - sigmoid_gate))).astype(BF)
-    up_grad = (hidden_grad * gate * sigmoid_gate).astype(BF)
-    two_part = dg(gate_full, gate_grad, 1, 0) + dg(up_full, up_grad, 1, 0)
-    down_other, two_other = swap(5, down_part[:, TOK:], two_part[:, TOK:])
-    result_t = (middle_t + down_part[:, :TOK] + down_other).astype(BF)
-    two_grad = two_part[:, :TOK] + two_other
-    incoming = dy_t.astype(F32)
-    middle_norm_grad, gain_two_grad = norm_backward(middle_t, gains[1], two_grad)
-    middle_grad = incoming + middle_norm_grad
-    middle_low = middle_grad.astype(BF)
-    attended_grad_t = dg(output_full, middle_low, 1, 0).astype(BF)
-    query_back, keyval_back, gate_part, up_part, down_sum = backward(
-        query_low, keys, level, attended_t, attended_grad_t, cosine, sine,
-        both_two, gate_grad, up_grad, hidden, both_dy,
+
+    (
+        query_back, keyval_back, gate_part, up_part, down_sum, result_t, middle_grad, middle_low, gain_two_grad,
+    ) = backward(
+        query_low, keys, level, attended_t, cosine, sine, two_all, dy_all, middle_t, gains,
+        gate_full, up_full, down_full, output_full,
     )
-    key_back, value_back = keyval_back[:KW], keyval_back[KW:]
-
-    one_grad = dg(query_full, query_back, 1, 0) + dg(key_full, key_back, 1, 0) + dg(value_full, value_back, 1, 0)
-    stream_norm_grad, gain_one_grad = norm_backward(stream_t.astype(F32), gains[0], one_grad)
-    input_grad = middle_grad + stream_norm_grad
-    grad_gains = jnp.stack([gain_one_grad, gain_two_grad]).reshape(2, 8, ROWS).transpose(1, 0, 2)
-    gain_rows = jnp.pad(grad_gains, ((0, 0), (0, 6), (0, 256 - ROWS)))
-    low, high, narrow, gate_sum, up_sum, down = finish(
-        one_t, attended_t, middle_low, query_back, keyval_back, gain_rows, gate_part, up_part, down_sum
+    low, high, narrow, gate_sum, up_sum, down, input_grad = finish(
+        one_t, attended_t, middle_low, query_back, keyval_back, gate_part, up_part, down_sum,
+        stream_t, middle_grad, gains, gain_two_grad, query_full, key_full, value_full,
     )
-    wide = jnp.concatenate([low, high], axis=2)
-    gains_sum = low[0, ROWS : ROWS + 2, :ROWS].astype(F32) + low[1, ROWS : ROWS + 2, :ROWS].astype(F32)
-    summed_rows = (
-        wide[0, :ROWS].astype(F32),
-        narrow[:, :ROWS].astype(F32),
-        wide[1, :ROWS].astype(F32),
-        jnp.stack([gate_sum[:ROWS], up_sum[:ROWS]]).astype(F32),
-        down.astype(F32),
-        gains_sum,
+    turned = lambda a: a.transpose(0, 2, 1)
+    state = (
+        query_weight, query_first, query_second,
+        turned(keyval_weight), turned(keyval_first), turned(keyval_second),
+        output_weight, output_first, output_second,
+        gateup_weight, gateup_first, gateup_second,
+        down_weight, down_first, down_second,
+        norm_gains, gains_first, gains_second,
     )
-    shards = (query_weight, keyval_weight, output_weight, gateup_weight, down_weight, norm_gains)
-    firsts = (query_first, keyval_first, output_first, gateup_first, down_first, gains_first)
-    seconds = (query_second, keyval_second, output_second, gateup_second, down_second, gains_second)
-    rates = (matrix_rate,) * 5 + (gain_rate,)
-    decays = (matrix_decay,) * 5 + (0.0,)
-    updated = [
-        adamw_update(shards[i], summed_rows[i], firsts[i], seconds[i], rates[i], decays[i])
-        for i in range(6)
-    ]
-    return (
-        result_t.T[None],
-        input_grad.T[None],
-        *[updated[i][0] for i in range(6)],
-        *[updated[i][1] for i in range(6)],
-        *[updated[i][2] for i in range(6)],
-    )
+    new = list(update_all(low, high, narrow, gate_sum, up_sum, down, state))
+    new[3:6] = [turned(a) for a in new[3:6]]
+    return (result_t.T[None], input_grad.T[None], *new[0::3], *new[1::3], *new[2::3])
 
 
 def solution(mesh):

time: 297 us -> 242 us (0.81)
  local copies, waits for them, and re-layouts: 29.5 us -> 9.65 us
  other arithmetic: 23.3 us -> 3.98 us
  matrix products: 14.6 us -> 0 us
    dot_general x10 -> x0, matrix products: 14.6 us -> none  [dg(): lax.dot_general(a, b, (((ca,), (cb,)), ((), ())), preferred_element_type=...]
    pallas_call x3 -> x2, Pallas kernels: 104 us -> 91.5 us  [the longest x1 81.9 us: forward(): pl.pallas_call(forward_kernel, name='forward', out_shape=(low(D, TOK), lo...]
    slice x6 -> x0, local copies, waits for them, and re-layouts: 11.2 us -> none  [the longest x1 4.67 us: body(): query_full, output_full = (qo_all[0].reshape(D, D), qo_all[1].reshape(D, D))]
    sub x4 -> x0, other arithmetic: 10.7 us -> none  [adamw_update(): weight - rate * (first_hat / (jnp.sqrt(second_hat) + adam_epsilon) + deca...]
    pallas_call x1, Pallas kernels: 66.3 us -> 75.5 us  [backward(): pl.pallas_call(backward_kernel, name='backward', out_shape=(jax.ShapeDtyp...]
    unnamed x103 -> x55, local copies, waits for them, and re-layouts: 10.3 us -> 9.65 us
where the time goes in v3:
time: 242 us
  Pallas kernels  227 us (94%)
  local copies, waits for them, and re-layouts  9.65 us (4%)
  other arithmetic  3.98 us (2%)
    pallas_call x1, Pallas kernels, forward(): pl.pallas_call(forward_kernel, name='forward', out_shape=(low(D, TOK), lo...  81.9 us
    pallas_call x1, Pallas kernels, backward(): pl.pallas_call(backward_kernel, name='backward', out_shape=(jax.ShapeDtyp...  75.5 us
    pallas_call x1, Pallas kernels, finish(): pl.pallas_call(finish_kernel, name='finish', out_shape=(jax.ShapeDtypeStr...  59.9 us
    unnamed x55, local copies, waits for them, and re-layouts  9.65 us
    pallas_call x1, Pallas kernels, update_all(): pl.pallas_call(update_kernel, name='update', grid=(steps,), out_shape=tup...  9.58 us

profile of v3, /device:TPU:1, one launch (start us, length us, event | category | flops | bytes accessed | tf_op | source)
XLA Modules:
  0.0 241.5 jit_solution(9544583173437287851)
XLA Ops:
  0.7 1.3 pad_convert_fusion.gain
  1.9 0.8 multiply_sine_fusion
  2.8 1.7 copy.40.kv
  4.5 1.9 pad_maximum_fusion.qo
  6.4 81.9 %forward.1 = (bf16[960,256]{1,0:T(8,128)(2,1)}, bf16[960,256]{1,0:T(8,128)(2,1)}, f32[16,1,256]{2,1,0:T(1,128)}, bf16[4,640,256]{2,1,0:T(8,128)(2,1)}, bf16[960,...) custom-call(bf16[960,256]{1,0:T(8,128)(2,1)} %bitcast.36, ...), custom_call_target="tpu_custom_call" | custom-call | tf_op jit(solution)/shard_map/forward/pallas_call | solution.py:370
  88.3 75.5 %backward.1 = (bf16[960,256]{1,0:T(8,128)(2,1)}, bf16[640,256]{1,0:T(8,128)(2,1)}, bf16[2,4,32,1280]{3,2,1,0:T(8,128)(2,1)}, bf16[4,32,1280]{2,1,0:T(8,128)(2,1)...) custom-call(bf16[960,256]{1,0:T(8,128)(2,1)} %get-tuple-element.70.q, ...), custom_call_target="tpu_custom_call" | custom-call | tf_op jit(solution)/shard_map/backward/pallas_call | solution.py:658
  163.8 0.0 copy-start.1
  163.8 0.0 copy-start.2
  163.9 0.0 copy-start.4
  163.9 0.0 copy-start.5
  163.9 0.0 copy-start.11
  163.9 0.0 copy-start.14
  164.0 0.0 copy-start.17
  164.0 0.0 copy-start.19
  164.0 59.9 %finish.1 = (bf16[2,128,512]{2,1,0:T(8,128)(2,1)}, bf16[2,128,448]{2,1,0:T(8,128)(2,1)}, bf16[2,128,320]{2,1,0:T(8,128)(2,1)}, bf16[128,2560]{1,0:T(8,128)(2,1)}...) custom-call(bf16[960,256]{1,0:T(8,128)(2,1)} %get-tuple-element.83.one, ...), custom_call_target="tpu_custom_call" | custom-call | tf_op jit(solution)/shard_map/finish/pallas_call | solution.py:1000
  224.1 1.1 copy-done.8
  225.2 1.1 copy-done.9
  226.3 1.1 copy-done.10
  227.4 0.9 copy-done.12
  228.3 0.9 copy-done.13
  229.3 0.9 copy-done.18
  230.2 9.6 %update.1 = (f32[120,960]{1,0:T(8,128)}, f32[120,960]{1,0:T(8,128)}, f32[120,960]{1,0:T(8,128)}, f32[2,320,120]{2,1,0:T(8,128)}, f32[2,320,120]{2,1,0:T(8,128)},...) custom-call(bf16[2,128,512]{2,1,0:T(8,128)(2,1)S(1)} %copy-done.12, ...), custom_call_target="tpu_custom_call" | custom-call | tf_op jit(solution)/shard_map/update/pallas_call | solution.py:1077
  239.8 0.8 copy.43
  240.6 0.9 copy.44
  (40 shorter events, 0.1 us)
Async XLA Ops:
  163.8 60.1 %copy-start = (bf16[2,120,2560]{2,1,0:T(8,128)(2,1)S(1)}, bf16[2,120,2560]{2,1,0:T(8,128)(2,1)}, u32[]{:S(2)}) copy-start(bf16[2,120,2560]{2,1,0:T(8,128)(2,1)} %refs_9_.1) | copy-start | bytes 3686404
  163.8 60.1 %copy-start.1 = (bf16[320,960]{1,0:T(8,128)(2,1)S(1)}, bf16[320,960]{1,0:T(8,128)(2,1)}, u32[]{:S(2)}) copy-start(bf16[320,960]{1,0:T(8,128)(2,1)} %refs_12_.1) | copy-start | bytes 1843204
  163.8 60.1 %copy-start.2 = (bf16[2,120,2560]{2,1,0:T(8,128)(2,1)S(1)}, bf16[2,120,2560]{2,1,0:T(8,128)(2,1)}, u32[]{:S(2)}) copy-start(bf16[2,120,2560]{2,1,0:T(8,128)(2,1)} %refs_10_.1) | copy-start | bytes 3686404
  163.9 60.1 %copy-start.3 = (bf16[2,120,2560]{2,1,0:T(8,128)(2,1)S(1)}, bf16[2,120,2560]{2,1,0:T(8,128)(2,1)}, u32[]{:S(2)}) copy-start(bf16[2,120,2560]{2,1,0:T(8,128)(2,1)} %refs_11_.1) | copy-start | bytes 3686404
  163.9 60.1 %copy-start.4 = (bf16[120,960]{1,0:T(8,128)(2,1)S(1)}, bf16[120,960]{1,0:T(8,128)(2,1)}, u32[]{:S(2)}) copy-start(bf16[120,960]{1,0:T(8,128)(2,1)} %refs_6_.1) | copy-start | bytes 691204
  163.9 60.1 %copy-start.5 = (bf16[120,960]{1,0:T(8,128)(2,1)S(1)}, bf16[120,960]{1,0:T(8,128)(2,1)}, u32[]{:S(2)}) copy-start(bf16[120,960]{1,0:T(8,128)(2,1)} %refs_0_.1) | copy-start | bytes 691204
  163.9 60.1 %copy-start.6 = (bf16[320,960]{1,0:T(8,128)(2,1)S(1)}, bf16[320,960]{1,0:T(8,128)(2,1)}, u32[]{:S(2)}) copy-start(bf16[320,960]{1,0:T(8,128)(2,1)} %refs_13_.1) | copy-start | bytes 1843204
  163.9 60.1 %copy-start.7 = (bf16[320,960]{1,0:T(8,128)(2,1)S(1)}, bf16[320,960]{1,0:T(8,128)(2,1)}, u32[]{:S(2)}) copy-start(bf16[320,960]{1,0:T(8,128)(2,1)} %refs_14_.1) | copy-start | bytes 1843204
  163.9 60.1 %copy-start.11 = (bf16[2,120,320]{1,2,0:T(8,128)(2,1)S(1)}, bf16[2,120,320]{1,2,0:T(8,128)(2,1)}, u32[]{:S(2)}) copy-start(bf16[2,120,320]{1,2,0:T(8,128)(2,1)} %param.23) | copy-start | bytes 460804
  163.9 60.1 %copy-start.14 = (bf16[120,960]{1,0:T(8,128)(2,1)S(1)}, bf16[120,960]{1,0:T(8,128)(2,1)}, u32[]{:S(2)}) copy-start(bf16[120,960]{1,0:T(8,128)(2,1)} %refs_1_.1) | copy-start | bytes 691204
  163.9 60.1 %copy-start.15 = (bf16[120,960]{1,0:T(8,128)(2,1)S(1)}, bf16[120,960]{1,0:T(8,128)(2,1)}, u32[]{:S(2)}) copy-start(bf16[120,960]{1,0:T(8,128)(2,1)} %refs_2_.1) | copy-start | bytes 691204
  164.0 60.1 %copy-start.16 = (bf16[120,960]{1,0:T(8,128)(2,1)S(1)}, bf16[120,960]{1,0:T(8,128)(2,1)}, u32[]{:S(2)}) copy-start(bf16[120,960]{1,0:T(8,128)(2,1)} %refs_7_.1) | copy-start | bytes 691204
  164.0 60.1 %copy-start.17 = (bf16[120,960]{1,0:T(8,128)(2,1)S(1)}, bf16[120,960]{1,0:T(8,128)(2,1)}, u32[]{:S(2)}) copy-start(bf16[120,960]{1,0:T(8,128)(2,1)} %refs_8_.1) | copy-start | bytes 691204
  164.0 60.1 %copy-start.19 = (bf16[2,120,320]{1,2,0:T(8,128)(2,1)S(1)}, bf16[2,120,320]{1,2,0:T(8,128)(2,1)}, u32[]{:S(2)}) copy-start(bf16[2,120,320]{1,2,0:T(8,128)(2,1)} %param.29) | copy-start | bytes 460804
  164.0 60.1 %copy-start.20 = (bf16[2,120,320]{1,2,0:T(8,128)(2,1)S(1)}, bf16[2,120,320]{1,2,0:T(8,128)(2,1)}, u32[]{:S(2)}) copy-start(bf16[2,120,320]{1,2,0:T(8,128)(2,1)} %param.35) | copy-start | bytes 460804
  164.0 60.1 %copy-start.21 = (bf16[2,120]{1,0:T(2,128)(2,1)S(1)}, bf16[2,120]{1,0:T(2,128)(2,1)}, u32[]{:S(2)}) copy-start(bf16[2,120]{1,0:T(2,128)(2,1)} %refs_15_.1) | copy-start | bytes 1444
  164.0 60.1 %copy-start.22 = (bf16[2,120]{1,0:T(2,128)(2,1)S(1)}, bf16[2,120]{1,0:T(2,128)(2,1)}, u32[]{:S(2)}) copy-start(bf16[2,120]{1,0:T(2,128)(2,1)} %refs_16_.1) | copy-start | bytes 1444
  164.0 60.1 %copy-start.23 = (bf16[2,120]{1,0:T(2,128)(2,1)S(1)}, bf16[2,120]{1,0:T(2,128)(2,1)}, u32[]{:S(2)}) copy-start(bf16[2,120]{1,0:T(2,128)(2,1)} %refs_17_.1) | copy-start | bytes 1444
  224.1 1.1 copy-start.8
  225.2 1.1 copy-start.9
  226.3 1.1 copy-start.10
  227.4 0.9 copy-start.12
  230.2 9.6 %copy-start.25 = (bf16[960,256]{1,0:T(8,128)(2,1)S(1)}, bf16[960,256]{1,0:T(8,128)(2,1)}, u32[]{:S(2)}) copy-start(bf16[960,256]{1,0:T(8,128)(2,1)} %get-tuple-element.82) | copy-start | bytes 1474564
  230.2 10.4 %copy-start.24 = (f32[960,256]{1,0:T(8,128)S(1)}, f32[960,256]{1,0:T(8,128)}, u32[]{:S(2)}) copy-start(f32[960,256]{1,0:T(8,128)} %get-tuple-element.95) | copy-start | bytes 2949124
  (2 other events, 1.9 us)

commit v4 on v3

--- a/solution.py
+++ b/solution.py
@@ -82,7 +82,7 @@
 
 
 def forward_kernel(
-    stream, cos, sin, qo, kv, gain, dy, gu, dn,
+    stream, cos, sin, qw, ow, kv, gain, dy, gu, dn,
     q_low, att, lse, kv_out, one, mid, two_all, dy_all, gains_out, q_all, o_all, k_all, v_all, gate_all, up_all, dn_all,
     keys, wide, ones, two, qo_land, kv_land, gain_land,
     send, recv, send_y, send_x, recv_w, send_ay, send_ax, send_as, recv_a, recv_as, local,
@@ -99,7 +99,15 @@
     def column(k):
         return 4 * xl + lax.rem(y + k + 1, 4) if k < 3 else 4 * (1 - xl) + lax.rem(y + k - 3, 4)
 
-    own_a = (qo.at[c], kv.at[c], gain)
+    def own_a(item):
+        return (None, kv.at[c], gain)[item]
+
+    def by_core(item, make):
+        if item:
+            make(own_a(item))
+        else:
+            pl.when(c == 0)(lambda: make(qw))
+            pl.when(c == 1)(lambda: make(ow))
 
     def slot_a(item, g, core):
         if item == 2:
@@ -110,13 +118,14 @@
         ref = slot_a(item, column(k), c)
         remote(ref, ref, send_as.at[0, 0], recv_a.at[item, column(k)], sibling).wait_recv()
 
-    def row_a(item, j):
-        return remote(own_a[item], slot_a(item, f, c), send_ay.at[item, j - 1], recv_a.at[item, f], at(x, y + j, z, c))
-
-    def side_a(item, j):
+    def row_a(item, j, source=None):
+        source = slot_a(item, f, c) if source is None else source
+        return remote(source, slot_a(item, f, c), send_ay.at[item, j - 1], recv_a.at[item, f], at(x, y + j, z, c))
+
+    def side_a(item, j, source=None):
         g = 4 * xl + lax.rem(y + j, 4)
         return remote(
-            own_a[item] if j == 0 else slot_a(item, g, c),
+            slot_a(item, g, c) if source is None else source,
             slot_a(item, g, c),
             send_ax.at[item, j],
             recv_a.at[item, g],
@@ -173,13 +182,18 @@
         pl.when(holds)(lambda: pass_on((2, 3), offsets))
 
     for item in (2, 1, 0):
-        side_a(item, 0).start()
-        for j in ORDER:
-            row_a(item, j).start()
+
+        def launch(source, item=item):
+            side_a(item, 0, source).start()
+            for j in ORDER:
+                row_a(item, j, source).start()
+
+        by_core(item, launch)
     copies = [
         pltpu.make_async_copy(gain, gain_land.at[f], local.at[0]),
         pltpu.make_async_copy(kv, kv_land.at[:, f], local.at[1]),
-        pltpu.make_async_copy(qo, qo_land.at[:, f], local.at[2]),
+        pltpu.make_async_copy(qw, qo_land.at[0, f], local.at[2]),
+        pltpu.make_async_copy(ow, qo_land.at[1, f], local.at[9]),
         pltpu.make_async_copy(own[0], gate_all.at[f], local.at[3]),
         pltpu.make_async_copy(own[1], up_all.at[f], local.at[8]),
         pltpu.make_async_copy(dy, dy_all.at[0], local.at[4]),
@@ -217,7 +231,7 @@
         take(1, k)
     take(0, 1)
 
-    for copy in copies[:3]:
+    for copy in copies[:4]:
         copy.wait()
     for g in range(8):
         tile = gain_land[g].T
@@ -333,7 +347,7 @@
             for item in (2, 3):
                 wait_slot(item, g)
 
-    for copy in copies[3:] + keep_a + [keep]:
+    for copy in copies[4:] + keep_a + [keep]:
         copy.wait()
     trade.wait()
     exchange.wait()
@@ -388,7 +402,7 @@
             low(8, ROWS, FH),
             low(4, KW, D),
         ),
-        in_specs=[VM] * 3 + [ANY] * 6,
+        in_specs=[VM] * 3 + [ANY] * 7,
         out_specs=(VM,) * 6 + (ANY,) * 2 + (VM,) + (ANY,) * 7,
         scratch_shapes=[
             pltpu.VMEM((4, 2 * KW, TOK), BF),
@@ -408,7 +422,7 @@
             sem((2, 7)),
             sem((3, 8)),
             sem((2, 8)),
-            sem((9,)),
+            sem((10,)),
         ],
         compiler_params=params(1),
     )(*args)
@@ -441,10 +455,10 @@
 
 def backward_kernel(
     q_low, keys, lse, att, cos, sin, two_all, dy_all, mid, gains, wg, wu, wd, wo,
-    q_back, kv_back, c0_out, c1_out, d_out, result, mid_grad, mid_low, gain_grad,
+    q_back, kv_back, c0_out, c1_out, c1y_out, d_out, result, mid_grad, mid_low, gain_grad,
     two, dy, gate_grad, up_grad, hidden, grad, down_part, down_got, two_part, two_got, send_s, recv_s,
-    mine, got, far_got, acc, c0, c0r, c1, c1r, c1s, c1t, d, dr, ds_, dt,
-    send, recv, send_z, recv_z, send_x, recv_x, send_t, recv_t, send_y, recv_y, send_d, recv_d,
+    mine, got, far_got, acc, c0, c0r, c1, c1r, c1s, c1t, c1u, d, dr, ds_, dt,
+    send, recv, send_z, recv_z, send_x, recv_x, send_t, recv_t, send_u, recv_u, send_y, recv_y, send_d, recv_d,
 ):
     x, y, z, c = place()
     xl = lax.rem(x, 2)
@@ -457,57 +471,63 @@
     along_x, along_y, along_z = ring(x, y, z, c)
     greet(along_x + along_y + along_z + [sibling])
     co, si = cos[...], sin[...]
-    nothing = [jnp.zeros((8, 256), F32)] * 8
-
-    def c0_z(j):
-        return remote(c0.at[:, :, quarter(z + j, 32)], c0r.at[j - 1], send_z.at[j - 1], recv_z.at[j - 1], along_z[j - 1])
+    nothing = {size: [jnp.zeros((8, size), F32)] * 8 for size in (128, 256)}
+
+    halves = (slice(0, 640), slice(640, FH))
+
+    def c0_z(i, j):
+        return remote(
+            c0.at[i, :, :, quarter(z + j, 32)], c0r.at[j - 1, i], send_z.at[i, j - 1], recv_z.at[i, j - 1], along_z[j - 1]
+        )
 
     def c1_x(i):
-        return remote(
-            c1.at[1 - xl, :, :, 640 * i : 640 * (i + 1)], c1r.at[i], send_x.at[i], recv_x.at[i], along_x[2 * i]
-        )
+        return remote(c1.at[i, 1 - xl], c1r.at[i], send_x.at[i], recv_x.at[i], along_x[2 * i])
 
     def c1_z(j):
-        return remote(c1s.at[:, quarter(z + j, 32)], c1t.at[j - 1], send_t.at[j - 1], recv_t.at[j - 1], along_z[j - 1])
+        return remote(c1s.at[0, :, quarter(z + j, 32)], c1t.at[j - 1], send_t.at[j - 1], recv_t.at[j - 1], along_z[j - 1])
+
+    def c1_y(j):
+        return remote(c1s.at[1, lax.rem(y + j, 4)], c1u.at[j - 1], send_u.at[j - 1], recv_u.at[j - 1], along_y[j - 1])
 
     def d_y(j):
         return remote(d.at[lax.rem(y + j, 4)], dr.at[j - 1], send_y.at[j - 1], recv_y.at[j - 1], along_y[j - 1])
 
-    def d_x(j):
-        return remote(ds_, dt.at[j - 1], send_d.at[j - 1], recv_d.at[j - 1], along_x[j - 1])
+    def d_block(k):
+        for j in (1, 2, 3):
+            pl.when(lax.rem(y + j, 4) == k)(lambda j=j: d_y(j).start())
+
+    def d_x(i):
+        return remote(ds_.at[160 * i : 160 * (i + 1)], dt.at[i], send_d.at[i], recv_d.at[i], along_x[2 * i])
 
     for i in (0, 1):
         two[:, TOK * i : TOK * (i + 1)] = two_all[i]
         dy[:, TOK * i : TOK * (i + 1)] = dy_all[i]
-    for start, stop in columns(FH):
-        gate = dot(wg[:, start:stop], two[...], 0, 0)
-        up = dot(wu[:, start:stop], two[...], 0, 0)
-        back = dot(wd[start:stop, :], dy[...], 1, 0)
-        sigmoid = jax.nn.sigmoid(gate)
-        silu = gate * sigmoid
-        hidden[start:stop, :] = (silu * up).astype(BF)
-        gate_grad[start:stop, :] = (back * up * sigmoid * (1.0 + gate * (1.0 - sigmoid))).astype(BF)
-        up_grad[start:stop, :] = (back * silu).astype(BF)
-
-    for start, stop in columns(FH):
-        part = planes(dot(two[...], gate_grad[start:stop, :], 1, 1), nothing)
-        for f in range(8):
-            c0[f // 4, f % 4, :, start:stop] = part[f]
-    for j in ORDER:
-        c0_z(j).start()
-    for start, stop in columns(D):
-        part = dot(hidden[...], dy[start:stop, :], 1, 1).astype(BF)
-        for k in range(4):
-            d[k, :, start:stop] = part[KW * k : KW * (k + 1)]
-    for j in ORDER:
-        d_y(j).start()
-    for start, stop in columns(FH):
-        part = planes(dot(two[...], up_grad[start:stop, :], 1, 1), nothing)
-        for f in range(8):
-            c1[f // 4, f % 4, :, start:stop] = part[f]
-    for i in (0, 1):
-        c1_x(i).start()
-
+    for i, half in enumerate(halves):
+        for start, stop in ((half.start, half.start + 256), (half.start + 256, half.start + 512), (half.start + 512, half.stop)):
+            gate = dot(wg[:, start:stop], two[...], 0, 0)
+            up = dot(wu[:, start:stop], two[...], 0, 0)
+            back = dot(wd[start:stop, :], dy[...], 1, 0)
+            sigmoid = jax.nn.sigmoid(gate)
+            silu = gate * sigmoid
+            hidden[start:stop, :] = (silu * up).astype(BF)
+            gate_grad[start:stop, :] = (back * up * sigmoid * (1.0 + gate * (1.0 - sigmoid))).astype(BF)
+            up_grad[start:stop, :] = (back * silu).astype(BF)
+        for start, stop in columns(D):
+            part = dot(hidden[half, :], dy[start:stop, :], 1, 1).astype(BF)
+            d[2 * i, :, start:stop] = part[:KW]
+            d[2 * i + 1, :, start:stop] = part[KW:]
+        d_block(2 * i)
+        d_block(2 * i + 1)
+        for source, into in ((gate_grad, c0), (up_grad, c1)):
+            for start, stop in ((0, 256), (256, 512), (512, 640)):
+                part = planes(dot(two[...], source[half.start + start : half.start + stop, :], 1, 1), nothing[stop - start])
+                for f in range(8):
+                    into[i, f // 4, f % 4, :, start:stop] = part[f]
+            if into is c0:
+                for j in ORDER:
+                    c0_z(i, j).start()
+            else:
+                c1_x(i).start()
     far_half = pl.ds(TOK, TOK)
     for start, stop in columns(D):
         two_part[start:stop, :] = dot(wg[start:stop, :], gate_grad[...], 1, 0) + dot(wu[start:stop, :], up_grad[...], 1, 0)
@@ -535,23 +555,20 @@
     def step_c1():
         for i in (0, 1):
             c1_x(i).wait_recv()
-        for k in range(4):
-            for i in (0, 1):
-                lanes = slice(640 * i, 640 * (i + 1))
-                c1s[k, :, lanes] = (c1[xl, k, :, lanes].astype(F32) + c1r[i, k].astype(F32)).astype(BF)
-        for j in ORDER:
-            c1_z(j).start()
+            for k in range(4):
+                c1s[i, k] = (c1[i, xl, k].astype(F32) + c1r[i, k].astype(F32)).astype(BF)
+            for j in ORDER:
+                (c1_z, c1_y)[i](j).start()
 
     def step_d():
         for j in (1, 2, 3):
             d_y(j).wait_recv()
         ds_[...] = summed(d[y], dr)
-        pl.when(holds)(lambda: d_x(2).start())
 
         @pl.when(jnp.logical_not(holds))
         def _():
+            d_x(0).start()
             d_x(1).start()
-            d_x(3).start()
 
     gap = lax.broadcasted_iota(jnp.int32, (TOK, TOK), 0) - lax.broadcasted_iota(jnp.int32, (TOK, TOK), 1)
 
@@ -607,9 +624,10 @@
 
     @pl.when(holds)
     def _():
-        for j in (1, 2, 3):
-            d_x(j).wait_recv()
-        d_out[...] = summed(ds_[...], dt)
+        for i in (0, 1):
+            d_x(i).wait_recv()
+            rows = slice(160 * i, 160 * (i + 1))
+            d_out[rows, :] = (ds_[rows, :].astype(F32) + dt[i].astype(F32)).astype(BF)
 
     @pl.when(jnp.logical_not(holds))
     def _():
@@ -623,15 +641,19 @@
         kv_back[64 * h : 64 * h + 32, :] = (a * co + b * si).astype(BF)
         kv_back[64 * h + 32 : 64 * h + 64, :] = (b * co - a * si).astype(BF)
     kv_back[KW:, :] = total[KW:, :].astype(BF)
-    for j in (1, 2, 3):
-        c0_z(j).wait_recv()
-    for i in (0, 1):
-        for k in range(4):
-            c0_out[i, k] = summed(c0[i, k, quarter(z, 32)], [c0r[j, i, k] for j in range(3)])
+    for i, half in enumerate(halves):
+        for j in (1, 2, 3):
+            c0_z(i, j).wait_recv()
+        for m in range(2):
+            for k in range(4):
+                c0_out[m, k, :, half] = summed(c0[i, m, k, quarter(z, 32)], [c0r[j, i, m, k] for j in range(3)])
     for j in (1, 2, 3):
         c1_z(j).wait_recv()
     for k in range(4):
-        c1_out[k] = summed(c1s[k, quarter(z, 32)], [c1t[j, k] for j in range(3)])
+        c1_out[k] = summed(c1s[0, k, quarter(z, 32)], [c1t[j, k] for j in range(3)])
+    for j in (1, 2, 3):
+        c1_y(j).wait_recv()
+    c1y_out[...] = summed(c1s[1, y], c1u)
 
     trade_two.wait_send()
     trade_down.wait_send()
@@ -639,17 +661,18 @@
     to_sib.wait_send()
     to_far.wait_send()
     for j in (1, 2, 3):
-        c0_z(j).wait_send()
+        c0_z(0, j).wait_send()
+        c0_z(1, j).wait_send()
         c1_z(j).wait_send()
+        c1_y(j).wait_send()
         d_y(j).wait_send()
     for i in (0, 1):
         c1_x(i).wait_send()
-    pl.when(holds)(lambda: d_x(2).wait_send())
 
     @pl.when(jnp.logical_not(holds))
     def _():
+        d_x(0).wait_send()
         d_x(1).wait_send()
-        d_x(3).wait_send()
 
 
 def backward(*args):
@@ -662,7 +685,8 @@
             jax.ShapeDtypeStruct((D, TOK), BF),
             jax.ShapeDtypeStruct((2 * KW, TOK), BF),
             jax.ShapeDtypeStruct((2, 4, 32, FH), BF),
-            jax.ShapeDtypeStruct((4, 32, FH), BF),
+            jax.ShapeDtypeStruct((4, 32, 640), BF),
+            jax.ShapeDtypeStruct((PAD, 640), BF),
             jax.ShapeDtypeStruct((KW, D), BF),
             jax.ShapeDtypeStruct((D, TOK), BF),
             jax.ShapeDtypeStruct((D, TOK), F32),
@@ -670,21 +694,22 @@
             jax.ShapeDtypeStruct((D, 1), F32),
         ),
         in_specs=[VM] * 14,
-        out_specs=(VM,) * 9,
+        out_specs=(VM,) * 10,
         scratch_shapes=[
             vm(D, 2 * TOK), vm(D, 2 * TOK), vm(FH, 2 * TOK), vm(FH, 2 * TOK), vm(FH, 2 * TOK), vm(D, TOK),
             pltpu.VMEM((D, 2 * TOK), F32), pltpu.VMEM((D, TOK), F32),
             pltpu.VMEM((D, 2 * TOK), F32), pltpu.VMEM((D, TOK), F32),
             sem((2,)), sem((2,)),
             vm(4, 2 * KW, TOK), vm(2, 2 * KW, TOK), vm(2 * KW, TOK), pltpu.VMEM((4, 2, 64, TOK), F32),
-            vm(2, 4, PAD, FH), vm(3, 2, 4, 32, FH),
-            vm(2, 4, PAD, FH), vm(2, 4, PAD, 640), vm(4, PAD, FH), vm(3, 4, 32, FH),
-            vm(4, KW, D), vm(3, KW, D), vm(KW, D), vm(3, KW, D),
+            vm(2, 2, 4, PAD, 640), vm(3, 2, 2, 4, 32, 640),
+            vm(2, 2, 4, PAD, 640), vm(2, 4, PAD, 640), vm(2, 4, PAD, 640), vm(3, 4, 32, 640), vm(3, PAD, 640),
+            vm(4, KW, D), vm(3, KW, D), vm(KW, D), vm(2, 160, D),
         ]
-        + [sem((3,))] * 4
+        + [sem((3,))] * 2
+        + [sem((2, 3))] * 2
         + [sem((2,))] * 2
-        + [sem((3,))] * 6,
-        compiler_params=params(2),
+        + [sem((3,))] * 8,
+        compiler_params=params(2, 61),
     )(*args)
 
 
@@ -692,7 +717,7 @@
 
 
 def finish_kernel(
-    one, att, mid, q_back, kv_back, c0, c1, dd, stream, mid_grad, gains, gain_two, wq, wk, wv,
+    one, att, mid, q_back, kv_back, c0, c1, c1y, dd, stream, mid_grad, gains, gain_two, wq, wk, wv,
     lo_sum, hi_sum, kv_sum, c0_sum, c1_sum, d_sum, in_grad,
     gain_cols,
     left, right, thin, both, lo, hi, kv,
@@ -700,8 +725,8 @@
     kv1, kv1r, kv2, kv2r, kv3, kv3r,
     hi1, hi1r, hi2, hi2r, hi3, hi3r,
     c02r, c02, c03r, c03,
-    c1r, c1s, c1t, c1u,
-    dr, ds_,
+    c1r, c1zr, c1s, c1t, c1u,
+    dr, dh, dx, ds_,
     send, recv, send_s, recv_s, send_g, recv_g, send_o, recv_o, local,
 ):
     x, y, z, c = place()
@@ -729,35 +754,39 @@
         return remote(src, dst.at[j - 1], send.at[item, phase, j - 1], recv.at[item, phase, j - 1], along[j - 1])
 
     def y1(item, j):
-        src, dst = {LO: (lo, lo1r), KV: (kv, kv1r)}[item]
-        return move(item, 0, j, src.at[:, lax.rem(y + j, 4)], dst, along_y)
+        return move(item, 0, j, lo.at[:, lax.rem(y + j, 4)], lo1r, along_y)
 
     def x2(item, j):
-        src, dst = {LO: (lo1, lo2r), KV: (kv1, kv2r)}[item]
-        return move(item, 1, j, src.at[xl if j == 2 else 1 - xl], dst, along_x)
+        return move(item, 1, j, lo1.at[xl if j == 2 else 1 - xl], lo2r, along_x)
 
     def z3(item, j):
         if item == DN:
             return move(item, 2, j, dd.at[quarter(z + j, 80)], dr, along_z)
-        src, dst = {LO: (lo2, lo3r), KV: (kv2, kv3r)}[item]
-        return move(item, 2, j, src.at[quarter(z + j, 32)], dst, along_z)
-
-    def z1(j):
-        return move(HI, 0, j, hi.at[:, :, quarter(z + j, 32)], hi1r, along_z)
+        return move(item, 2, j, lo2.at[quarter(z + j, 32)], lo3r, along_z)
+
+    def z1(item, j):
+        src, dst = {HI: (hi, hi1r), KV: (kv, kv1r)}[item]
+        return move(item, 0, j, src.at[:, :, quarter(z + j, 32)], dst, along_z)
 
     def y2(item, j):
-        src, dst = {HI: (hi1, hi2r), C0: (c0, c02r)}[item]
+        src, dst = {HI: (hi1, hi2r), KV: (kv1, kv2r), C0: (c0, c02r)}[item]
         return move(item, 1, j, src.at[:, lax.rem(y + j, 4)], dst, along_y)
 
     def x3(item, j):
-        src, dst = {HI: (hi2, hi3r), C0: (c02, c03r)}[item]
+        src, dst = {HI: (hi2, hi3r), KV: (kv2, kv3r), C0: (c02, c03r)}[item]
         return move(item, 2, j, src.at[xl if j == 2 else 1 - xl], dst, along_x)
 
     def y_up(j):
         return move(C1, 0, j, c1.at[lax.rem(y + j, 4)], c1r, along_y)
 
+    def z_up(j):
+        return move(C1, 2, j, c1y.at[quarter(z + j, 32)], c1zr, along_z)
+
     def x_up():
         return remote(c1s, c1t, send.at[C1, 1, 0], recv.at[C1, 1, 0], along_x[1])
+
+    def x_down():
+        return remote(dh, dx, send.at[DN, 1, 0], recv.at[DN, 1, 0], along_x[1])
 
     for core in (0, 1):
 
@@ -769,6 +798,7 @@
     for j in ORDER:
         y2(C0, j).start()
         y_up(j).start()
+        z_up(j).start()
 
     @pl.when(holds)
     def _():
@@ -790,6 +820,28 @@
         thin[:, near] = kv_back[KW:, :]
 
     both[:, near] = one[...]
+
+    trade(0, one, left.at[:, far]).wait_recv()
+    trade(1, one, right.at[:, far]).wait_recv()
+
+    def wide_part(start, stop, into, shift, extra):
+        part = planes(dot(left[...], right[start:stop, :], 1, 1), extra)
+        for f in range(8):
+            into[f // 4, f % 4, :, start - shift : stop - shift] = part[f]
+
+    nothing = [jnp.zeros((8, 256), F32)] * 8
+    wide_part(0, 256, lo, 0, nothing)
+    wide_part(256, 512, lo, 0, nothing)
+    for j in ORDER:
+        y1(LO, j).start()
+    trade(3, one, both.at[:, far]).wait_recv()
+    trade(2, kv_back.at[:KW], thin.at[:, far]).wait_recv()
+    part = planes(dot(both[...], thin[...], 1, 1), [jnp.zeros((8, KW), F32)] * 8)
+    for f in range(8):
+        kv[f // 4, f % 4] = part[f]
+    for j in ORDER:
+        z1(KV, j).start()
+    wide_part(768, D, hi, WIDE, [jnp.zeros((8, D - 768), F32)] * 8)
 
     source = stream[...].astype(F32)
     scale = lax.rsqrt(jnp.sum(source * source, axis=0, keepdims=True) / D + norm_epsilon)
@@ -815,30 +867,9 @@
         tile = jnp.where(lane == 0, first_col, jnp.where(lane == 1, second_col, 0.0)).T
         gain.append(jnp.concatenate([tile[:8], jnp.zeros((8, 128), F32)], axis=1))
 
-    trade(3, one, both.at[:, far]).wait_recv()
-    trade(2, kv_back.at[:KW], thin.at[:, far]).wait_recv()
-    nothing = [jnp.zeros((8, KW), F32)] * 8
-    part = planes(dot(both[...], thin[...], 1, 1), nothing)
-    for f in range(8):
-        kv[f // 4, f % 4] = part[f]
+    wide_part(512, 768, hi, WIDE, gain)
     for j in ORDER:
-        y1(KV, j).start()
-    trade(0, one, left.at[:, far]).wait_recv()
-    trade(1, one, right.at[:, far]).wait_recv()
-    for start, stop in ((256, 512), (0, 256), (512, 768), (768, D)):
-        size = stop - start
-        extra = [gain[f] if start == 0 else jnp.zeros((8, size), F32) for f in range(8)]
-        part = planes(dot(left[...], right[start:stop, :], 1, 1), extra)
-        for f in range(8):
-            if start < WIDE:
-                lo[f // 4, f % 4, :, start:stop] = part[f]
-            else:
-                hi[f // 4, f % 4, :, start - WIDE : stop - WIDE] = part[f]
-        if start == 0:
-            for j in ORDER:
-                y1(LO, j).start()
-    for j in ORDER:
-        z1(j).start()
+        z1(HI, j).start()
 
     def arrived(make, *key):
         for j in (1, 2, 3):
@@ -850,7 +881,9 @@
     for j in ORDER:
         x3(C0, j).start()
     arrived(y_up)
-    c1s[...] = summed(c1[y], c1r)
+    c1s[:, 0:640] = summed(c1[y], c1r)
+    arrived(z_up)
+    c1s[:, 640:FH] = summed(c1y[quarter(z, 32)], c1zr)
     x_up().start()
 
     part_of = {LO: lo3, HI: hi3, KV: kv3, C0: c03, C1: c1u, DN: ds_}
@@ -899,7 +932,13 @@
     @pl.when(holds)
     def _():
         arrived(z3, DN)
-        ds_[...] = summed(dd[quarter(z, 80)], dr)
+        dh[...] = summed(dd[quarter(z, 80)], dr)
+        x_down().start()
+
+    @pl.when(holds)
+    def _():
+        x_down().wait_recv()
+        ds_[...] = (dh[...].astype(F32) + dx[...].astype(F32)).astype(BF)
         publish(DN)
 
     x_up().wait_recv()
@@ -909,41 +948,34 @@
     c03[...] = summed(c02[xl], c03r)
     publish(C0)
 
-    arrived(y1, KV)
-    for i in range(2):
-        kv1[i] = summed(kv[i, y], [kv1r[j, i] for j in range(3)])
-    for j in ORDER:
-        x2(KV, j).start()
     arrived(y1, LO)
     for i in range(2):
         lo1[i] = summed(lo[i, y], [lo1r[j, i] for j in range(3)])
     for j in ORDER:
         x2(LO, j).start()
-    arrived(z1)
-    for i in range(2):
-        for k in range(4):
-            hi1[i, k] = summed(hi[i, k, quarter(z, 32)], [hi1r[j, i, k] for j in range(3)])
-    for j in ORDER:
-        y2(HI, j).start()
-    arrived(x2, KV)
-    kv2[...] = summed(kv1[xl], kv2r)
-    for j in ORDER:
-        z3(KV, j).start()
+    for item, first, out, got in ((KV, kv, kv1, kv1r), (HI, hi, hi1, hi1r)):
+        arrived(z1, item)
+        for i in range(2):
+            for k in range(4):
+                out[i, k] = summed(first[i, k, quarter(z, 32)], [got[j, i, k] for j in range(3)])
+        for j in ORDER:
+            y2(item, j).start()
     arrived(x2, LO)
     lo2[...] = summed(lo1[xl], lo2r)
     for j in ORDER:
         z3(LO, j).start()
-    arrived(y2, HI)
-    for i in range(2):
-        hi2[i] = summed(hi1[i, y], [hi2r[j, i] for j in range(3)])
-    for j in ORDER:
-        x3(HI, j).start()
-    arrived(z3, KV)
-    kv3[...] = summed(kv2[quarter(z, 32)], kv3r)
-    publish(KV)
+    for item, first, out, got in ((KV, kv1, kv2, kv2r), (HI, hi1, hi2, hi2r)):
+        arrived(y2, item)
+        for i in range(2):
+            out[i] = summed(first[i, y], [got[j, i] for j in range(3)])
+        for j in ORDER:
+            x3(item, j).start()
     arrived(z3, LO)
     lo3[...] = summed(lo2[quarter(z, 32)], lo3r)
     publish(LO)
+    arrived(x3, KV)
+    kv3[...] = summed(kv2[xl], kv3r)
+    publish(KV)
     arrived(x3, HI)
     hi3[...] = summed(hi2[xl], hi3r)
     publish(HI)
@@ -971,11 +1003,11 @@
 
     for j in (1, 2, 3):
         for make, key in (
-            (y1, LO), (x2, LO), (z3, LO), (y1, KV), (x2, KV), (z3, KV), (y2, HI), (x3, HI), (y2, C0), (x3, C0),
+            (y1, LO), (x2, LO), (z3, LO), (z1, KV), (y2, KV), (x3, KV), (z1, HI), (y2, HI), (x3, HI), (y2, C0), (x3, C0),
         ):
             make(key, j).wait_send()
-        z1(j).wait_send()
         y_up(j).wait_send()
+        z_up(j).wait_send()
     x_up().wait_send()
     for item in (LO, HI, KV, C0, C1):
         settled(item)
@@ -984,6 +1016,7 @@
     def _():
         for j in (1, 2, 3):
             z3(DN, j).wait_send()
+        x_down().wait_send()
         settled(DN)
 
 
@@ -994,6 +1027,12 @@
     def yxz(width):
         return [
             vm(2, PAD, width), vm(3, 2, PAD, width), vm(PAD, width), vm(3, PAD, width),
+            vm(32, width), vm(3, 32, width),
+        ]
+
+    def zyx(width):
+        return [
+            vm(2, 4, 32, width), vm(3, 2, 4, 32, width), vm(2, 32, width), vm(3, 2, 32, width),
             vm(32, width), vm(3, 32, width),
         ]
 
@@ -1009,7 +1048,7 @@
             jax.ShapeDtypeStruct((KW, D), BF),
             jax.ShapeDtypeStruct((D, TOK), F32),
         ),
-        in_specs=[VM] * 15,
+        in_specs=[VM] * 16,
         out_specs=(ANY,) * 6 + (VM,),
         scratch_shapes=[
             pltpu.VMEM((D, 1), F32),
@@ -1017,14 +1056,11 @@
             vm(2, 4, PAD, WIDE), vm(2, 4, PAD, NARROW), vm(2, 4, PAD, KW),
         ]
         + yxz(WIDE)
-        + yxz(KW)
-        + [
-            vm(2, 4, 32, NARROW), vm(3, 2, 4, 32, NARROW), vm(2, 32, NARROW), vm(3, 2, 32, NARROW),
-            vm(32, NARROW), vm(3, 32, NARROW),
-        ]
+        + zyx(KW)
+        + zyx(NARROW)
         + [vm(3, 2, 32, FH), vm(2, 32, FH), vm(3, 32, FH), vm(32, FH)]
-        + [vm(3, 32, FH), vm(32, FH), vm(32, FH), vm(32, FH)]
-        + [vm(3, 80, D), vm(80, D)]
+        + [vm(3, 32, 640), vm(3, 32, 640), vm(32, FH), vm(32, FH), vm(32, FH)]
+        + [vm(3, 80, D), vm(80, D), vm(80, D), vm(80, D)]
         + [sem((6, 3, 3)), sem((6, 3, 3)), sem((4,)), sem((4,)), sem((6, 3)), sem((6, 3)), sem((6, 4)), sem((6, 4)), sem((6,))],
         compiler_params=params(3),
     )(*args)
@@ -1034,11 +1070,9 @@
     weight = weight.astype(F32)
     first_new = beta_first * first.astype(F32) + (1.0 - beta_first) * gradient
     second_new = beta_second * second.astype(F32) + (1.0 - beta_second) * gradient * gradient
-    first_hat = first_new / (1.0 - beta_first**STEP)
-    second_hat = second_new / (1.0 - beta_second**STEP)
-    weight_new = weight - rate * (
-        first_hat / (jnp.sqrt(second_hat) + adam_epsilon) + decay * weight
-    )
+    first_hat = first_new * (rate / (1.0 - beta_first**STEP))
+    second_hat = second_new * (1.0 / (1.0 - beta_second**STEP))
+    weight_new = weight * (1.0 - rate * decay) - first_hat / (jnp.sqrt(second_hat) + adam_epsilon)
     return (weight_new, first_new, second_new)
 
 
@@ -1061,7 +1095,7 @@
             update(which, (slice(None), slice(WIDE, D)), hi[core].astype(F32)[:ROWS])
         for m in (0, 1):
             update(1, m, narrow[m].astype(F32).T[:, :ROWS])
-        gains = lo[0, 112:, :128].astype(F32) + lo[1, 112:, :128].astype(F32)
+        gains = hi[0, 112:, :128].astype(F32) + hi[1, 112:, :128].astype(F32)
         update(5, slice(None), gains[8:10, :ROWS], gain_rate, 0.0)
 
 
@@ -1081,7 +1115,7 @@
         out_shape=tuple(jax.ShapeDtypeStruct(a.shape, F32) for a in state),
         in_specs=[fixed(lo), fixed(hi), fixed(narrow), sums, sums, rows] + specs,
         out_specs=tuple(specs),
-        compiler_params=pltpu.CompilerParams(vmem_limit_bytes=40 * 2**20),
+        compiler_params=pltpu.CompilerParams(vmem_limit_bytes=62 * 2**20),
     )(lo, hi, narrow, gate, up, down, *state)
 
 
@@ -1121,7 +1155,7 @@
         query_low, attended_t, level, keys, one_t, middle_t, two_all, dy_all, gains,
         query_all, output_all, key_all, value_all, gate_all, up_all, dn_all,
     ) = forward(
-        stream_t, cosine, sine, jnp.stack([query_weight, output_weight]), keyval_weight, gain_tile, dy_t,
+        stream_t, cosine, sine, query_weight, output_weight, keyval_weight, gain_tile, dy_t,
         gateup_weight, down_weight,
     )
     query_full, output_full = query_all.reshape(D, D), output_all.reshape(D, D)
@@ -1130,13 +1164,13 @@
     down_full = dn_all.reshape(FH, D)
 
     (
-        query_back, keyval_back, gate_part, up_part, down_sum, result_t, middle_grad, middle_low, gain_two_grad,
+        query_back, keyval_back, gate_part, up_part, up_row, down_sum, result_t, middle_grad, middle_low, gain_two_grad,
     ) = backward(
         query_low, keys, level, attended_t, cosine, sine, two_all, dy_all, middle_t, gains,
         gate_full, up_full, down_full, output_full,
     )
     low, high, narrow, gate_sum, up_sum, down, input_grad = finish(
-        one_t, attended_t, middle_low, query_back, keyval_back, gate_part, up_part, down_sum,
+        one_t, attended_t, middle_low, query_back, keyval_back, gate_part, up_part, up_row, down_sum,
         stream_t, middle_grad, gains, gain_two_grad, query_full, key_full, value_full,
     )
     turned = lambda a: a.transpose(0, 2, 1)

time: 242 us -> 233 us (0.963)
  local copies, waits for them, and re-layouts: 9.65 us -> 3.46 us
    pallas_call x1, Pallas kernels: 75.5 us -> 62.4 us  [backward(): pl.pallas_call(backward_kernel, name='backward', out_shape=(jax.ShapeDtyp...]
    pallas_call x1, Pallas kernels: 59.9 us -> 66.4 us  [finish(): pl.pallas_call(finish_kernel, name='finish', out_shape=(jax.ShapeDtypeStr...]
    unnamed x55 -> x7, local copies, waits for them, and re-layouts: 9.65 us -> 3.46 us
    pallas_call x1, Pallas kernels: 9.58 us -> 15.2 us  [update_all(): pl.pallas_call(update_kernel, name='update', grid=(steps,), out_shape=tup...]
where the time goes in v4:
time: 233 us; the launch traced here: 232 us
  Pallas kernels  226 us (97%)
  local copies, waits for them, and re-layouts  3.46 us (1%)
    pallas_call x1, Pallas kernels, forward(): pl.pallas_call(forward_kernel, name='forward', out_shape=(low(D, TOK), lo...  81.9 us
    pallas_call x1, Pallas kernels, finish(): pl.pallas_call(finish_kernel, name='finish', out_shape=(jax.ShapeDtypeStr...  66.4 us
    pallas_call x1, Pallas kernels, backward(): pl.pallas_call(backward_kernel, name='backward', out_shape=(jax.ShapeDtyp...  62.4 us
    pallas_call x1, Pallas kernels, update_all(): pl.pallas_call(update_kernel, name='update', grid=(steps,), out_shape=tup...  15.2 us

profile of v4, /device:TPU:1, one launch (start us, length us, event | category | flops | bytes accessed | tf_op | source)
XLA Modules:
  0.0 232.3 jit_solution(261944815755789444)
XLA Ops:
  0.7 1.3 pad_convert_fusion.gain
  1.9 0.8 multiply_sine_fusion
  2.8 1.7 copy.40.kv
  4.5 81.9 %forward.1 = (bf16[960,256]{1,0:T(8,128)(2,1)}, bf16[960,256]{1,0:T(8,128)(2,1)}, f32[16,1,256]{2,1,0:T(1,128)}, bf16[4,640,256]{2,1,0:T(8,128)(2,1)}, bf16[960,...) custom-call(bf16[960,256]{1,0:T(8,128)(2,1)} %bitcast.29, ...), custom_call_target="tpu_custom_call" | custom-call | tf_op jit(solution)/shard_map/forward/pallas_call | solution.py:384
  86.4 62.4 %backward.1 = (bf16[960,256]{1,0:T(8,128)(2,1)}, bf16[640,256]{1,0:T(8,128)(2,1)}, bf16[2,4,32,1280]{3,2,1,0:T(8,128)(2,1)}, bf16[4,32,640]{2,1,0:T(8,128)(2,1)}...) custom-call(bf16[960,256]{1,0:T(8,128)(2,1)} %get-tuple-element.71.q, ...), custom_call_target="tpu_custom_call" | custom-call | tf_op jit(solution)/shard_map/backward/pallas_call | solution.py:681
  148.9 66.4 %finish.1 = (bf16[2,128,512]{2,1,0:T(8,128)(2,1)}, bf16[2,128,448]{2,1,0:T(8,128)(2,1)}, bf16[2,128,320]{2,1,0:T(8,128)(2,1)}, bf16[128,2560]{1,0:T(8,128)(2,1)}...) custom-call(bf16[960,256]{1,0:T(8,128)(2,1)} %get-tuple-element.84.one, ...), custom_call_target="tpu_custom_call" | custom-call | tf_op jit(solution)/shard_map/finish/pallas_call | solution.py:1039
  215.3 0.0 copy-start.1
  215.3 0.0 copy-start
  215.3 15.2 %update.1 = (f32[120,960]{1,0:T(8,128)}, f32[120,960]{1,0:T(8,128)}, f32[120,960]{1,0:T(8,128)}, f32[2,320,120]{2,1,0:T(8,128)}, f32[2,320,120]{2,1,0:T(8,128)},...) custom-call(bf16[2,128,512]{2,1,0:T(8,128)(2,1)} %get-tuple-element., ...), custom_call_target="tpu_custom_call" | custom-call | tf_op jit(solution)/shard_map/update/pallas_call | solution.py:1111
  230.5 0.0 copy-done.1
  230.5 0.8 copy.43
  231.3 0.0 copy-done
  231.3 0.9 copy.44
  (2 shorter events, 0.0 us)
Async XLA Ops:
  215.3 15.2 %copy-start.1 = (bf16[960,256]{1,0:T(8,128)(2,1)S(1)}, bf16[960,256]{1,0:T(8,128)(2,1)}, u32[]{:S(2)}) copy-start(bf16[960,256]{1,0:T(8,128)(2,1)} %get-tuple-element.83) | copy-start | bytes 1474564
  215.3 16.0 %copy-start = (f32[960,256]{1,0:T(8,128)S(1)}, f32[960,256]{1,0:T(8,128)}, u32[]{:S(2)}) copy-start(f32[960,256]{1,0:T(8,128)} %get-tuple-element.97) | copy-start | bytes 2949124

commit v5 on v4

--- a/solution.py
+++ b/solution.py
@@ -50,6 +50,13 @@
     return {"rep": z, "fsdp": lax.rem(x, 2) * 4 + y, "ctx": (x // 2) * 2 + core}
 
 
+def ring(x, y, z, c):
+    along_x = [at(x + j, y, z, c) for j in (1, 2, 3)]
+    along_y = [at(x, y + j, z, c) for j in (1, 2, 3)]
+    along_z = [at(x, y, z + j, c) for j in (1, 2, 3)]
+    return along_x, along_y, along_z
+
+
 def greet(devices):
     barrier = pltpu.get_barrier_semaphore()
     for device in devices:
@@ -82,10 +89,10 @@
 
 
 def forward_kernel(
-    stream, cos, sin, qw, ow, kv, gain, dy, gu, dn,
+    stream, cos, sin, kv_turned, gain_row, qw, ow, dy, gu, dn,
     q_low, att, lse, kv_out, one, mid, two_all, dy_all, gains_out, q_all, o_all, k_all, v_all, gate_all, up_all, dn_all,
-    keys, wide, ones, two, qo_land, kv_land, gain_land,
-    send, recv, send_y, send_x, recv_w, send_ay, send_ax, send_as, recv_a, recv_as, local,
+    keys, wide, ones, two, qo_land, kv_land, gain_land, kv, gain,
+    send, recv, send_zd, recv_zd, send_y, send_x, recv_w, send_ay, send_ax, send_as, recv_a, recv_as, local,
 ):
     x, y, z, c = place()
     xl = lax.rem(x, 2)
@@ -94,10 +101,16 @@
     me = 2 * (x // 2) + c
     sib_slot, far_slot, diag_slot = me + 1 - 2 * c, lax.rem(me + 2, 4), lax.rem(me + 2, 4) + 1 - 2 * c
     sibling, far = at(x, y, z, 1 - c), at(x + 2, y, z, c)
-    greet([at(x, y + j, z, c) for j in (1, 2, 3)] + [at(x + j, y, z, c) for j in (1, 2, 3)] + [sibling])
+    along_x, along_y, along_z = ring(x, y, z, c)
+    greet(along_x + along_y + along_z + [sibling])
 
     def column(k):
         return 4 * xl + lax.rem(y + k + 1, 4) if k < 3 else 4 * (1 - xl) + lax.rem(y + k - 3, 4)
+
+    for m in (0, 1):
+        kv[m] = kv_turned[m].astype(F32).T.astype(BF)
+    gain[...] = jnp.zeros_like(gain)
+    gain[0:2, 0:ROWS] = gain_row[...].astype(F32)
 
     def own_a(item):
         return (None, kv.at[c], gain)[item]
@@ -172,14 +185,38 @@
             at(x + (1, 3, 1, 3)[item], y, z, c),
         )
 
+    def send_ring(item):
+        j = (3, 1, 3, 1)[item]
+        ref = slot(item, 4 * xl + lax.rem(y + j, 4))
+        return remote(ref, ref, send_y.at[item, 1], recv_w.at[item, 4 * xl + lax.rem(y + j, 4)], at(x, y + 4 - j, z, c))
+
+    def crossing(item, j, action):
+        if item < 2:
+            action()
+        else:
+            pl.when(lax.rem(y + j, 4) == z)(action)
+
     def pass_on(items, offsets):
         for item in items:
             for j in offsets:
                 wait_slot(item, 4 * xl + lax.rem(y + j, 4))
-                send_side(item, j).start()
+                if j == (3, 1, 3, 1)[item]:
+                    send_ring(item).start()
+                crossing(item, j, lambda: send_side(item, j).start())
 
     def pass_down(offsets):
         pl.when(holds)(lambda: pass_on((2, 3), offsets))
+
+    def down_z(j):
+        return remote(dn_all.at[z], dn_all.at[z], send_zd.at[j - 1], recv_zd.at[j - 1], along_z[j - 1])
+
+    def share_down():
+        @pl.when(jnp.logical_not(holds))
+        def _():
+            for item in (2, 3):
+                wait_slot(item, 4 * (1 - xl) + z)
+            for j in ORDER:
+                down_z(j).start()
 
     for item in (2, 1, 0):
 
@@ -214,14 +251,15 @@
     wait_a(2, 3)
     for k in (0, 2):
         take(0, k)
-    for j in ORDER:
-        for item in (0, 1):
+    @pl.when(holds)
+    def _():
+        for item in (2, 3):
+            for j in (1, 3):
+                send_row(item, j).start()
+
+    for item in (0, 1):
+        for j in (1, 3):
             send_row(item, j).start()
-
-        @pl.when(holds)
-        def _():
-            for item in (2, 3):
-                send_row(item, j).start()
 
     take(2, 1)
     take(1, 1)
@@ -262,13 +300,13 @@
     to_sib.start()
     for k in (4, 6, 5):
         take(0, k)
+    @pl.when(jnp.logical_and(holds, y == z))
+    def _():
+        for item in (2, 3):
+            send_side(item, 0).start()
+
     for item in (0, 1):
         send_side(item, 0).start()
-
-    @pl.when(holds)
-    def _():
-        for item in (2, 3):
-            send_side(item, 0).start()
 
     taken(0)
     exchange = remote(dy, dy_all.at[1], send.at[4], recv.at[4], sibling)
@@ -288,7 +326,7 @@
             rows = start + h
             q_low[rows : rows + 32, :] = ((a * co - b * si).astype(BF) * score_scale).astype(BF)
             q_low[rows + 32 : rows + 64, :] = ((b * co + a * si).astype(BF) * score_scale).astype(BF)
-    pass_on((0,), (1, 3))
+    pass_down((1, 3))
     remote(keys.at[far_slot], keys.at[far_slot], send.at[0], recv.at[0], far).wait_recv()
     on = remote(keys.at[far_slot], keys.at[far_slot], send.at[2], recv.at[2], sibling)
     on.start()
@@ -314,10 +352,11 @@
             acc += dot(keys[j, vrows, :], e[j].astype(BF), 1, 0)
         ones[rows, :] = acc / total
         lse[pl.ds(h, 1), 0, :] = top + jnp.log(total)
-        pl.when(h == 1)(lambda: pass_on((1,), (1, 3)))
-        pl.when(h == 4)(lambda: pass_down((1, 3)))
-        pl.when(h == 9)(lambda: pass_on((0,), (2,)))
-        pl.when(h == 13)(lambda: pass_on((1,), (2,)))
+        pl.when(h == 1)(lambda: pass_on((0,), (1, 3)))
+        pl.when(h == 5)(lambda: pass_down((2,)))
+        pl.when(h == 7)(lambda: pass_on((1,), (1, 3)))
+        pl.when(h == 9)(share_down)
+        pl.when(h == 13)(lambda: pass_on((0,), (2,)))
         return carry
 
     lax.fori_loop(0, QUERY_HEADS, head, 0)
@@ -335,17 +374,19 @@
     keep.start()
     trade = remote(two, two_all.at[1], send.at[3], recv.at[3], sibling)
     trade.start()
-    pass_down((2,))
+    pass_on((1,), (2,))
 
     for k in range(4):
         g = 4 * (1 - xl) + lax.rem(y + k, 4)
         for item in (0, 1):
             wait_slot(item, g)
 
-        @pl.when(jnp.logical_not(holds))
-        def _():
-            for item in (2, 3):
-                wait_slot(item, g)
+    @pl.when(jnp.logical_not(holds))
+    def _():
+        for j in ORDER:
+            ref = dn_all.at[lax.rem(z + 4 - j, 4)]
+            remote(ref, ref, send_zd.at[j - 1], recv_zd.at[j - 1], sibling).wait_recv()
+            down_z(j).wait_send()
 
     for copy in copies[4:] + keep_a + [keep]:
         copy.wait()
@@ -365,10 +406,11 @@
 
     def sent(items):
         for item in items:
-            for j in ORDER:
+            for j in (1, 3):
                 send_row(item, j).wait_send()
+            send_ring(item).wait_send()
             for j in range(4):
-                send_side(item, j).wait_send()
+                crossing(item, j, lambda: send_side(item, j).wait_send())
 
     sent((0, 1))
 
@@ -402,7 +444,7 @@
             low(8, ROWS, FH),
             low(4, KW, D),
         ),
-        in_specs=[VM] * 3 + [ANY] * 7,
+        in_specs=[VM] * 5 + [ANY] * 5,
         out_specs=(VM,) * 6 + (ANY,) * 2 + (VM,) + (ANY,) * 7,
         scratch_shapes=[
             pltpu.VMEM((4, 2 * KW, TOK), BF),
@@ -412,8 +454,12 @@
             pltpu.VMEM((2, 8, ROWS, D), BF),
             pltpu.VMEM((2, 8, ROWS, KW), BF),
             pltpu.VMEM((8, 8, 128), F32),
+            pltpu.VMEM((2, ROWS, KW), BF),
+            pltpu.VMEM((8, 128), F32),
             sem((5,)),
             sem((5,)),
+            sem((3,)),
+            sem((3,)),
             sem((4, 3)),
             sem((4, 4)),
             sem((4, 8)),
@@ -433,13 +479,6 @@
     for i in range(count):
         total += got[i].astype(F32)
     return total.astype(BF)
-
-
-def ring(x, y, z, c):
-    along_x = [at(x + j, y, z, c) for j in (1, 2, 3)]
-    along_y = [at(x, y + j, z, c) for j in (1, 2, 3)]
-    along_z = [at(x, y, z + j, c) for j in (1, 2, 3)]
-    return along_x, along_y, along_z
 
 
 def quarter(index, size):
@@ -1144,7 +1183,6 @@
     ctx = lax.axis_index("ctx")
     core = lax.rem(ctx, 2)
     stream_t, dy_t = tokens[0].T, cotangent[0].T
-    gain_tile = jnp.pad(norm_gains.astype(F32), ((0, 6), (0, 8)))
     positions = (ctx * TOK + jnp.arange(TOK, dtype=jnp.int32)).astype(F32)
     counter = jnp.arange(HALF, dtype=F32)
     frequency = 1.0 / rotary_base ** (counter * (2.0 / HEAD_WIDTH))
@@ -1155,7 +1193,7 @@
         query_low, attended_t, level, keys, one_t, middle_t, two_all, dy_all, gains,
         query_all, output_all, key_all, value_all, gate_all, up_all, dn_all,
     ) = forward(
-        stream_t, cosine, sine, query_weight, output_weight, keyval_weight, gain_tile, dy_t,
+        stream_t, cosine, sine, keyval_weight.transpose(0, 2, 1), norm_gains, query_weight, output_weight, dy_t,
         gateup_weight, down_weight,
     )
     query_full, output_full = query_all.reshape(D, D), output_all.reshape(D, D)

time: 233 us -> 229 us (0.983)
    pallas_call x1, Pallas kernels: 81.9 us -> 84.4 us  [forward(): pl.pallas_call(forward_kernel, name='forward', out_shape=(low(D, TOK), lo...]
where the time goes in v5:
time: 229 us
  Pallas kernels  225 us (98%)
    pallas_call x1, Pallas kernels, forward(): pl.pallas_call(forward_kernel, name='forward', out_shape=(low(D, TOK), lo...  84.4 us
    pallas_call x1, Pallas kernels, finish(): pl.pallas_call(finish_kernel, name='finish', out_shape=(jax.ShapeDtypeStr...  65 us
    pallas_call x1, Pallas kernels, backward(): pl.pallas_call(backward_kernel, name='backward', out_shape=(jax.ShapeDtyp...  60.7 us
    pallas_call x1, Pallas kernels, update_all(): pl.pallas_call(update_kernel, name='update', grid=(steps,), out_shape=tup...  15.2 us

profile of v5, /device:TPU:1, one launch (start us, length us, event | category | flops | bytes accessed | tf_op | source)
XLA Modules:
  0.0 228.5 jit_solution(7469910171884423785)
XLA Ops:
  0.7 0.8 multiply_sine_fusion
  1.5 84.4 %forward.1 = (bf16[960,256]{1,0:T(8,128)(2,1)}, bf16[960,256]{1,0:T(8,128)(2,1)}, f32[16,1,256]{2,1,0:T(1,128)}, bf16[4,640,256]{2,1,0:T(8,128)(2,1)}, bf16[960,...) custom-call(bf16[960,256]{1,0:T(8,128)(2,1)} %bitcast.30, ...), custom_call_target="tpu_custom_call" | custom-call | tf_op jit(solution)/shard_map/forward/pallas_call | solution.py:426
  85.9 60.7 %backward.1 = (bf16[960,256]{1,0:T(8,128)(2,1)}, bf16[640,256]{1,0:T(8,128)(2,1)}, bf16[2,4,32,1280]{3,2,1,0:T(8,128)(2,1)}, bf16[4,32,640]{2,1,0:T(8,128)(2,1)}...) custom-call(bf16[960,256]{1,0:T(8,128)(2,1)} %get-tuple-element.71.q, ...), custom_call_target="tpu_custom_call" | custom-call | tf_op jit(solution)/shard_map/backward/pallas_call | solution.py:720
  146.6 65.0 %finish.1 = (bf16[2,128,512]{2,1,0:T(8,128)(2,1)}, bf16[2,128,448]{2,1,0:T(8,128)(2,1)}, bf16[2,128,320]{2,1,0:T(8,128)(2,1)}, bf16[128,2560]{1,0:T(8,128)(2,1)}...) custom-call(bf16[960,256]{1,0:T(8,128)(2,1)} %get-tuple-element.84.one, ...), custom_call_target="tpu_custom_call" | custom-call | tf_op jit(solution)/shard_map/finish/pallas_call | solution.py:1078
  211.6 0.0 copy-start.1
  211.6 0.0 copy-start
  211.6 15.2 %update.1 = (f32[120,960]{1,0:T(8,128)}, f32[120,960]{1,0:T(8,128)}, f32[120,960]{1,0:T(8,128)}, f32[2,320,120]{2,1,0:T(8,128)}, f32[2,320,120]{2,1,0:T(8,128)},...) custom-call(bf16[2,128,512]{2,1,0:T(8,128)(2,1)} %get-tuple-element., ...), custom_call_target="tpu_custom_call" | custom-call | tf_op jit(solution)/shard_map/update/pallas_call | solution.py:1150
  226.8 0.0 copy-done.1
  226.8 0.8 copy.42
  227.6 0.0 copy-done
  227.6 0.9 copy.43
  (2 shorter events, 0.0 us)
Async XLA Ops:
  211.6 15.2 %copy-start.1 = (bf16[960,256]{1,0:T(8,128)(2,1)S(1)}, bf16[960,256]{1,0:T(8,128)(2,1)}, u32[]{:S(2)}) copy-start(bf16[960,256]{1,0:T(8,128)(2,1)} %get-tuple-element.83) | copy-start | bytes 1474564
  211.6 16.0 %copy-start = (f32[960,256]{1,0:T(8,128)S(1)}, f32[960,256]{1,0:T(8,128)}, u32[]{:S(2)}) copy-start(f32[960,256]{1,0:T(8,128)} %get-tuple-element.97) | copy-start | bytes 2949124
